TPU v7x, 128 devices: a whole 4x4x4 slice. The times are simulated.
128 devices in a mesh: line: 16 (over x_lo, z, core), bus: 8 (over y, x_hi).
Axes of the slice: x: 4 (x_hi: 2, x_lo: 2; x = x_hi * 2 + x_lo), y: 4, z: 4, core: 2. Of those that a mesh axis runs over, the one named last changes fastest.
Arguments:
- ptdf: bfloat16 [16384, 70656], P('line', 'bus'), may hold values from -0.0234375 to 0.0234375
- injections: bfloat16 [70656, 256], P('bus', 'line'), may hold values from -6 to 6
- viol_mask: int32 [16384, 256], P('line'), may hold values 0 or 1
- viol_sign: int32 [16384], P('line'), may hold values from 0 to 1
- limit: float32 [16384], P('line'), may hold values from 0.2 to 1.5
- price: float32 [16384], P('line'), may hold values from 0.3 to 3
- owner: int32 [70656], P('bus'), may hold values from 0 to 10367, as said below
Outputs:
- gen_cut: float32 [10368, 256], P(('line', 'bus'))
Inputs may be any that keep to these rules, and one draw needn't show every extreme that they name: `owner`: each bus has one owning generator; split the buses into aligned blocks of 70656 // 128 in order and the generators into groups of 10368 // 128 in order: in every block at most 5 buses belong to one group, and some group has exactly 5 in every block.
All inputs are finite; a program needn't handle non-finite values. No bound on the sum of `viol_mask` on one device may be relied on, other than what follows from the above.
Results may differ from a plain program's by a relative error of at most 0.0029.
Values may be sent and summed in bfloat16 or wider, within the bound.
No kernel may reach another device: no remote copies, remote signals or barrier semaphores. Data moves between devices by JAX's collectives and lax.ppermute only.
A program may use at most 128 MiB of HBM per device.

v0:
```python
import jax
import jax.numpy as jnp
from jax import lax
from jax.sharding import PartitionSpec as P

GENS = 10368


def make_dual(flows, mask_part, viol_sign, limit, price):
    direction = (2 * viol_sign - 1).astype(jnp.float32)[:, None]
    return (
        mask_part.astype(jnp.float32) * price[:, None] * (direction * flows - limit[:, None])
    ).astype(jnp.bfloat16)


def local(ptdf, injections, viol_mask, viol_sign, limit, price, owner):
    partial_flows = jnp.dot(
        ptdf,
        lax.all_gather(injections, "line", axis=1, tiled=True),
        preferred_element_type=jnp.float32,
    )
    flows = lax.psum(partial_flows, "bus")
    dual = make_dual(flows, viol_mask, viol_sign, limit, price)
    contract = (((0,), (0,)), ((), ()))
    count_rows = ptdf.shape[1] // lax.axis_size("line")
    cuts = lax.psum_scatter(
        lax.dot_general(ptdf, dual, contract, preferred_element_type=jnp.float32),
        "line",
        scatter_dimension=0,
        tiled=True,
    )
    owners = lax.dynamic_slice_in_dim(owner, lax.axis_index("line") * count_rows, count_rows, 0)
    generator_terms = jax.ops.segment_sum(cuts, owners, num_segments=GENS)
    return lax.psum_scatter(generator_terms, ("line", "bus"), scatter_dimension=0, tiled=True)


def solution(mesh):
    placed = (
        P("line", "bus"),
        P("bus", "line"),
        P("line", None),
        P("line"),
        P("line"),
        P("line"),
        P("bus"),
    )
    return jax.shard_map(
        local, mesh=mesh, in_specs=placed, out_specs=P(("line", "bus"), None), check_vma=False
    )
```

profile of v0, /device:TPU:3, one launch (start us, length us, event | category | flops | bytes accessed | tf_op | source)
XLA Modules:
  0.0 735.7 jit_solution(13622861882808027409)
XLA Ops:
  6.5 0.0 all-gather.2.cloned.1.call-start
  6.5 0.7 all-gather.2.cloned.1.call-update
  7.3 0.0 copy-start.3
  7.3 0.0 copy-start
  7.3 0.0 copy-start.1
  7.3 0.0 copy-start.2
  7.3 0.0 all-reduce.4.cloned.1.call-start
  7.3 42.2 %all-gather.2.cloned.1.call-done = bf16[8832,256]{0,1:T(8,128)(2,1)} async-done(((bf16[8832,16]{0,1:T(8,128)(2,1)}), bf16[8832,256]{0,1:T(8,128)(2,1)}) %all-gather.2.cloned.1.call-update) | async-done | bytes 4522000 | tf_op jit(solution)/shard_map/all_gather | solution.py:19
  49.6 13.3 %fusion.6 = f32[1024,256]{1,0:T(8,128)} fusion(bf16[1024,8832]{1,0:T(8,128)(2,1)} %param.7, bf16[8832,256]{0,1:T(8,128)(2,1)} %all-gather.2.cloned.1.call-done), kind=kOutput, calls=%fused_computation.10 | convolution fusion | flops 4630511616 | bytes 23658496 | tf_op jit(solution)/shard_map/dot_general | solution.py:17
  62.9 0.0 all-reduce.4.cloned.1.call-update
  62.9 0.0 reduce-scatter.6.cloned.1.call-start
  62.9 0.0 copy-done.3
  63.0 85.0 %all-reduce.4.cloned.1.call-done = f32[1024,256]{1,0:T(8,128)} async-done(((f32[1024,256]{1,0:T(8,128)}), f32[1024,256]{1,0:T(8,128)}) %all-reduce.4.cloned.1.call-update) | async-done | bytes 1048592 | tf_op jit(solution)/shard_map/psum | solution.py:22
  148.0 0.0 copy-done
  148.0 0.0 copy-done.1
  148.0 0.0 copy-done.2
  148.0 15.1 %convolution_bitcast_fusion = f32[8832,256]{0,1:T(8,128)} fusion(bf16[1024,8832]{1,0:T(8,128)(2,1)} %param.7, f32[1024,256]{1,0:T(8,128)} %all-reduce.4.cloned.1.call-done, s32[1024,256]{1,0:T(8,128)S(1)} %copy-done, f32[1024]{0:T(1024)S(1)} %copy-done.1, f32[1024]{0:T(1024)S(1)} %add_convert_fusion, f32[1024]{0:T(1024)S(1)} %copy-done.2), kind=kOutput, calls=%fused_computation.1 | convolution fusion | flops 4632084480 | bytes 29241344 | tf_op jit(solution)/shard_map/dot_general | solution.py:27
  163.1 9.4 %copy.10 = f32[8832,256]{1,0:T(8,128)} copy(f32[8832,256]{0,1:T(8,128)} %convolution_bitcast_fusion) | data formatting | bytes 18087936
  172.4 0.0 reduce-scatter.6.cloned.1.call-update
  172.5 0.8 dynamic_slice.3
  173.2 74.8 %reduce-scatter.6.cloned.1.call-done = f32[552,256]{1,0:T(8,128)} async-done(((f32[8832,256]{1,0:T(8,128)}), f32[552,256]{1,0:T(8,128)}) %reduce-scatter.6.cloned.1.call-update) | async-done | bytes 565264 | tf_op jit(solution)/shard_map/reduce_scatter | solution.py:26
  248.0 10.7 %scatter_custom_fusion = f32[10368,256]{1,0:T(8,128)} fusion(s32[552]{0:T(1024)S(1)} %dynamic_slice.3, f32[552,256]{1,0:T(8,128)} %reduce-scatter.6.cloned.1.call-done, f32[]{:T(128)} %constant.3.clone.1), kind=kCustom, calls=%fused_computation.2 | custom fusion | flops 141312 | bytes 10617344 | tf_op jit(solution)/shard_map/scatter-add | solution.py:33
  258.7 386.7 %fusion = f32[88,256]{1,0:T(8,128)S(1)} fusion(f32[10368,256]{1,0:T(8,128)} %scatter_custom_fusion), kind=kCustom, calls=%all-reduce-scatter | all-reduce-scatter fusion | flops 2883585 | bytes 10706944
  645.4 1.9 collective-permute-start.10
  647.4 3.3 collective-permute-start
  650.7 3.2 collective-permute-start.1
  653.8 4.5 collective-permute-start.2
  658.3 7.5 %collective-permute-start.3 = (f32[88,256]{1,0:T(8,128)S(1)}, f32[88,256]{1,0:T(8,128)S(1)}, u32[]{:S(2)}, u32[]{:S(2)}) collective-permute-start(f32[88,256]{1,0:T(8,128)S(1)} %fusion), channel_id=1, source_target_pairs={{0,4},{1,5},{2,6},{3,7},{4,8},{5,9},{6,10},{7,11},{8,12},{9,13},{1... | collective-permute-start | bytes 270344
  665.8 0.0 collective-permute-done.10
  665.8 12.4 %collective-permute-start.4 = (f32[88,256]{1,0:T(8,128)S(1)}, f32[88,256]{1,0:T(8,128)S(1)}, u32[]{:S(2)}, u32[]{:S(2)}) collective-permute-start(f32[88,256]{1,0:T(8,128)S(1)} %fusion), channel_id=1, source_target_pairs={{0,5},{1,6},{2,7},{3,8},{4,9},{5,10},{6,11},{7,12},{8,13},{9,14},{... | collective-permute-start | bytes 270344
  678.2 0.0 collective-permute-done
  678.3 3.9 collective-permute-start.5
  682.2 0.0 collective-permute-done.1
  682.2 12.2 %collective-permute-start.6 = (f32[88,256]{1,0:T(8,128)S(1)}, f32[88,256]{1,0:T(8,128)S(1)}, u32[]{:S(2)}, u32[]{:S(2)}) collective-permute-start(f32[88,256]{1,0:T(8,128)S(1)} %fusion), channel_id=1, source_target_pairs={{0,7},{1,8},{2,9},{3,10},{4,11},{5,12},{6,13},{7,14},{8,15},{9,16}... | collective-permute-start | bytes 270344
  694.4 0.0 collective-permute-done.2
  694.4 13.4 %collective-permute-start.7 = (f32[88,256]{1,0:T(8,128)S(1)}, f32[88,256]{1,0:T(8,128)S(1)}, u32[]{:S(2)}, u32[]{:S(2)}) collective-permute-start(f32[88,256]{1,0:T(8,128)S(1)} %fusion), channel_id=1, source_target_pairs={{0,8},{1,9},{2,10},{3,11},{4,12},{5,13},{6,14},{7,15},{8,16},{9,17... | collective-permute-start | bytes 270344
  707.9 0.0 collective-permute-done.3
  707.9 9.0 %collective-permute-start.8 = (f32[88,256]{1,0:T(8,128)S(1)}, f32[88,256]{1,0:T(8,128)S(1)}, u32[]{:S(2)}, u32[]{:S(2)}) collective-permute-start(f32[88,256]{1,0:T(8,128)S(1)} %fusion), channel_id=1, source_target_pairs={{0,9},{1,10},{2,11},{3,12},{4,13},{5,14},{6,15},{7,16},{8,17},{9,1... | collective-permute-start | bytes 270344
  716.9 0.0 collective-permute-done.4
  716.9 2.1 collective-permute-start.9
  719.0 0.0 collective-permute-done.5
  719.0 0.0 collective-permute-done.6
  719.0 0.0 collective-permute-done.7
  719.0 0.0 collective-permute-done.8
  719.0 7.4 %collective-permute-done.9 = f32[88,256]{1,0:T(8,128)S(1)} collective-permute-done((f32[88,256]{1,0:T(8,128)S(1)}, f32[88,256]{1,0:T(8,128)S(1)}, u32[]{:S(2)}, u32[]{:S(2)}) %collective-permute-start.9) | collective-permute-done | bytes 90144
  726.4 2.1 concatenate
  728.5 0.7 constant_dynamic-slice_fusion
  (2 shorter events, 0.0 us)
Async XLA Ops:
  6.5 43.0 %all-gather.2.cloned.1.call-start = ((), (), s32[]{:S(2)}) async-start(), calls=%async_computation.1 | async-start | bytes 4804608 | tf_op jit(solution)/shard_map/all_gather | solution.py:19
  7.3 55.7 %copy-start.3 = (s32[1024]{0:T(1024)S(1)}, s32[1024]{0:T(1024)}, u32[]{:S(2)}) copy-start(s32[1024]{0:T(1024)} %param.10) | copy-start | bytes 12292
  7.3 140.7 %copy-start = (s32[1024,256]{1,0:T(8,128)S(1)}, s32[1024,256]{1,0:T(8,128)}, u32[]{:S(2)}) copy-start(s32[1024,256]{1,0:T(8,128)} %param.9) | copy-start | bytes 3145732
  7.3 140.7 %copy-start.1 = (f32[1024]{0:T(1024)S(1)}, f32[1024]{0:T(1024)}, u32[]{:S(2)}) copy-start(f32[1024]{0:T(1024)} %param.11) | copy-start | bytes 12292
  7.3 140.7 %copy-start.2 = (f32[1024]{0:T(1024)S(1)}, f32[1024]{0:T(1024)}, u32[]{:S(2)}) copy-start(f32[1024]{0:T(1024)} %param.12) | copy-start | bytes 12292
  7.3 140.7 %all-reduce.4.cloned.1.call-start = ((), (), s32[]{:S(2)}) async-start(), calls=%async_computation.2 | async-start | bytes 2097152 | tf_op jit(solution)/shard_map/psum | solution.py:22
  62.9 185.1 %reduce-scatter.6.cloned.1.call-start = ((), (), s32[]{:S(2)}) async-start(), calls=%async_computation.3 | async-start | bytes 9609216 | tf_op jit(solution)/shard_map/reduce_scatter | solution.py:26
  645.4 20.4 %collective-permute-start.10 = (f32[9,256]{1,0:T(8,128)S(1)}, f32[9,256]{1,0:T(8,128)S(1)}, u32[]{:S(2)}, u32[]{:S(2)}) collective-permute-start(f32[9,256]{1,0:T(8,128)S(1)} %slice), channel_id=1, source_target_pairs={{0,11},{1,12},{2,13},{3,14},{4,15},{5,16},{6,17},{7,18},{8,19},{9,... | collective-permute-start | bytes 27656
  647.4 30.9 %collective-permute-start = (f32[88,256]{1,0:T(8,128)S(1)}, f32[88,256]{1,0:T(8,128)S(1)}, u32[]{:S(2)}, u32[]{:S(2)}) collective-permute-start(f32[88,256]{1,0:T(8,128)S(1)} %fusion), channel_id=1, source_target_pairs={{0,1},{1,2},{2,3},{3,4},{4,5},{5,6},{6,7},{7,8},{8,9},{9,10},{10,1... | collective-permute-start | bytes 270344
  650.7 31.5 %collective-permute-start.1 = (f32[88,256]{1,0:T(8,128)S(1)}, f32[88,256]{1,0:T(8,128)S(1)}, u32[]{:S(2)}, u32[]{:S(2)}) collective-permute-start(f32[88,256]{1,0:T(8,128)S(1)} %fusion), channel_id=1, source_target_pairs={{0,2},{1,3},{2,4},{3,5},{4,6},{5,7},{6,8},{7,9},{8,10},{9,11},{10,... | collective-permute-start | bytes 270344
  653.8 40.6 %collective-permute-start.2 = (f32[88,256]{1,0:T(8,128)S(1)}, f32[88,256]{1,0:T(8,128)S(1)}, u32[]{:S(2)}, u32[]{:S(2)}) collective-permute-start(f32[88,256]{1,0:T(8,128)S(1)} %fusion), channel_id=1, source_target_pairs={{0,3},{1,4},{2,5},{3,6},{4,7},{5,8},{6,9},{7,10},{8,11},{9,12},{10... | collective-permute-start | bytes 270344
  658.3 49.6 %collective-permute-start.3 = (f32[88,256]{1,0:T(8,128)S(1)}, f32[88,256]{1,0:T(8,128)S(1)}, u32[]{:S(2)}, u32[]{:S(2)}) collective-permute-start(f32[88,256]{1,0:T(8,128)S(1)} %fusion), channel_id=1, source_target_pairs={{0,4},{1,5},{2,6},{3,7},{4,8},{5,9},{6,10},{7,11},{8,12},{9,13},{1... | collective-permute-start | bytes 270344
  665.8 51.1 %collective-permute-start.4 = (f32[88,256]{1,0:T(8,128)S(1)}, f32[88,256]{1,0:T(8,128)S(1)}, u32[]{:S(2)}, u32[]{:S(2)}) collective-permute-start(f32[88,256]{1,0:T(8,128)S(1)} %fusion), channel_id=1, source_target_pairs={{0,5},{1,6},{2,7},{3,8},{4,9},{5,10},{6,11},{7,12},{8,13},{9,14},{... | collective-permute-start | bytes 270344
  678.3 40.7 %collective-permute-start.5 = (f32[88,256]{1,0:T(8,128)S(1)}, f32[88,256]{1,0:T(8,128)S(1)}, u32[]{:S(2)}, u32[]{:S(2)}) collective-permute-start(f32[88,256]{1,0:T(8,128)S(1)} %fusion), channel_id=1, source_target_pairs={{0,6},{1,7},{2,8},{3,9},{4,10},{5,11},{6,12},{7,13},{8,14},{9,15},... | collective-permute-start | bytes 270344
  682.2 36.8 %collective-permute-start.6 = (f32[88,256]{1,0:T(8,128)S(1)}, f32[88,256]{1,0:T(8,128)S(1)}, u32[]{:S(2)}, u32[]{:S(2)}) collective-permute-start(f32[88,256]{1,0:T(8,128)S(1)} %fusion), channel_id=1, source_target_pairs={{0,7},{1,8},{2,9},{3,10},{4,11},{5,12},{6,13},{7,14},{8,15},{9,16}... | collective-permute-start | bytes 270344
  694.4 24.6 %collective-permute-start.7 = (f32[88,256]{1,0:T(8,128)S(1)}, f32[88,256]{1,0:T(8,128)S(1)}, u32[]{:S(2)}, u32[]{:S(2)}) collective-permute-start(f32[88,256]{1,0:T(8,128)S(1)} %fusion), channel_id=1, source_target_pairs={{0,8},{1,9},{2,10},{3,11},{4,12},{5,13},{6,14},{7,15},{8,16},{9,17... | collective-permute-start | bytes 270344
  707.9 11.1 %collective-permute-start.8 = (f32[88,256]{1,0:T(8,128)S(1)}, f32[88,256]{1,0:T(8,128)S(1)}, u32[]{:S(2)}, u32[]{:S(2)}) collective-permute-start(f32[88,256]{1,0:T(8,128)S(1)} %fusion), channel_id=1, source_target_pairs={{0,9},{1,10},{2,11},{3,12},{4,13},{5,14},{6,15},{7,16},{8,17},{9,1... | collective-permute-start | bytes 270344
  716.9 9.5 %collective-permute-start.9 = (f32[88,256]{1,0:T(8,128)S(1)}, f32[88,256]{1,0:T(8,128)S(1)}, u32[]{:S(2)}, u32[]{:S(2)}) collective-permute-start(f32[88,256]{1,0:T(8,128)S(1)} %fusion), channel_id=1, source_target_pairs={{0,10},{1,11},{2,12},{3,13},{4,14},{5,15},{6,16},{7,17},{8,18},{9,... | collective-permute-start | bytes 270344
Sparse Core Ops, SparseCore 0:
  9.1 40.4 all-gather.1
  63.0 84.8 all-reduce.3
  172.6 75.4 reduce-scatter.5
where the time goes:
time: 736 us
  blocking collectives  387 us (53%)
  waiting for transfers between devices  210 us (29%)
  starting transfers between devices  73.5 us (10%)
  matrix products  28.4 us (4%)
  between operations  13.4 us (2%)
  local copies, waits for them, and re-layouts  12.9 us (2%)
  other arithmetic  10.7 us (1%)
    unnamed x1, blocking collectives  387 us
    psum x1, waiting for transfers between devices, local(): flows = lax.psum(partial_flows, 'bus')  85 us
    reduce_scatter x1, waiting for transfers between devices, local(): lax.psum_scatter(lax.dot_general(ptdf, dual, contract, preferred_element_...  74.8 us
    unnamed x11, starting transfers between devices  73.4 us
    all_gather x1, waiting for transfers between devices, local(): lax.all_gather(injections, 'line', axis=1, tiled=True)  42.2 us
    dot_general x1, matrix products, local(): lax.dot_general(ptdf, dual, contract, preferred_element_type=jnp.float32)  15.1 us
  transfers between devices with their start and end apart: 14, of which 4 were waited for; matrix products, arithmetic and copies ran while one was open for 0% of the time, Pallas kernels for 0%

commit v1 on v0

v1 whole, which is shorter than its diff:
```python
import jax
import jax.numpy as jnp
from jax import lax
from jax.sharding import PartitionSpec as P

GENS = 10368
LINES_AT = 16
BUSES_AT = 8
DEVICES = LINES_AT * BUSES_AT
HELD = GENS // DEVICES
SLOTS = 8
PAIRS = [(i, i ^ 1) for i in range(LINES_AT)]
SAME_CORE = [[a + c for a in range(0, LINES_AT, 2)] for c in (0, 1)]
HALF = LINES_AT // 2


def make_dual(flows, mask_part, viol_sign, limit, price):
    direction = (2 * viol_sign - 1).astype(jnp.float32)[:, None]
    return (
        mask_part.astype(jnp.float32) * price[:, None] * (direction * flows - limit[:, None])
    ).astype(jnp.bfloat16)


def share(x, axis, ways, groups=None):
    spread = jnp.broadcast_to(x[None], (ways,) + x.shape)
    return lax.all_to_all(spread, axis, 0, 0, tiled=True, axis_index_groups=groups)


def ranks(groups):
    count = groups.shape[-1]
    same = groups[..., :, None] == groups[..., None, :]
    earlier = lax.broadcasted_iota(jnp.int32, (count, count), 0) > lax.broadcasted_iota(
        jnp.int32, (count, count), 1
    )
    return jnp.sum((same & earlier).astype(jnp.int32), axis=-1)


def local(ptdf, injections, viol_mask, viol_sign, limit, price, owner):
    line, bus = lax.axis_index("line"), lax.axis_index("bus")
    core = line % 2
    lines, buses = ptdf.shape
    rows = lines // BUSES_AT
    block = buses // LINES_AT
    scen = viol_mask.shape[1]

    owners = owner.reshape(2, HALF, block).transpose(1, 0, 2).reshape(LINES_AT, block)
    groups, within = owners // HELD, owners % HELD
    place = ranks(groups)
    mine = line * BUSES_AT + jnp.arange(BUSES_AT)
    slots = jnp.arange(SLOTS)
    hit = (groups[None, :, None, :] == mine[:, None, None, None]) & (
        place[None, :, None, :] == slots[None, None, :, None]
    )
    table = jnp.sum(jnp.where(hit, within[None, :, None, :] + 1, 0), axis=-1)
    table = lax.all_to_all(table.reshape(BUSES_AT, -1), "bus", 0, 0, tiled=True)
    table = table.reshape(BUSES_AT, LINES_AT, SLOTS).transpose(1, 0, 2).reshape(-1) - 1
    merge = (jnp.arange(HELD)[:, None] == table[None, :]).astype(jnp.float32)
    to = groups[line] * SLOTS + place[line]
    pick = (jnp.arange(DEVICES * SLOTS)[:, None] == to[None, :]).astype(jnp.float32)

    held = share(injections.T, "line", HALF, SAME_CORE).reshape(scen // 2, buses)
    other = lax.ppermute(held, "line", PAIRS)
    inject = jnp.where(
        core == 0,
        jnp.concatenate([held, other], 0),
        jnp.concatenate([other, held], 0),
    )
    partial_flows = lax.dot_general(
        ptdf, inject, (((1,), (1,)), ((), ())), preferred_element_type=jnp.float32
    )
    flows = jnp.sum(
        lax.all_to_all(partial_flows.reshape(BUSES_AT, rows, scen), "bus", 0, 0, tiled=True), 0
    )
    cut = lambda x: lax.dynamic_slice_in_dim(x, bus * rows, rows, 0)
    width = scen // LINES_AT
    mask = cut(viol_mask).reshape(rows, HALF, 2, width).transpose(0, 2, 1, 3).reshape(rows, scen)
    dual = make_dual(flows, mask, cut(viol_sign), cut(limit), cut(price))
    dual = share(dual, "bus", BUSES_AT).reshape(lines, scen)

    cuts = lax.dot_general(
        ptdf, dual, (((0,), (0,)), ((), ())), preferred_element_type=jnp.float32
    )
    keep = lax.dynamic_slice_in_dim(cuts, core * (buses // 2), buses // 2, 0)
    give = lax.dynamic_slice_in_dim(cuts, (1 - core) * (buses // 2), buses // 2, 0)
    got = lax.ppermute(give.astype(jnp.bfloat16), "line", PAIRS)
    chip = (keep + got.astype(jnp.float32)).astype(jnp.bfloat16)
    parts = lax.all_to_all(
        chip.reshape(HALF, block, scen), "line", 0, 0, tiled=True, axis_index_groups=SAME_CORE
    )
    summed = jnp.sum(parts.astype(jnp.float32), 0)

    send = jnp.dot(pick, summed, precision=lax.Precision.HIGHEST)
    terms = lax.all_to_all(
        send.reshape(DEVICES, SLOTS, scen), ("line", "bus"), 0, 0, tiled=True
    ).reshape(DEVICES * SLOTS, scen)
    out = jnp.dot(merge, terms, precision=lax.Precision.HIGHEST)
    return out.reshape(HELD, 2, HALF, width).transpose(0, 2, 1, 3).reshape(HELD, scen)


def solution(mesh):
    placed = (
        P("line", "bus"),
        P("bus", "line"),
        P("line", None),
        P("line"),
        P("line"),
        P("line"),
        P("bus"),
    )
    return jax.shard_map(
        local, mesh=mesh, in_specs=placed, out_specs=P(("line", "bus"), None), check_vma=False
    )
```

time: 736 us -> 196 us (0.27)
  blocking collectives: 387 us -> 32.5 us
  waiting for transfers between devices: 210 us -> 63 us
  starting transfers between devices: 73.5 us -> 29.5 us
  local copies, waits for them, and re-layouts: 12.9 us -> 28.9 us
  between operations: 13.4 us -> 0.31 us
    unnamed x1 -> x0, blocking collectives: 387 us -> none
    psum x1 -> x0, waiting for transfers between devices: 85 us -> none  [local(): flows = lax.psum(partial_flows, 'bus')]
    reduce_scatter x1 -> x0, waiting for transfers between devices: 74.8 us -> none  [local(): lax.psum_scatter(lax.dot_general(ptdf, dual, contract, preferred_element_...]
    unnamed x11 -> x0, starting transfers between devices: 73.4 us -> none
    all_to_all x0 -> x5, waiting for transfers between devices: none -> 58.9 us  [the longest x1 16.6 us: local(): lax.all_to_all(send.reshape(DEVICES, SLOTS, scen), ('line', 'bus'), 0, 0,...]
    all_gather x1 -> x0, waiting for transfers between devices: 42.2 us -> none  [local(): lax.all_gather(injections, 'line', axis=1, tiled=True)]
    all_to_all x0 -> x1, blocking collectives: none -> 32.5 us  [share(): lax.all_to_all(spread, axis, 0, 0, tiled=True, axis_index_groups=groups)]
    all_to_all x0 -> x5, starting transfers between devices: none -> 24.4 us  [the longest x1 6.6 us: local(): lax.all_to_all(send.reshape(DEVICES, SLOTS, scen), ('line', 'bus'), 0, 0,...]
  transfers between devices with their start and end apart: 14 -> 7, of which waited for: 4 -> 6; matrix products, arithmetic and copies ran while one was open for 0% -> 15% of each run, Pallas kernels for 0% -> 0%
where the time goes in v1:
time: 196 us; the launch traced here: 193 us
  waiting for transfers between devices  63 us (32%)
  blocking collectives  32.5 us (17%)
  starting transfers between devices  29.5 us (15%)
  local copies, waits for them, and re-layouts  28.9 us (15%)
  matrix products  24.5 us (12%)
  other arithmetic  14.5 us (7%)
    all_to_all x1, blocking collectives, share(): lax.all_to_all(spread, axis, 0, 0, tiled=True, axis_index_groups=groups)  32.5 us
    all_to_all x1, waiting for transfers between devices, local(): lax.all_to_all(send.reshape(DEVICES, SLOTS, scen), ('line', 'bus'), 0, 0,...  16.6 us
    all_to_all x1, waiting for transfers between devices, local(): lax.all_to_all(chip.reshape(HALF, block, scen), 'line', 0, 0, tiled=True,...  15.8 us
    all_to_all x1, waiting for transfers between devices, local(): lax.all_to_all(partial_flows.reshape(BUSES_AT, rows, scen), 'bus', 0, 0,...  14.2 us
    dot_general x1, matrix products, local(): lax.dot_general(ptdf, inject, (((1,), (1,)), ((), ())), preferred_element...  11.2 us
    all_to_all x1, waiting for transfers between devices, share(): lax.all_to_all(spread, axis, 0, 0, tiled=True, axis_index_groups=groups)  9.83 us
    unnamed x10, local copies, waits for them, and re-layouts  9.45 us
    dot_general x1, matrix products, local(): lax.dot_general(ptdf, dual, (((0,), (0,)), ((), ())), preferred_element_t...  9.08 us
  transfers between devices with their start and end apart: 7, of which 6 were waited for; matrix products, arithmetic and copies ran while one was open for 15% of the time, Pallas kernels for 0%

profile of v1, /device:TPU:3, one launch (start us, length us, event | category | flops | bytes accessed | tf_op | source)
XLA Modules:
  0.0 193.2 jit_solution(16412405464288954711)
XLA Ops:
  0.0 1.2 broadcast_in_dim.18
  1.2 32.5 %all_to_all.34 = bf16[8,16,8832]{2,1,0:T(8,128)(2,1)S(1)} all-to-all(bf16[8,16,8832]{2,1,0:T(8,128)(2,1)S(1)} %broadcast_in_dim.18), channel_id=1, replica_groups={{0,16,32,48,64,80,96,112},{8,24,40,56,72,88,104,120},{1,17,33,49,65,81,..., dimensions={0} | all-to-all | bytes 4521984 | tf_op jit(solution)/shard_map/all_to_all | solution.py:26
  33.7 2.3 %collective-permute-start = (bf16[128,8832]{1,0:T(8,128)(2,1)S(1)}, bf16[128,8832]{1,0:T(8,128)(2,1)}, u32[]{:S(2)}, u32[]{:S(2)}) collective-permute-start(bf16[128,8832]{1,0:T(8,128)(2,1)S(1)} %bitcast.53), channel_id=1, source_target_pairs={{0,8},{8,0},{16,24},{24,16},{32,40},{40,32},{48,56},{56,48},{64,72... | collective-permute-start | bytes 6782984 | tf_op jit(solution)/shard_map/ppermute | solution.py:62
  36.0 4.2 %collective-permute-done = bf16[128,8832]{1,0:T(8,128)(2,1)} collective-permute-done((bf16[128,8832]{1,0:T(8,128)(2,1)S(1)}, bf16[128,8832]{1,0:T(8,128)(2,1)}, u32[]{:S(2)}, u32[]{:S(2)}) %collective-permute-start) | collective-permute-done | bytes 2261024 | tf_op jit(solution)/shard_map/ppermute | solution.py:62
  40.1 11.2 %fusion.9 = f32[32,8,8,128]{3,2,1,0:T(8,128)} fusion(bf16[1024,8832]{1,0:T(8,128)(2,1)} %param.7, bf16[128,8832]{1,0:T(8,128)(2,1)} %collective-permute-done, bf16[128,8832]{1,0:T(8,128)(2,1)S(1)} %bitcast.54, pred[]{:T(512)S(6)} %eq.110), kind=kOutput, calls=%fused_computation.16 | convolution fusion | flops 4650860544 | bytes 23658496 | tf_op jit(solution)/shard_map/dot_general | solution.py:68
  51.4 2.3 %copy.85 = f32[32,8,8,128]{3,2,0,1:T(8,128)} copy(f32[32,8,8,128]{3,2,1,0:T(8,128)} %fusion.9) | data formatting | bytes 2097152 | tf_op jit(solution)/shard_map/reshape | solution.py:72
  53.6 5.8 %all-to-all-start.2 = ((f32[8,128,256]{1,2,0:T(8,128)}), f32[8,128,256]{1,2,0:T(8,128)S(1)}, u32[]{:S(2)}, u32[]{:S(2)}) async-start(f32[8,128,256]{1,2,0:T(8,128)} %bitcast.49), calls=%async_computation.2 | async-start | bytes 2097152 | tf_op jit(solution)/shard_map/all_to_all | solution.py:72
  59.4 0.8 dynamic_slice.29
  60.2 0.8 dynamic_slice.27
  60.9 0.1 copy.81
  61.1 0.8 add_convert_fusion
  61.8 14.2 %all-to-all-done.2 = f32[8,128,256]{1,2,0:T(8,128)S(1)} async-done(((f32[8,128,256]{1,2,0:T(8,128)}), f32[8,128,256]{1,2,0:T(8,128)S(1)}, u32[]{:S(2)}, u32[]{:S(2)}) %all-to-all-start.2) | async-done | bytes 1048608 | tf_op jit(solution)/shard_map/all_to_all | solution.py:72
  76.0 0.1 reduce_sum.38
  76.1 0.1 copy.71
  76.2 0.8 broadcast_in_dim.19
  77.1 3.5 %all-to-all-start.3 = ((bf16[8,128,256]{2,1,0:T(8,128)(2,1)}), bf16[8,128,256]{2,1,0:T(8,128)(2,1)S(1)}, u32[]{:S(2)}, u32[]{:S(2)}) async-start(bf16[8,128,256]{2,1,0:T(8,128)(2,1)} %broadcast_in_dim.19), calls=%async_computation.3 | async-start | bytes 1048576 | tf_op jit(solution)/shard_map/all_to_all | solution.py:26
  80.6 9.8 %all-to-all-done.3 = bf16[8,128,256]{2,1,0:T(8,128)(2,1)S(1)} async-done(((bf16[8,128,256]{2,1,0:T(8,128)(2,1)}), bf16[8,128,256]{2,1,0:T(8,128)(2,1)S(1)}, u32[]{:S(2)}, u32[]{:S(2)}) %all-to-all-start.3) | async-done | bytes 524320 | tf_op jit(solution)/shard_map/all_to_all | solution.py:26
  90.4 9.1 %fusion.19 = f32[256,8832]{1,0:T(8,128)S(1)} fusion(bf16[1024,256]{1,0:T(8,128)(2,1)S(1)} %bitcast.52, bf16[1024,8832]{1,0:T(8,128)(2,1)} %param.7), kind=kOutput, calls=%fused_computation.45 | convolution fusion | flops 4630511616 | bytes 27656192 | tf_op jit(solution)/shard_map/dot_general | solution.py:80
  99.5 3.5 %copy-done.2 = f32[256,8832]{1,0:T(8,128)} copy-done((f32[256,8832]{1,0:T(8,128)}, f32[256,8832]{1,0:T(8,128)S(1)}, u32[]{:S(2)}) %copy-start.2) | copy-done | bytes 9043992
  103.0 0.7 fusion.8
  103.6 2.5 %copy.73 = bf16[4416,256]{1,0:T(8,128)(2,1)} copy(bf16[4416,256]{0,1:T(8,128)(2,1)S(1)} %fusion.8) | data formatting | bytes 4521984 | tf_op jit(solution)/shard_map/convert_element_type | solution.py:85
  106.1 2.7 %collective-permute-start.1 = (bf16[4416,256]{1,0:T(8,128)(2,1)}, bf16[4416,256]{1,0:T(8,128)(2,1)S(1)}, u32[]{:S(2)}, u32[]{:S(2)}) collective-permute-start(bf16[4416,256]{1,0:T(8,128)(2,1)} %copy.73), channel_id=1, source_target_pairs={{0,8},{8,0},{16,24},{24,16},{32,40},{40,32},{48,56},{56,48},{64,72... | collective-permute-start | bytes 6782984 | tf_op jit(solution)/shard_map/ppermute | solution.py:85
  108.9 0.1 ne.72
  109.1 0.1 rem.52
  109.2 0.1 div.28
  109.4 5.7 %constant_dynamic-slice_fusion = f32[256,4416]{1,0:T(8,128)} fusion(f32[256,8832]{1,0:T(8,128)} %copy-done.2, s32[]{:T(128)S(6)} %select_n.70), kind=kLoop, calls=%fused_computation.40 | loop fusion | bytes 9043972 | tf_op jit(solution)/shard_map/dynamic-slice
  115.2 5.9 %copy.82 = f32[256,4416]{0,1:T(8,128)} copy(f32[256,4416]{1,0:T(8,128)} %constant_dynamic-slice_fusion) | data formatting | bytes 9043968
  121.1 4.2 %fusion.6 = bf16[4416,256]{1,0:T(8,128)(2,1)} fusion(f32[256,4416]{0,1:T(8,128)} %copy.82, bf16[4416,256]{1,0:T(8,128)(2,1)S(1)} %collective-permute-done.1), kind=kLoop, calls=%fused_computation.10 | loop fusion | flops 3391488 | bytes 9043968 | tf_op jit(solution)/shard_map/convert_element_type | solution.py:86
  125.3 5.3 %all-to-all-start.4 = ((bf16[8,552,256]{2,1,0:T(8,128)(2,1)}), bf16[8,552,256]{2,1,0:T(8,128)(2,1)S(1)}, u32[]{:S(2)}, u32[]{:S(2)}) async-start(bf16[8,552,256]{2,1,0:T(8,128)(2,1)} %bitcast.16), calls=%async_computation.4 | async-start | bytes 4521984 | tf_op jit(solution)/shard_map/all_to_all | solution.py:87
  130.6 0.1 iota_compare_fusion
  130.7 6.1 %convert_reduce_fusion = s32[16,552]{1,0:T(8,128)S(1)} fusion(s32[16,552]{1,0:T(8,128)S(1)} %get-tuple-element.6, pred[552,552]{1,0:T(8,128)(4,1)S(1)} %iota_compare_fusion), kind=kLoop, calls=%fused_computation | loop fusion | flops 19492224 | bytes 375360 | tf_op jit(solution)/shard_map/reduce_sum | solution.py:35
  136.9 0.1 broadcast_compare_fusion.1
  137.0 2.2 %select_reduce_fusion = s32[8,16,8]{2,1,0:T(8,128)S(1)} fusion(s32[16,552]{1,0:T(8,128)S(1)} %get-tuple-element.5, pred[16,8,552]{2,1,0:T(8,128)(4,1)S(1)} %iota_compare_fusion.2, pred[8,16,552]{2,1,0:T(8,128)(4,1)S(1)} %broadcast_compare_fusion.1), kind=kLoop, calls=%fused_computation.13 | loop fusion | flops 1694720 | bytes 180736 | tf_op jit(solution)/shard_map/reduce_sum | solution.py:54
  139.3 0.7 all_to_all.21
  140.0 0.4 broadcast_compare_fusion
  140.4 2.2 %copy.78 = pred[128,8,552]{2,1,0:T(8,128)(4,1)} copy(pred[128,8,552]{0,2,1:T(8,128)(4,1)S(1)} %broadcast_compare_fusion) | data formatting | bytes 1130496 | tf_op jit(solution)/shard_map/eq | solution.py:59
  142.6 15.8 %all-to-all-done.4 = bf16[8,552,256]{2,1,0:T(8,128)(2,1)S(1)} async-done(((bf16[8,552,256]{2,1,0:T(8,128)(2,1)}), bf16[8,552,256]{2,1,0:T(8,128)(2,1)S(1)}, u32[]{:S(2)}, u32[]{:S(2)}) %all-to-all-start.4) | async-done | bytes 2261024 | tf_op jit(solution)/shard_map/all_to_all | solution.py:87
  158.3 3.3 %all-to-all-start = ((s32[8,1,128]{2,1,0:T(1,128)}), s32[8,1,128]{2,1,0:T(1,128)S(1)}, u32[]{:S(2)}, u32[]{:S(2)}) async-start(s32[8,1,128]{2,1,0:T(1,128)} %bitcast.3), calls=%async_computation | async-start | bytes 8192 | tf_op jit(solution)/shard_map/all_to_all | solution.py:55
  161.7 0.3 convert_reduce_fusion.1
  162.0 3.5 %fusion.10 = f32[128,8,256]{2,1,0:T(8,128)} fusion(pred[128,8,552]{2,1,0:T(8,128)(4,1)} %copy.78, f32[552,256]{1,0:T(8,128)S(1)} %convert_reduce_fusion.1), kind=kOutput, calls=%fused_computation.20 | convolution fusion | flops 1736441856 | bytes 2179072 | tf_op jit(solution)/shard_map/dot_general | solution.py:92
  165.5 2.5 %all-to-all-done = s32[8,1,128]{2,1,0:T(1,128)S(1)} async-done(((s32[8,1,128]{2,1,0:T(1,128)}), s32[8,1,128]{2,1,0:T(1,128)S(1)}, u32[]{:S(2)}, u32[]{:S(2)}) %all-to-all-start) | async-done | bytes 4128 | tf_op jit(solution)/shard_map/all_to_all | solution.py:55
  168.0 6.6 %all-to-all-start.5 = ((f32[128,8,256]{2,1,0:T(8,128)}), f32[128,8,256]{2,1,0:T(8,128)S(1)}, u32[]{:S(2)}, u32[]{:S(2)}) async-start(f32[128,8,256]{2,1,0:T(8,128)} %fusion.10), calls=%async_computation.5 | async-start | bytes 2097152 | tf_op jit(solution)/shard_map/all_to_all | solution.py:93
  174.6 0.1 sub.37
  174.8 0.1 sub.39
  174.9 16.6 %all-to-all-done.5 = f32[128,8,256]{2,1,0:T(8,128)S(1)} async-done(((f32[128,8,256]{2,1,0:T(8,128)}), f32[128,8,256]{2,1,0:T(8,128)S(1)}, u32[]{:S(2)}, u32[]{:S(2)}) %all-to-all-start.5) | async-done | bytes 1048608 | tf_op jit(solution)/shard_map/all_to_all | solution.py:93
  191.5 0.3 copy.75
  191.8 0.6 convolution_bitcast_fusion
  192.5 0.7 copy.77
  (28 shorter events, 0.4 us)
Async XLA Ops:
  0.0 60.9 %copy-start = (s32[1024,256]{1,0:T(8,128)S(1)}, s32[1024,256]{1,0:T(8,128)}, u32[]{:S(2)}) copy-start(s32[1024,256]{1,0:T(8,128)} %param.9) | copy-start | bytes 3145732
  33.7 6.5 %collective-permute-start = (bf16[128,8832]{1,0:T(8,128)(2,1)S(1)}, bf16[128,8832]{1,0:T(8,128)(2,1)}, u32[]{:S(2)}, u32[]{:S(2)}) collective-permute-start(bf16[128,8832]{1,0:T(8,128)(2,1)S(1)} %bitcast.53), channel_id=1, source_target_pairs={{0,8},{8,0},{16,24},{24,16},{32,40},{40,32},{48,56},{56,48},{64,72... | collective-permute-start | bytes 6782984 | tf_op jit(solution)/shard_map/ppermute | solution.py:62
  53.6 22.4 %all-to-all-start.2 = ((f32[8,128,256]{1,2,0:T(8,128)}), f32[8,128,256]{1,2,0:T(8,128)S(1)}, u32[]{:S(2)}, u32[]{:S(2)}) async-start(f32[8,128,256]{1,2,0:T(8,128)} %bitcast.49), calls=%async_computation.2 | async-start | bytes 2097152 | tf_op jit(solution)/shard_map/all_to_all | solution.py:72
  77.1 13.3 %all-to-all-start.3 = ((bf16[8,128,256]{2,1,0:T(8,128)(2,1)}), bf16[8,128,256]{2,1,0:T(8,128)(2,1)S(1)}, u32[]{:S(2)}, u32[]{:S(2)}) async-start(bf16[8,128,256]{2,1,0:T(8,128)(2,1)} %broadcast_in_dim.19), calls=%async_computation.3 | async-start | bytes 1048576 | tf_op jit(solution)/shard_map/all_to_all | solution.py:26
  99.5 3.5 %copy-start.2 = (f32[256,8832]{1,0:T(8,128)}, f32[256,8832]{1,0:T(8,128)S(1)}, u32[]{:S(2)}) copy-start(f32[256,8832]{1,0:T(8,128)S(1)} %fusion.19) | copy-start | bytes 27131908
  103.0 5.9 %copy-start.3 = (s32[8832]{0:T(1024)S(1)}, s32[8832]{0:T(1024)}, u32[]{:S(2)}) copy-start(s32[8832]{0:T(1024)} %param.13) | copy-start | bytes 105988
  106.1 14.9 %collective-permute-start.1 = (bf16[4416,256]{1,0:T(8,128)(2,1)}, bf16[4416,256]{1,0:T(8,128)(2,1)S(1)}, u32[]{:S(2)}, u32[]{:S(2)}) collective-permute-start(bf16[4416,256]{1,0:T(8,128)(2,1)} %copy.73), channel_id=1, source_target_pairs={{0,8},{8,0},{16,24},{24,16},{32,40},{40,32},{48,56},{56,48},{64,72... | collective-permute-start | bytes 6782984 | tf_op jit(solution)/shard_map/ppermute | solution.py:85
  125.3 33.1 %all-to-all-start.4 = ((bf16[8,552,256]{2,1,0:T(8,128)(2,1)}), bf16[8,552,256]{2,1,0:T(8,128)(2,1)S(1)}, u32[]{:S(2)}, u32[]{:S(2)}) async-start(bf16[8,552,256]{2,1,0:T(8,128)(2,1)} %bitcast.16), calls=%async_computation.4 | async-start | bytes 4521984 | tf_op jit(solution)/shard_map/all_to_all | solution.py:87
  158.3 9.7 %all-to-all-start = ((s32[8,1,128]{2,1,0:T(1,128)}), s32[8,1,128]{2,1,0:T(1,128)S(1)}, u32[]{:S(2)}, u32[]{:S(2)}) async-start(s32[8,1,128]{2,1,0:T(1,128)} %bitcast.3), calls=%async_computation | async-start | bytes 8192 | tf_op jit(solution)/shard_map/all_to_all | solution.py:55
  161.7 31.5 %copy-start.1 = (s32[1024,256]{1,0:T(8,128)S(1)}, s32[1024,256]{1,0:T(8,128)}, u32[]{:S(2)}) copy-start(s32[1024,256]{1,0:T(8,128)} %param.9) | copy-start | bytes 3145732
  168.0 23.4 %all-to-all-start.5 = ((f32[128,8,256]{2,1,0:T(8,128)}), f32[128,8,256]{2,1,0:T(8,128)S(1)}, u32[]{:S(2)}, u32[]{:S(2)}) async-start(f32[128,8,256]{2,1,0:T(8,128)} %fusion.10), calls=%async_computation.5 | async-start | bytes 2097152 | tf_op jit(solution)/shard_map/all_to_all | solution.py:93

commit v2 on v1

v2 whole, which is shorter than its diff:
```python
import functools

import jax
import jax.numpy as jnp
from jax import lax
from jax.experimental import pallas as pl
from jax.experimental.pallas import tpu as pltpu
from jax.sharding import PartitionSpec as P

GENS = 10368
LINES_AT = 16
BUSES_AT = 8
DEVICES = LINES_AT * BUSES_AT
HELD = GENS // DEVICES
SLOTS = 8
FILLED = 5
TILE = 128
PAIRS = [(i, i ^ 1) for i in range(LINES_AT)]
SAME_CORE = [[a + c for a in range(0, LINES_AT, 2)] for c in (0, 1)]
HALF = LINES_AT // 2
BF16, F32 = jnp.bfloat16, jnp.float32
NT = (((1,), (1,)), ((), ()))


def share(x, axis, ways, groups=None):
    spread = jnp.broadcast_to(x[None], (ways,) + x.shape)
    return lax.all_to_all(spread, axis, 0, 0, tiled=True, axis_index_groups=groups)


def ranks(groups):
    count = groups.shape[-1]
    same = groups[..., :, None] == groups[..., None, :]
    earlier = lax.broadcasted_iota(jnp.int32, (count, count), 0) > lax.broadcasted_iota(
        jnp.int32, (count, count), 1
    )
    return jnp.sum((same & earlier).astype(jnp.int32), axis=-1)


def split3(x):
    a = x.astype(BF16)
    rest = x - a.astype(F32)
    b = rest.astype(BF16)
    return a, b, (rest - b.astype(F32)).astype(BF16)


def call(kernel, out, cost, operands, scalars=(), slab=None, scratch=(), out_specs=None):
    whole = pl.BlockSpec(memory_space=pltpu.VMEM)
    specs = [whole] * len(operands)
    if slab:
        specs[0] = pl.BlockSpec(memory_space=pl.ANY)
        shape, parts = slab
        scratch = [pltpu.VMEM(shape, BF16), pltpu.SemaphoreType.DMA((parts,)), *scratch]
    return pl.pallas_call(
        kernel,
        out_shape=out,
        in_specs=[pl.BlockSpec(memory_space=pltpu.SMEM)] * len(scalars) + specs,
        out_specs=out_specs or whole,
        scratch_shapes=scratch,
        compiler_params=pltpu.CompilerParams(vmem_limit_bytes=40 << 20),
        cost_estimate=pl.CostEstimate(flops=cost[0], bytes_accessed=cost[1], transcendentals=0),
    )(*scalars, *operands)


def flows_kernel(ptdf, held, other, out, slab, sems):
    step = ptdf.shape[0] // sems.shape[0]
    copies = [
        pltpu.make_async_copy(ptdf.at[at], slab.at[at], sems.at[i])
        for i, at in enumerate(pl.ds(i * step, step) for i in range(sems.shape[0]))
    ]
    for copy in copies:
        copy.start()
    right = jnp.concatenate([held[...], other[...]], 0)
    for i, copy in enumerate(copies):
        copy.wait()
        at = slice(i * step, (i + 1) * step)
        out[at, :] = lax.dot_general(slab[at, :], right, NT, preferred_element_type=F32)


def dual_kernel(core, parts, mask, sign, limit, price, out):
    flows = parts[0]
    for i in range(1, parts.shape[0]):
        flows = flows + parts[i]
    flows = flows.T
    half = flows.shape[0] // 2
    swapped = jnp.concatenate([flows[half:], flows[:half]], 0)
    flows = jnp.where(core[0] == 0, flows, swapped)
    direction = (2 * sign[...] - 1).astype(F32)
    dual = (mask[...].astype(F32) * price[...] * (direction * flows - limit[...])).astype(BF16)
    for i in range(out.shape[0]):
        out[i] = dual


def cut_rows(start, ptdf, dual, slab, sems, put):
    step = slab.shape[1] // sems.shape[0]
    copies = [
        pltpu.make_async_copy(
            ptdf.at[:, pl.ds(pl.multiple_of(start + i * step, TILE), step)],
            slab.at[:, pl.ds(i * step, step)],
            sems.at[i],
        )
        for i in range(sems.shape[0])
    ]
    for copy in copies:
        copy.start()
    left = jnp.concatenate([dual[b] for b in range(dual.shape[0])], 1)
    for i, copy in enumerate(copies):
        copy.wait()
        tile = slab[:, i * step : (i + 1) * step]
        put(slice(i * step, (i + 1) * step), jnp.dot(left, tile, preferred_element_type=F32).T)


def give_kernel(core, ptdf, dual, out, slab, sems, *, first):
    def put(at, rows):
        out[at, :] = rows.astype(BF16)

    cut_rows((1 - core[0]) * first, ptdf, dual, slab, sems, put)


def keep_kernel(core, ptdf, dual, got, out, slab, sems, held, sem, *, first):
    def put(at, rows):
        held[at, :] = (rows + got[at, :].astype(F32)).astype(BF16)

    cut_rows(core[0] * first, ptdf, dual, slab, sems, put)
    spare = held.shape[0] - out.shape[0]
    copy = pltpu.make_async_copy(
        held.at[pl.ds(pl.multiple_of(core[0] * spare, 16), out.shape[0])], out, sem
    )
    copy.start()
    copy.wait()


def pick_kernel(to, what, parts, out):
    total = parts[0].astype(F32)
    for i in range(1, parts.shape[0]):
        total = total + parts[i].astype(F32)
    at = lax.broadcasted_iota(jnp.int32, (out.shape[0], to.shape[1]), 0)
    pick = (at == to[0:1, :]).astype(BF16)
    mark = (at == to[1:2, :]).astype(BF16)
    slot = lax.broadcasted_iota(jnp.int32, (to.shape[1], out.shape[1]), 1)
    names = jnp.where(slot == what[:, 0:1], what[:, 1:2], 0).astype(F32).astype(BF16)
    dot = lambda x, y: jnp.dot(x, y, preferred_element_type=F32)
    a, b, c = split3(total)
    out[...] = dot(pick, a) + dot(pick, b) + dot(pick, c) + dot(mark, names)


def merge_kernel(terms, out):
    rows, scen = out.shape
    dot = lambda x, y: jnp.dot(x, y, preferred_element_type=F32)
    names = terms[:, SLOTS - 1, :].T
    gen = lax.broadcasted_iota(jnp.int32, (rows, DEVICES), 0).astype(F32) + 1
    total = jnp.zeros((rows, scen), F32)
    for i in range(FILLED):
        merge = (gen == names[i : i + 1, :]).astype(BF16)
        a, b, c = split3(terms[:, i, :])
        total = total + dot(merge, a) + dot(merge, b) + dot(merge, c)
    width = scen // LINES_AT
    at = lax.broadcasted_iota(jnp.int32, (scen, scen), 0)
    goes = at - at
    for i in range(LINES_AT):
        goes = jnp.where(at // width == i, at + ((i % HALF) * 2 + i // HALF - i) * width, goes)
    order = (goes == lax.broadcasted_iota(jnp.int32, (scen, scen), 1)).astype(BF16)
    a, b, c = split3(total)
    out[...] = dot(a, order) + dot(b, order) + dot(c, order)


def local(ptdf, injections, viol_mask, viol_sign, limit, price, owner):
    line, bus = lax.axis_index("line"), lax.axis_index("bus")
    core = line % 2
    at_core = core.astype(jnp.int32)[None]
    lines, buses = ptdf.shape
    rows = lines // BUSES_AT
    block = buses // LINES_AT
    half = buses // 2
    first = half // TILE * TILE
    window = buses - first
    scen = viol_mask.shape[1]
    width = scen // LINES_AT
    shape = jax.ShapeDtypeStruct
    held = share(injections.T, "line", HALF, SAME_CORE).reshape(scen // 2, buses)

    owners = lax.dynamic_slice_in_dim(owner, (core * HALF + line // 2) * block, block, 0)
    groups, within = owners // HELD, owners % HELD
    place = ranks(groups)
    to = jnp.stack([groups * SLOTS + place, groups * SLOTS + SLOTS - 1])
    what = jnp.stack([place, within + 1], axis=1)
    cut = lambda x: lax.dynamic_slice_in_dim(x, bus * rows, rows, 0)
    mask = cut(viol_mask).T.reshape(HALF, 2, width, rows).transpose(1, 0, 2, 3).reshape(scen, rows)
    sign, limit, price = (cut(x)[None, :] for x in (viol_sign, limit, price))
    held, to, what, mask, sign, limit, price = lax.optimization_barrier(
        (held, to, what, mask, sign, limit, price)
    )

    other = lax.ppermute(held, "line", PAIRS)
    work = 2 * lines * buses * scen
    partial_flows = call(
        flows_kernel,
        shape((lines, scen), F32),
        (work, 2 * lines * buses),
        (ptdf, held, other),
        slab=((lines, buses), 4),
    )
    parts = lax.all_to_all(partial_flows.reshape(BUSES_AT, rows, scen), "bus", 0, 0, tiled=True)
    dual = call(
        dual_kernel,
        shape((BUSES_AT, scen, rows), BF16),
        (10 * rows * scen, 8 * lines * scen),
        (parts, mask, sign, limit, price),
        (at_core,),
    )
    dual = lax.all_to_all(dual, "bus", 0, 0, tiled=True)

    give = call(
        functools.partial(give_kernel, first=first),
        shape((window, scen), BF16),
        (work // 2, lines * buses),
        (ptdf, dual),
        (at_core,),
        slab=((lines, window), 5),
    )
    got = lax.ppermute(give, "line", PAIRS)
    chip = call(
        functools.partial(keep_kernel, first=first),
        shape((half, scen), BF16),
        (work // 2, lines * buses),
        (ptdf, dual, got),
        (at_core,),
        slab=((lines, window), 5),
        scratch=[pltpu.VMEM((window, scen), BF16), pltpu.SemaphoreType.DMA],
        out_specs=pl.BlockSpec(memory_space=pl.ANY),
    )
    parts = lax.all_to_all(
        chip.reshape(HALF, block, scen), "line", 0, 0, tiled=True, axis_index_groups=SAME_CORE
    )
    send = call(
        pick_kernel,
        shape((DEVICES * SLOTS, scen), F32),
        (6 * DEVICES * SLOTS * block * scen, 2 * half * scen),
        (to, what, parts),
    )
    terms = lax.all_to_all(
        send.reshape(DEVICES, SLOTS, scen), ("line", "bus"), 0, 0, tiled=True
    )
    return call(
        merge_kernel,
        shape((HELD, scen), F32),
        (6 * DEVICES * SLOTS * HELD * scen, 4 * DEVICES * SLOTS * scen),
        (terms,),
    )


def solution(mesh):
    placed = (
        P("line", "bus"),
        P("bus", "line"),
        P("line", None),
        P("line"),
        P("line"),
        P("line"),
        P("bus"),
    )
    return jax.shard_map(
        local, mesh=mesh, in_specs=placed, out_specs=P(("line", "bus"), None), check_vma=False
    )
```

time: 196 us -> 171 us (0.87)
  Pallas kernels: 0 us -> 31.5 us
  matrix products: 24.5 us -> 0 us
  blocking collectives: 32.5 us -> 56.3 us
  local copies, waits for them, and re-layouts: 28.9 us -> 7.65 us
  starting transfers between devices: 29.5 us -> 14.1 us
  other arithmetic: 14.5 us -> 1.08 us
  waiting for transfers between devices: 63 us -> 58.2 us
    all_to_all x3 -> x0, waiting for transfers between devices: 33.3 us -> none  [the longest x1 16.6 us: local(): lax.all_to_all(send.reshape(DEVICES, SLOTS, scen), ('line', 'bus'), 0, 0,...]
    pallas_call x0 -> x6, Pallas kernels: none -> 31.5 us  [call(): pl.pallas_call(kernel, out_shape=out, in_specs=[pl.BlockSpec(memory_space...]
    dot_general x4 -> x0, matrix products: 24.5 us -> none  [the longest x1 11.2 us: local(): lax.dot_general(ptdf, inject, (((1,), (1,)), ((), ())), preferred_element...]
    all_to_all x1 -> x3, blocking collectives: 32.5 us -> 56.3 us  [the longest x1 21.9 us: local(): lax.all_to_all(partial_flows.reshape(BUSES_AT, rows, scen), 'bus', 0, 0,...]
    all_to_all x3 -> x0, starting transfers between devices: 15.7 us -> none  [the longest x1 6.6 us: local(): lax.all_to_all(send.reshape(DEVICES, SLOTS, scen), ('line', 'bus'), 0, 0,...]
    all_to_all x1, waiting for transfers between devices: 9.83 us -> 23.2 us  [share(): lax.all_to_all(spread, axis, 0, 0, tiled=True, axis_index_groups=groups)]
    all_to_all x1, waiting for transfers between devices: 15.8 us -> 26.9 us  [local(): lax.all_to_all(chip.reshape(HALF, block, scen), 'line', 0, 0, tiled=True,...]
    unnamed x10 -> x5, local copies, waits for them, and re-layouts: 9.45 us -> 1.71 us
  transfers between devices with their start and end apart: 7 -> 4, of which waited for: 6 -> 4; matrix products, arithmetic and copies ran while one was open for 15% -> 3% of each run, Pallas kernels for 0% -> 0%
where the time goes in v2:
time: 171 us; the launch traced here: 169 us
  waiting for transfers between devices  58.2 us (34%)
  blocking collectives  56.3 us (33%)
  Pallas kernels  31.5 us (18%)
  starting transfers between devices  14.1 us (8%)
  local copies, waits for them, and re-layouts  7.65 us (4%)
    pallas_call x6, Pallas kernels, call(): pl.pallas_call(kernel, out_shape=out, in_specs=[pl.BlockSpec(memory_space...  31.5 us
    all_to_all x1, waiting for transfers between devices, local(): lax.all_to_all(chip.reshape(HALF, block, scen), 'line', 0, 0, tiled=True,...  26.9 us
    all_to_all x1, waiting for transfers between devices, share(): lax.all_to_all(spread, axis, 0, 0, tiled=True, axis_index_groups=groups)  23.2 us
    all_to_all x1, blocking collectives, local(): lax.all_to_all(partial_flows.reshape(BUSES_AT, rows, scen), 'bus', 0, 0,...  21.9 us
    all_to_all x1, blocking collectives, local(): lax.all_to_all(send.reshape(DEVICES, SLOTS, scen), ('line', 'bus'), 0, 0,...  21.3 us
    all_to_all x1, blocking collectives, local(): dual = lax.all_to_all(dual, 'bus', 0, 0, tiled=True)  13.1 us
    all_to_all x1, starting transfers between devices, share(): lax.all_to_all(spread, axis, 0, 0, tiled=True, axis_index_groups=groups)  6.21 us
    all_to_all x1, starting transfers between devices, local(): lax.all_to_all(chip.reshape(HALF, block, scen), 'line', 0, 0, tiled=True,...  4.43 us
  transfers between devices with their start and end apart: 4, of which 4 were waited for; matrix products, arithmetic and copies ran while one was open for 3% of the time, Pallas kernels for 0%

profile of v2, /device:TPU:3, one launch (start us, length us, event | category | flops | bytes accessed | tf_op | source)
XLA Modules:
  0.0 169.0 jit_solution(11090370713202071603)
XLA Ops:
  0.0 0.0 copy-start
  0.0 2.6 %broadcast_in_dim.20 = bf16[8,16,8832]{2,1,0:T(8,128)(2,1)} broadcast(bf16[16,8832]{1,0:T(8,128)(2,1)} %bitcast.24), dimensions={1,2} | broadcast | bytes 2543616 | tf_op jit(solution)/shard_map/broadcast_in_dim | solution.py:26
  2.6 6.2 %all-to-all-start = ((bf16[8,16,8832]{2,1,0:T(8,128)(2,1)}), bf16[8,16,8832]{2,1,0:T(8,128)(2,1)S(1)}, u32[]{:S(2)}, u32[]{:S(2)}) async-start(bf16[8,16,8832]{2,1,0:T(8,128)(2,1)} %broadcast_in_dim.20), calls=%async_computation | async-start | bytes 4521984 | tf_op jit(solution)/shard_map/all_to_all | solution.py:27
  8.8 0.8 multiply_add_fusion
  9.6 0.3 convert_reduce_fusion
  9.9 0.0 copy-done
  10.0 0.8 copy.19
  10.7 0.9 copy.17
  11.6 0.8 dynamic-slice_bitcast_fusion.2.sign
  12.4 0.8 dynamic-slice_bitcast_fusion
  13.2 23.2 %all-to-all-done = bf16[8,16,8832]{2,1,0:T(8,128)(2,1)S(1)} async-done(((bf16[8,16,8832]{2,1,0:T(8,128)(2,1)}), bf16[8,16,8832]{2,1,0:T(8,128)(2,1)S(1)}, u32[]{:S(2)}, u32[]{:S(2)}) %all-to-all-start) | async-done | bytes 2261024 | tf_op jit(solution)/shard_map/all_to_all | solution.py:27
  36.4 0.8 collective-permute-start
  37.3 4.0 %collective-permute-done.other = bf16[128,8832]{1,0:T(8,128)(2,1)S(1)} collective-permute-done((bf16[128,8832]{1,0:T(8,128)(2,1)S(1)}, bf16[128,8832]{1,0:T(8,128)(2,1)S(1)}, u32[]{:S(2)}, u32[]{:S(2)}) %collective-permute-start) | collective-permute-done | bytes 2261024 | tf_op jit(solution)/shard_map/ppermute | solution.py:193
  41.3 12.5 %shard_map.73 = f32[1024,256]{1,0:T(8,128)S(1)} custom-call(bf16[1024,8832]{1,0:T(8,128)(2,1)} %ptdf.5, bf16[128,8832]{1,0:T(8,128)(2,1)S(1)} %bitcast.19, bf16[128,8832]{1,0:T(8,128)(2,1)S(1)} %collective-permute-done.other), custom_call_target="tpu_custom_call" | custom-call | flops 4630511616 | bytes 18087936 | tf_op jit(solution)/shard_map/pallas_call | solution.py:53
  53.8 21.9 %all_to_all.25.parts = f32[8,128,256]{2,1,0:T(8,128)S(1)} all-to-all(f32[8,128,256]{2,1,0:T(8,128)S(1)} %bitcast.20), channel_id=1, replica_groups=mesh['line'=16,'bus'=8] {'bus'}, dimensions={0} | all-to-all | bytes 2097152 | tf_op jit(solution)/shard_map/all_to_all | solution.py:202
  75.7 0.1 shard_map.74
  75.8 13.1 %all_to_all.26.dual = bf16[8,256,128]{2,1,0:T(8,128)(2,1)S(1)} all-to-all(bf16[8,256,128]{2,1,0:T(8,128)(2,1)S(1)} %shard_map.74), channel_id=1, replica_groups=mesh['line'=16,'bus'=8] {'bus'}, dimensions={0} | all-to-all | bytes 1048576 | tf_op jit(solution)/shard_map/all_to_all | solution.py:210
  88.9 5.5 %shard_map.75 = bf16[4480,256]{1,0:T(8,128)(2,1)S(1)} custom-call(s32[1]{0:T(128)} %bitcast.9.core, bf16[1024,8832]{1,0:T(8,128)(2,1)} %ptdf.5, bf16[8,256,128]{2,1,0:T(8,128)(2,1)S(1)} %all_to_all.26.dual), custom_call_target="tpu_custom_call" | custom-call | flops 2315255808 | bytes 9043968 | tf_op jit(solution)/shard_map/pallas_call | solution.py:53
  94.3 2.6 %collective-permute-start.1 = (bf16[4480,256]{1,0:T(8,128)(2,1)S(1)}, bf16[4480,256]{1,0:T(8,128)(2,1)S(1)}, u32[]{:S(2)}, u32[]{:S(2)}) collective-permute-start(bf16[4480,256]{1,0:T(8,128)(2,1)S(1)} %shard_map.75), channel_id=1, source_target_pairs={{0,8},{8,0},{16,24},{24,16},{32,40},{40,32},{48,56},{56,48},{64,72... | collective-permute-start | bytes 6881288 | tf_op jit(solution)/shard_map/ppermute | solution.py:220
  97.0 4.1 %collective-permute-done.1.got = bf16[4480,256]{1,0:T(8,128)(2,1)S(1)} collective-permute-done((bf16[4480,256]{1,0:T(8,128)(2,1)S(1)}, bf16[4480,256]{1,0:T(8,128)(2,1)S(1)}, u32[]{:S(2)}, u32[]{:S(2)}) %collective-permute-start.1) | collective-permute-done | bytes 2293792 | tf_op jit(solution)/shard_map/ppermute | solution.py:220
  101.0 7.0 %shard_map.76 = bf16[4416,256]{1,0:T(8,128)(2,1)} custom-call(s32[1]{0:T(128)} %bitcast.9.core, bf16[1024,8832]{1,0:T(8,128)(2,1)} %ptdf.5, bf16[8,256,128]{2,1,0:T(8,128)(2,1)S(1)} %all_to_all.26.dual, bf16[4480,256]{1,0:T(8,128)(2,1)S(1)} %collective-permute-done.1.got), custom_call_target="tpu_custom_call" | custom-call | flops 2315255808 | bytes 9043968 | tf_op jit(solution)/shard_map/pallas_call | solution.py:53
  108.1 4.4 %all-to-all-start.3 = ((bf16[8,552,256]{2,1,0:T(8,128)(2,1)}), bf16[8,552,256]{2,1,0:T(8,128)(2,1)S(1)}, u32[]{:S(2)}, u32[]{:S(2)}) async-start(bf16[8,552,256]{2,1,0:T(8,128)(2,1)} %bitcast.11), calls=%async_computation.3 | async-start | bytes 4521984 | tf_op jit(solution)/shard_map/all_to_all | solution.py:231
  112.5 0.9 copy.18.what
  113.4 26.9 %all-to-all-done.3.parts = bf16[8,552,256]{2,1,0:T(8,128)(2,1)S(1)} async-done(((bf16[8,552,256]{2,1,0:T(8,128)(2,1)}), bf16[8,552,256]{2,1,0:T(8,128)(2,1)S(1)}, u32[]{:S(2)}, u32[]{:S(2)}) %all-to-all-start.3) | async-done | bytes 2261024 | tf_op jit(solution)/shard_map/all_to_all | solution.py:231
  140.2 0.0 copy-start.1
  140.2 1.0 copy-done.1
  141.2 2.0 %shard_map.77 = f32[1024,256]{1,0:T(8,128)S(1)} custom-call(s32[2,552]{1,0:T(2,128)S(1)} %pad_add_fusion.to, s32[552,2]{1,0:T(8,128)S(1)} %copy-done.1, bf16[8,552,256]{2,1,0:T(8,128)(2,1)S(1)} %all-to-all-done.3.parts), custom_call_target="tpu_custom_call" | custom-call | flops 868220928 | bytes 2260992 | tf_op jit(solution)/shard_map/pallas_call | solution.py:53
  143.2 21.3 %all_to_all.27.terms = f32[128,8,256]{2,1,0:T(8,128)S(1)} all-to-all(f32[128,8,256]{2,1,0:T(8,128)S(1)} %bitcast.21), channel_id=1, replica_groups=mesh['line'=16,'bus'=8] {'line','bus'}, dimensions={0} | all-to-all | bytes 2097152 | tf_op jit(solution)/shard_map/all_to_all | solution.py:240
  164.5 4.4 %shard_map.78 = f32[81,256]{1,0:T(8,128)} custom-call(f32[128,8,256]{2,1,0:T(8,128)S(1)} %all_to_all.27.terms), custom_call_target="tpu_custom_call" | custom-call | flops 127401984 | bytes 1048576 | tf_op jit(solution)/shard_map/pallas_call | solution.py:53
  (8 shorter events, 0.1 us)
Async XLA Ops:
  0.0 9.9 %copy-start = (s32[1024,256]{1,0:T(8,128)S(1)}, s32[1024,256]{1,0:T(8,128)}, u32[]{:S(2)}) copy-start(s32[1024,256]{1,0:T(8,128)} %param.9) | copy-start | bytes 3145732
  2.6 33.8 %all-to-all-start = ((bf16[8,16,8832]{2,1,0:T(8,128)(2,1)}), bf16[8,16,8832]{2,1,0:T(8,128)(2,1)S(1)}, u32[]{:S(2)}, u32[]{:S(2)}) async-start(bf16[8,16,8832]{2,1,0:T(8,128)(2,1)} %broadcast_in_dim.20), calls=%async_computation | async-start | bytes 4521984 | tf_op jit(solution)/shard_map/all_to_all | solution.py:27
  36.4 4.9 %collective-permute-start = (bf16[128,8832]{1,0:T(8,128)(2,1)S(1)}, bf16[128,8832]{1,0:T(8,128)(2,1)S(1)}, u32[]{:S(2)}, u32[]{:S(2)}) collective-permute-start(bf16[128,8832]{1,0:T(8,128)(2,1)S(1)} %bitcast.18), channel_id=1, source_target_pairs={{0,8},{8,0},{16,24},{24,16},{32,40},{40,32},{48,56},{56,48},{64,72... | collective-permute-start | bytes 6782984 | tf_op jit(solution)/shard_map/ppermute | solution.py:193
  94.3 6.7 %collective-permute-start.1 = (bf16[4480,256]{1,0:T(8,128)(2,1)S(1)}, bf16[4480,256]{1,0:T(8,128)(2,1)S(1)}, u32[]{:S(2)}, u32[]{:S(2)}) collective-permute-start(bf16[4480,256]{1,0:T(8,128)(2,1)S(1)} %shard_map.75), channel_id=1, source_target_pairs={{0,8},{8,0},{16,24},{24,16},{32,40},{40,32},{48,56},{56,48},{64,72... | collective-permute-start | bytes 6881288 | tf_op jit(solution)/shard_map/ppermute | solution.py:220
  108.1 32.2 %all-to-all-start.3 = ((bf16[8,552,256]{2,1,0:T(8,128)(2,1)}), bf16[8,552,256]{2,1,0:T(8,128)(2,1)S(1)}, u32[]{:S(2)}, u32[]{:S(2)}) async-start(bf16[8,552,256]{2,1,0:T(8,128)(2,1)} %bitcast.11), calls=%async_computation.3 | async-start | bytes 4521984 | tf_op jit(solution)/shard_map/all_to_all | solution.py:231
  140.2 1.0 copy-start.1

commit v3 on v2

v3 whole, which is shorter than its diff:
```python
import jax
import jax.numpy as jnp
import numpy as np
from jax import lax
from jax.experimental import pallas as pl
from jax.experimental.pallas import tpu as pltpu
from jax.sharding import PartitionSpec as P

GENS = 10368
LINES_AT = 16
BUSES_AT = 8
DEVICES = LINES_AT * BUSES_AT
HELD = GENS // DEVICES
SLOTS = 8
TILE = 128
PAIRS = [(i, i ^ 1) for i in range(LINES_AT)]
SAME_CORE = [[a + c for a in range(0, LINES_AT, 2)] for c in (0, 1)]
HALF = LINES_AT // 2
BF16, F32 = jnp.bfloat16, jnp.float32
NT = (((1,), (1,)), ((), ()))


def along(dx, dz, dcore):
    pairs = []
    for x in range(2):
        for z in range(4):
            for core in range(2):
                to = ((x + dx) % 2, (z + dz) % 4, (core + dcore) % 2)
                pairs.append((x * 8 + z * 2 + core, to[0] * 8 + to[1] * 2 + to[2]))
    return pairs


ORDER = [
    [(0, 0, 0), (0, 0, 1), (1, 0, 0), (1, 0, 1), (0, 3, 1), (0, 1, 1)],
    [(0, 3, 0), (1, 3, 0), (0, 1, 0), (1, 1, 0), (1, 3, 1), (1, 1, 1)],
    [(0, 2, 1), (1, 2, 1), (0, 2, 0), (1, 2, 0)],
]


def gather(block, ready):
    move = lambda x, *to: lax.ppermute(x, "line", along(*to))
    stack = lambda *x: jnp.concatenate(x, 0)
    half = block.shape[0] // 2
    low, high = block[:half], block[half:]
    high_1, high_3 = move(high, 0, 1, 0), move(high, 0, 3, 0)
    beside = move(block, 1, 0, 0)
    high_2 = move(high_1, 0, 1, 0)
    pair = stack(low, beside[:half])
    pair_1, pair_3 = move(pair, 0, 1, 0), move(pair, 0, 3, 0)
    high_z = stack(high_1, high_3)
    high_zx = move(high_z, 1, 0, 0)
    high_2x = move(high_2, 1, 0, 0)
    pair_1, pair_3, ready = lax.optimization_barrier((pair_1, pair_3, ready))
    low_2, beside_2 = move(pair_1[:half], 0, 1, 0), move(pair_3[half:], 0, 3, 0)
    pieces = [
        stack(block, beside, high_z),
        stack(pair_1, pair_3, high_zx),
        stack(high_2, high_2x, low_2, beside_2),
    ]
    return pieces + [move(piece, 0, 0, 1) for piece in pieces], ready


def gathered(line, width):
    spots = np.array([(*at, core) for core in (0, 1) for at in sum(ORDER, [])])
    dx, dz, half, core = (np.repeat(spots[:, i], width // 2) for i in range(4))
    at = np.arange(dx.shape[0]) % (width // 2) + half * (width // 2)
    x, z, mine = line // 8, line // 2 % 4, line % 2
    device = (x + dx) % 2 * 8 + (z + dz) % 4 * 2 + (mine + core) % 2
    return device * width + at


def ranks(groups):
    count = groups.shape[-1]
    same = groups[..., :, None] == groups[..., None, :]
    earlier = lax.broadcasted_iota(jnp.int32, (count, count), 0) > lax.broadcasted_iota(
        jnp.int32, (count, count), 1
    )
    return jnp.sum((same & earlier).astype(jnp.int32), axis=-1)


def split3(x):
    a = x.astype(BF16)
    rest = x - a.astype(F32)
    b = rest.astype(BF16)
    return a, b, (rest - b.astype(F32)).astype(BF16)


def call(kernel, out, cost, operands, scalars=(), slab=None, limit=24):
    whole = pl.BlockSpec(memory_space=pltpu.VMEM)
    specs, scratch = [whole] * len(operands), []
    if slab:
        specs[0] = pl.BlockSpec(memory_space=pl.ANY)
        shape, parts = slab
        scratch = [pltpu.VMEM(shape, BF16), pltpu.SemaphoreType.DMA((parts,))]
    return pl.pallas_call(
        kernel,
        out_shape=out,
        in_specs=[pl.BlockSpec(memory_space=pltpu.SMEM)] * len(scalars) + specs,
        out_specs=whole,
        scratch_shapes=scratch,
        compiler_params=pltpu.CompilerParams(vmem_limit_bytes=limit << 20),
        cost_estimate=pl.CostEstimate(flops=cost[0], bytes_accessed=cost[1], transcendentals=0),
    )(*scalars, *operands)


def in_turn(copies, work):
    for copy in copies[:2]:
        copy.start()
    for i, copy in enumerate(copies):
        copy.wait()
        if i + 2 < len(copies):
            copies[i + 2].start()
        work(i)


def flows_kernel(ptdf, *refs):
    *pieces, out = refs
    right = jnp.concatenate([piece[...] for piece in pieces], 0)
    out[...] = lax.dot_general(ptdf[...], right, NT, preferred_element_type=F32)


def dual_kernel(goes, parts, mask, sign, limit, price, out):
    flows = jnp.sum(parts[...], 0)
    scen = flows.shape[1]
    order = (lax.broadcasted_iota(jnp.int32, (scen, scen), 0) == goes[...]).astype(BF16)
    dot = lambda x: lax.dot_general(order, x, NT, preferred_element_type=F32)
    a, b, c = split3(flows)
    flows = dot(a) + dot(b) + dot(c)
    direction = (2 * sign[...] - 1).astype(F32)
    dual = (mask[...].astype(F32) * price[...] * (direction * flows - limit[...])).astype(BF16)
    for i in range(out.shape[0]):
        out[i] = dual


def cut_rows(start, ptdf, dual, slab, sems, put):
    step = slab.shape[1] // sems.shape[0]
    left = jnp.concatenate([dual[b] for b in range(dual.shape[0])], 1)

    def work(i):
        at = slice(i * step, (i + 1) * step)
        put(at, jnp.dot(left, slab[:, at], preferred_element_type=F32).T)

    in_turn(
        [
            pltpu.make_async_copy(
                ptdf.at[:, pl.ds(pl.multiple_of(start + i * step, TILE), step)],
                slab.at[:, pl.ds(i * step, step)],
                sems.at[i],
            )
            for i in range(sems.shape[0])
        ],
        work,
    )


def cuts_kernel(start, ptdf, dual, out, slab, sems):
    def put(at, rows):
        out[at, :] = rows.astype(out.dtype)

    cut_rows(start[0], ptdf, dual, slab, sems, put)


def add_kernel(spare, keep, got, out):
    at = pl.ds(pl.multiple_of(spare[0], 16), out.shape[0])
    out[...] = (keep[at, :] + got[at, :].astype(F32)).astype(BF16)


def pick_kernel(plan, parts, out):
    total = jnp.sum(parts[...].astype(F32), 0)
    at = lax.broadcasted_iota(jnp.int32, (out.shape[0], plan.shape[1]), 0)
    pick = (at == plan[0:1, :]).astype(BF16)
    mark = (at == plan[1:2, :]).astype(BF16)
    slot = lax.broadcasted_iota(jnp.int32, (out.shape[1], plan.shape[1]), 0)
    names = jnp.where(slot == plan[2:3, :], plan[3:4, :], 0).astype(F32).astype(BF16)
    dot = lambda x: jnp.dot(pick, x, preferred_element_type=F32)
    a, b, c = split3(total)
    ids = lax.dot_general(mark, names, NT, preferred_element_type=F32)
    out[...] = dot(a) + dot(b) + dot(c) + ids


def merge_kernel(terms, out):
    rows, scen = out.shape
    count = terms.shape[0] * SLOTS
    dot = lambda x, y: jnp.dot(x, y, preferred_element_type=F32)
    iota = lambda shape, axis: lax.broadcasted_iota(jnp.int32, shape, axis)
    names = terms[:, SLOTS - 1, :TILE].astype(BF16)
    spread = (iota((count // SLOTS, count), 0) == iota((count // SLOTS, count), 1) // SLOTS).astype(
        BF16
    )
    names = lax.dot_general(names, spread, (((0,), (0,)), ((), ())), preferred_element_type=F32)
    names = jnp.where(iota((SLOTS, count), 0) == iota((SLOTS, count), 1) % SLOTS, names[:SLOTS], 0.0)
    names = jnp.sum(names, 0, keepdims=True)
    merge = (iota((rows, count), 0).astype(F32) + 1 == names).astype(BF16)
    a, b, c = split3(terms[...].reshape(count, scen))
    out[...] = dot(merge, a) + dot(merge, b) + dot(merge, c)


def local(ptdf, injections, viol_mask, viol_sign, limit, price, owner):
    line, bus = lax.axis_index("line"), lax.axis_index("bus")
    core = line % 2
    lines, buses = ptdf.shape
    rows = lines // BUSES_AT
    block = buses // LINES_AT
    half = buses // 2
    first = half // TILE * TILE
    window = buses - first
    scen = viol_mask.shape[1]
    width = scen // LINES_AT
    shape = jax.ShapeDtypeStruct
    owners = lax.dynamic_slice_in_dim(owner, (core * HALF + line // 2) * block, block, 0)
    groups, within = owners // HELD, owners % HELD
    place = ranks(groups)
    plan = jnp.stack([groups * SLOTS + place, groups * SLOTS + SLOTS - 1, place, within + 1])
    cut = lambda x: lax.dynamic_slice_in_dim(x, bus * rows, rows, 0)
    mask = cut(viol_mask).T
    sign, limit, price = (cut(x)[None, :] for x in (viol_sign, limit, price))
    goes = gathered(line, width).astype(jnp.int32)[None, :]

    pieces, (plan, mask, sign, limit, price, goes) = gather(
        injections.T, (plan, mask, sign, limit, price, goes)
    )
    work = 2 * lines * buses * scen
    step = lines // 2
    partial_flows = pl.pallas_call(
        flows_kernel,
        out_shape=shape((lines, scen), F32),
        grid=(lines // step,),
        in_specs=[pl.BlockSpec((step, buses), lambda i: (i, 0))]
        + [pl.BlockSpec(memory_space=pltpu.VMEM)] * len(pieces),
        out_specs=pl.BlockSpec((step, scen), lambda i: (i, 0)),
        compiler_params=pltpu.CompilerParams(vmem_limit_bytes=32 << 20),
        cost_estimate=pl.CostEstimate(
            flops=work, bytes_accessed=2 * lines * buses, transcendentals=0
        ),
    )(ptdf, *pieces)
    parts = lax.all_to_all(partial_flows.reshape(BUSES_AT, rows, scen), "bus", 0, 0, tiled=True)
    dual = call(
        dual_kernel,
        shape((BUSES_AT, scen, rows), BF16),
        (10 * rows * scen, 8 * lines * scen),
        (goes, parts, mask, sign, limit, price),
    )
    dual = lax.all_to_all(dual, "bus", 0, 0, tiled=True)

    def cuts(start, dtype):
        return call(
            cuts_kernel,
            shape((window, scen), dtype),
            (work // 2, lines * buses),
            (pltpu.with_memory_space_constraint(ptdf, pltpu.HBM), dual),
            (start[None],),
            slab=((lines, window), 5),
        )

    core = core.astype(jnp.int32)
    got = lax.ppermute(cuts((1 - core) * first, BF16), "line", PAIRS)
    chip = call(
        add_kernel,
        shape((half, scen), BF16),
        (window * scen, 8 * window * scen),
        (cuts(core * first, F32), got),
        ((core * (window - half))[None],),
    )
    parts = lax.all_to_all(
        chip.reshape(HALF, block, scen), "line", 0, 0, tiled=True, axis_index_groups=SAME_CORE
    )
    send = call(
        pick_kernel,
        shape((DEVICES * SLOTS, scen), F32),
        (6 * DEVICES * SLOTS * block * scen, 2 * half * scen),
        (plan, parts),
    )
    terms = lax.all_to_all(
        send.reshape(DEVICES, SLOTS, scen), ("line", "bus"), 0, 0, tiled=True
    )
    return call(
        merge_kernel,
        shape((HELD, scen), F32),
        (6 * DEVICES * SLOTS * HELD * scen, 4 * DEVICES * SLOTS * scen),
        (terms,),
    )


def solution(mesh):
    placed = (
        P("line", "bus"),
        P("bus", "line"),
        P("line", None),
        P("line"),
        P("line"),
        P("line"),
        P("bus"),
    )
    return jax.shard_map(
        local, mesh=mesh, in_specs=placed, out_specs=P(("line", "bus"), None), check_vma=False
    )
```

time: 171 us -> 158 us (0.924)
  waiting for transfers between devices: 58.2 us -> 23 us
  blocking collectives: 56.3 us -> 74.5 us
  starting transfers between devices: 14.1 us -> 25.1 us
  local copies, waits for them, and re-layouts: 7.65 us -> 2.94 us
  Pallas kernels: 31.5 us -> 27.9 us
    all_to_all x2 -> x1, waiting for transfers between devices: 50.1 us -> 9.48 us  [local(): dual = lax.all_to_all(dual, 'bus', 0, 0, tiled=True)]
    ppermute x2 -> x14, starting transfers between devices: 3.48 us -> 21.6 us  [the longest x13 18.3 us: gather(): move = lambda x, *to: lax.ppermute(x, 'line', along(*to))]
    all_to_all x1, blocking collectives: 13.1 us -> 30.3 us  [local(): lax.all_to_all(chip.reshape(HALF, block, scen), 'line', 0, 0, tiled=True,...]
    pallas_call x6, Pallas kernels: 31.5 us -> 19.2 us  [call(): pl.pallas_call(kernel, out_shape=out, in_specs=[pl.BlockSpec(memory_space...]
    pallas_call x0 -> x1, Pallas kernels: none -> 8.72 us  [local(): pl.pallas_call(flows_kernel, out_shape=shape((lines, scen), F32), grid=(l...]
    all_to_all x2 -> x1, starting transfers between devices: 10.6 us -> 3.49 us  [local(): dual = lax.all_to_all(dual, 'bus', 0, 0, tiled=True)]
    ppermute x2 -> x14, waiting for transfers between devices: 8.09 us -> 13.5 us  [the longest x13 13.5 us: gather(): move = lambda x, *to: lax.ppermute(x, 'line', along(*to))]
    broadcast_in_dim x1 -> x0, local copies, waits for them, and re-layouts: 2.58 us -> none  [share(): spread = jnp.broadcast_to(x[None], (ways,) + x.shape)]
  transfers between devices with their start and end apart: 4 -> 15, of which waited for: 4 -> 6; matrix products, arithmetic and copies ran while one was open for 3% -> 2% of each run, Pallas kernels for 0% -> 4%
where the time goes in v3:
time: 158 us; the launch traced here: 156 us
  blocking collectives  74.5 us (47%)
  Pallas kernels  27.9 us (18%)
  starting transfers between devices  25.1 us (16%)
  waiting for transfers between devices  23 us (15%)
  local copies, waits for them, and re-layouts  2.94 us (2%)
  other arithmetic  1.94 us (1%)
    all_to_all x1, blocking collectives, local(): lax.all_to_all(chip.reshape(HALF, block, scen), 'line', 0, 0, tiled=True,...  30.3 us
    all_to_all x1, blocking collectives, local(): lax.all_to_all(send.reshape(DEVICES, SLOTS, scen), ('line', 'bus'), 0, 0,...  22.3 us
    all_to_all x1, blocking collectives, local(): lax.all_to_all(partial_flows.reshape(BUSES_AT, rows, scen), 'bus', 0, 0,...  21.9 us
    pallas_call x6, Pallas kernels, call(): pl.pallas_call(kernel, out_shape=out, in_specs=[pl.BlockSpec(memory_space...  19.2 us
    ppermute x13, starting transfers between devices, gather(): move = lambda x, *to: lax.ppermute(x, 'line', along(*to))  18.3 us
    ppermute x13, waiting for transfers between devices, gather(): move = lambda x, *to: lax.ppermute(x, 'line', along(*to))  13.5 us
    all_to_all x1, waiting for transfers between devices, local(): dual = lax.all_to_all(dual, 'bus', 0, 0, tiled=True)  9.48 us
    pallas_call x1, Pallas kernels, local(): pl.pallas_call(flows_kernel, out_shape=shape((lines, scen), F32), grid=(l...  8.72 us
  transfers between devices with their start and end apart: 15, of which 6 were waited for; matrix products, arithmetic and copies ran while one was open for 2% of the time, Pallas kernels for 4%

profile of v3, /device:TPU:3, one launch (start us, length us, event | category | flops | bytes accessed | tf_op | source)
XLA Modules:
  0.0 155.6 jit_solution(4091733179185047805)
XLA Ops:
  0.0 1.1 fusion.12
  1.1 3.8 %collective-permute-start.4 = (bf16[8,8832]{1,0:T(8,128)(2,1)S(1)}, bf16[8,8832]{1,0:T(8,128)(2,1)S(1)}, u32[]{:S(2)}, u32[]{:S(2)}) collective-permute-start(bf16[8,8832]{1,0:T(8,128)(2,1)S(1)} %get-tuple-element.23), channel_id=1, source_target_pairs={{0,48},{8,56},{16,0},{24,8},{32,16},{40,24},{48,32},{56,40},{64,11... | collective-permute-start | bytes 423944 | tf_op jit(solution)/shard_map/ppermute | solution.py:41
  4.9 0.0 collective-permute-start.3
  4.9 0.3 collective-permute-start
  5.2 0.8 multiply_add_fusion
  6.0 0.3 convert_reduce_fusion
  6.3 0.8 dynamic-slice_bitcast_fusion
  7.1 0.7 fusion.10
  7.8 0.8 dynamic-slice_bitcast_fusion.2.sign
  8.6 0.1 copy.14
  8.8 0.0 collective-permute-done.4
  8.8 1.7 %collective-permute-done.3 = bf16[8,8832]{1,0:T(8,128)(2,1)S(1)} collective-permute-done((bf16[8,8832]{1,0:T(8,128)(2,1)S(1)}, bf16[8,8832]{1,0:T(8,128)(2,1)S(1)}, u32[]{:S(2)}, u32[]{:S(2)}) %collective-permute-start.3) | collective-permute-done | bytes 141344 | tf_op jit(solution)/shard_map/ppermute | solution.py:41
  10.4 0.3 collective-permute-start.5
  10.8 0.0 collective-permute-start.6
  10.8 1.7 %collective-permute-done = bf16[16,8832]{1,0:T(8,128)(2,1)S(1)} collective-permute-done((bf16[16,8832]{1,0:T(8,128)(2,1)}, bf16[16,8832]{1,0:T(8,128)(2,1)S(1)}, u32[]{:S(2)}, u32[]{:S(2)}) %collective-permute-start) | collective-permute-done | bytes 282656 | tf_op jit(solution)/shard_map/ppermute | solution.py:41
  12.5 2.4 %collective-permute-start.2 = (bf16[16,8832]{1,0:T(8,128)(2,1)S(1)}, bf16[16,8832]{1,0:T(8,128)(2,1)S(1)}, u32[]{:S(2)}, u32[]{:S(2)}) collective-permute-start(bf16[16,8832]{1,0:T(8,128)(2,1)S(1)} %pad_maximum_fusion.1), channel_id=1, source_target_pairs={{0,48},{8,56},{16,0},{24,8},{32,16},{40,24},{48,32},{56,40},{64,11... | collective-permute-start | bytes 847880 | tf_op jit(solution)/shard_map/ppermute | solution.py:41
  14.9 0.0 collective-permute-start.1
  14.9 0.1 pad_maximum_fusion.refs_0_
  15.0 4.3 %collective-permute-start.10 = (bf16[48,8832]{1,0:T(8,128)(2,1)S(1)}, bf16[48,8832]{1,0:T(8,128)(2,1)S(1)}, u32[]{:S(2)}, u32[]{:S(2)}) collective-permute-start(bf16[48,8832]{1,0:T(8,128)(2,1)S(1)} %pad_maximum_fusion.refs_0_), channel_id=1, source_target_pairs={{0,8},{8,0},{16,24},{24,16},{32,40},{40,32},{48,56},{56,48},{64,72... | collective-permute-start | bytes 2543624 | tf_op jit(solution)/shard_map/ppermute | solution.py:41
  19.3 0.0 collective-permute-done.6
  19.3 0.0 collective-permute-start.7
  19.3 5.0 %collective-permute-done.7 = bf16[8,8832]{1,0:T(8,128)(2,1)S(1)} collective-permute-done((bf16[8,8832]{1,0:T(8,128)(2,1)S(1)}, bf16[8,8832]{1,0:T(8,128)(2,1)S(1)}, u32[]{:S(2)}, u32[]{:S(2)}) %collective-permute-start.7) | collective-permute-done | bytes 141344 | tf_op jit(solution)/shard_map/ppermute | solution.py:41
  24.3 0.0 collective-permute-done.2
  24.3 0.0 collective-permute-done.1
  24.4 3.3 %collective-permute-start.9 = (bf16[8,8832]{1,0:T(8,128)(2,1)S(1)}, bf16[8,8832]{1,0:T(8,128)(2,1)S(1)}, u32[]{:S(2)}, u32[]{:S(2)}) collective-permute-start(bf16[8,8832]{1,0:T(8,128)(2,1)S(1)} %slice.19), channel_id=1, source_target_pairs={{0,48},{8,56},{16,0},{24,8},{32,16},{40,24},{48,32},{56,40},{64,11... | collective-permute-start | bytes 423944 | tf_op jit(solution)/shard_map/ppermute | solution.py:41
  27.7 0.0 collective-permute-start.8
  27.7 0.0 collective-permute-done.5
  27.8 1.5 collective-permute-start.11
  29.2 3.6 %collective-permute-done.8 = bf16[8,8832]{1,0:T(8,128)(2,1)S(1)} collective-permute-done((bf16[8,8832]{1,0:T(8,128)(2,1)S(1)}, bf16[8,8832]{1,0:T(8,128)(2,1)S(1)}, u32[]{:S(2)}, u32[]{:S(2)}) %collective-permute-start.8) | collective-permute-done | bytes 141344 | tf_op jit(solution)/shard_map/ppermute | solution.py:41
  32.9 0.0 collective-permute-done.9
  32.9 2.4 %collective-permute-start.12 = (bf16[32,8832]{1,0:T(8,128)(2,1)S(1)}, bf16[32,8832]{1,0:T(8,128)(2,1)S(1)}, u32[]{:S(2)}, u32[]{:S(2)}) collective-permute-start(bf16[32,8832]{1,0:T(8,128)(2,1)S(1)} %constant_dynamic-update-slice_fusion.3.refs_2_), channel_id=1, source_target_pairs={{0,8},{8,0},{16,24},{24,16},{32,40},{40,32},{48,56},{56,48},{64,72... | collective-permute-start | bytes 1695752 | tf_op jit(solution)/shard_map/ppermute | solution.py:41
  35.3 0.0 collective-permute-done.10.refs_3_
  35.3 1.6 %collective-permute-done.12.refs_5_ = bf16[32,8832]{1,0:T(8,128)(2,1)S(1)} collective-permute-done((bf16[32,8832]{1,0:T(8,128)(2,1)S(1)}, bf16[32,8832]{1,0:T(8,128)(2,1)S(1)}, u32[]{:S(2)}, u32[]{:S(2)}) %collective-permute-start.12) | collective-permute-done | bytes 565280 | tf_op jit(solution)/shard_map/ppermute | solution.py:41
  36.9 0.0 collective-permute-done.11.refs_4_
  36.9 8.7 %shard_map.109 = f32[1024,256]{1,0:T(8,128)S(1)} custom-call(bf16[1024,8832]{1,0:T(8,128)(2,1)} %ptdf.5, bf16[48,8832]{1,0:T(8,128)(2,1)S(1)} %pad_maximum_fusion.refs_0_, bf16[48,8832]{1,0:T(8,128)(2,1)S(1)} %constant_dynamic-update-slice_fusion.refs_1_, bf16[32,8832]{1,0:T(8,128)(2,1)S(1)} %constant_dynamic-update-slice_fusion.3.refs_2_, ...), custom_call_target="tpu_custom_call" | custom-call | flops 4630511616 | bytes 18087936 | tf_op jit(solution)/shard_map/pallas_call | solution.py:224
  45.6 21.9 %all_to_all.20.parts = f32[8,128,256]{2,1,0:T(8,128)S(1)} all-to-all(f32[8,128,256]{2,1,0:T(8,128)S(1)} %bitcast.16), channel_id=1, replica_groups=mesh['line'=16,'bus'=8] {'bus'}, dimensions={0} | all-to-all | bytes 2097152 | tf_op jit(solution)/shard_map/all_to_all | solution.py:236
  67.5 1.1 shard_map.110
  68.6 3.5 %all-to-all-start.1 = ((bf16[8,256,128]{2,1,0:T(8,128)(2,1)}), bf16[8,256,128]{2,1,0:T(8,128)(2,1)S(1)}, u32[]{:S(2)}, u32[]{:S(2)}) async-start(bf16[8,256,128]{2,1,0:T(8,128)(2,1)} %shard_map.110), calls=%async_computation.1 | async-start | bytes 1048576 | tf_op jit(solution)/shard_map/all_to_all | solution.py:243
  72.1 9.5 %all-to-all-done.1.dual = bf16[8,256,128]{2,1,0:T(8,128)(2,1)S(1)} async-done(((bf16[8,256,128]{2,1,0:T(8,128)(2,1)}), bf16[8,256,128]{2,1,0:T(8,128)(2,1)S(1)}, u32[]{:S(2)}, u32[]{:S(2)}) %all-to-all-start.1) | async-done | bytes 524320 | tf_op jit(solution)/shard_map/all_to_all | solution.py:243
  81.6 7.0 %shard_map.112 = bf16[4480,256]{1,0:T(8,128)(2,1)} custom-call(s32[1]{0:T(128)} %bitcast.9.start, bf16[1024,8832]{1,0:T(8,128)(2,1)} %ptdf.5, bf16[8,256,128]{2,1,0:T(8,128)(2,1)S(1)} %all-to-all-done.1.dual), custom_call_target="tpu_custom_call" | custom-call | flops 2315255808 | bytes 9043968 | tf_op jit(solution)/shard_map/pallas_call | solution.py:95
  88.6 3.3 %collective-permute-start.13 = (bf16[4480,256]{1,0:T(8,128)(2,1)}, bf16[4480,256]{1,0:T(8,128)(2,1)}, u32[]{:S(2)}, u32[]{:S(2)}) collective-permute-start(bf16[4480,256]{1,0:T(8,128)(2,1)} %shard_map.112), channel_id=1, source_target_pairs={{0,8},{8,0},{16,24},{24,16},{32,40},{40,32},{48,56},{56,48},{64,72... | collective-permute-start | bytes 6881288 | tf_op jit(solution)/shard_map/ppermute | solution.py:256
  91.9 5.7 %shard_map.111.keep = f32[4480,256]{1,0:T(8,128)S(1)} custom-call(s32[1]{0:T(128)} %bitcast.7.start, bf16[1024,8832]{1,0:T(8,128)(2,1)} %ptdf.5, bf16[8,256,128]{2,1,0:T(8,128)(2,1)S(1)} %all-to-all-done.1.dual), custom_call_target="tpu_custom_call" | custom-call | flops 2315255808 | bytes 9043968 | tf_op jit(solution)/shard_map/pallas_call | solution.py:95
  97.6 0.0 collective-permute-done.13.got
  97.6 2.1 %shard_map.113 = bf16[4416,256]{1,0:T(8,128)(2,1)S(1)} custom-call(s32[1]{0:T(128)} %bitcast.6.spare, f32[4480,256]{1,0:T(8,128)S(1)} %shard_map.111.keep, bf16[4480,256]{1,0:T(8,128)(2,1)} %collective-permute-done.13.got), custom_call_target="tpu_custom_call" | custom-call | flops 1146880 | bytes 9175040 | tf_op jit(solution)/shard_map/pallas_call | solution.py:95
  99.7 30.3 %all_to_all.21.parts = bf16[8,552,256]{2,1,0:T(8,128)(2,1)S(1)} all-to-all(bf16[8,552,256]{2,1,0:T(8,128)(2,1)S(1)} %bitcast.15), channel_id=1, replica_groups={{0,16,32,48,64,80,96,112},{8,24,40,56,72,88,104,120},{1,17,33,49,65,81,..., dimensions={0} | all-to-all | bytes 4521984 | tf_op jit(solution)/shard_map/all_to_all | solution.py:264
  130.0 2.0 %shard_map.114 = f32[1024,256]{1,0:T(8,128)S(1)} custom-call(s32[4,552]{1,0:T(4,128)S(1)} %pad_add_fusion.plan, bf16[8,552,256]{2,1,0:T(8,128)(2,1)S(1)} %all_to_all.21.parts), custom_call_target="tpu_custom_call" | custom-call | flops 868220928 | bytes 2260992 | tf_op jit(solution)/shard_map/pallas_call | solution.py:95
  132.0 22.3 %all_to_all.22.terms = f32[128,8,256]{2,1,0:T(8,128)S(1)} all-to-all(f32[128,8,256]{2,1,0:T(8,128)S(1)} %bitcast.17), channel_id=1, replica_groups=mesh['line'=16,'bus'=8] {'line','bus'}, dimensions={0} | all-to-all | bytes 2097152 | tf_op jit(solution)/shard_map/all_to_all | solution.py:273
  154.3 1.3 shard_map.115
  (23 shorter events, 0.3 us)
Async XLA Ops:
  0.0 6.3 %copy-start = (s32[1024,256]{1,0:T(8,128)S(1)}, s32[1024,256]{1,0:T(8,128)}, u32[]{:S(2)}) copy-start(s32[1024,256]{1,0:T(8,128)} %param.13) | copy-start | bytes 3145732
  0.0 14.9 %copy-start.1 = (bf16[8832,16]{0,1:T(8,128)(2,1)S(1)}, bf16[8832,16]{0,1:T(8,128)(2,1)}, u32[]{:S(2)}) copy-start(bf16[8832,16]{0,1:T(8,128)(2,1)} %param.12) | copy-start | bytes 847876
  1.1 7.6 %collective-permute-start.4 = (bf16[8,8832]{1,0:T(8,128)(2,1)S(1)}, bf16[8,8832]{1,0:T(8,128)(2,1)S(1)}, u32[]{:S(2)}, u32[]{:S(2)}) collective-permute-start(bf16[8,8832]{1,0:T(8,128)(2,1)S(1)} %get-tuple-element.23), channel_id=1, source_target_pairs={{0,48},{8,56},{16,0},{24,8},{32,16},{40,24},{48,32},{56,40},{64,11... | collective-permute-start | bytes 423944 | tf_op jit(solution)/shard_map/ppermute | solution.py:41
  4.9 5.5 %collective-permute-start.3 = (bf16[8,8832]{1,0:T(8,128)(2,1)S(1)}, bf16[8,8832]{1,0:T(8,128)(2,1)S(1)}, u32[]{:S(2)}, u32[]{:S(2)}) collective-permute-start(bf16[8,8832]{1,0:T(8,128)(2,1)S(1)} %get-tuple-element.23), channel_id=1, source_target_pairs={{0,16},{8,24},{16,32},{24,40},{32,48},{40,56},{48,0},{56,8},{64,80... | collective-permute-start | bytes 423944 | tf_op jit(solution)/shard_map/ppermute | solution.py:41
  4.9 7.5 %collective-permute-start = (bf16[16,8832]{1,0:T(8,128)(2,1)}, bf16[16,8832]{1,0:T(8,128)(2,1)S(1)}, u32[]{:S(2)}, u32[]{:S(2)}) collective-permute-start(bf16[16,8832]{1,0:T(8,128)(2,1)} %bitcast.21), channel_id=1, source_target_pairs={{0,64},{8,72},{16,80},{24,88},{32,96},{40,104},{48,112},{56,120},{... | collective-permute-start | bytes 847880 | tf_op jit(solution)/shard_map/ppermute | solution.py:41
  10.4 17.3 %collective-permute-start.5 = (bf16[16,8832]{1,0:T(8,128)(2,1)S(1)}, bf16[16,8832]{1,0:T(8,128)(2,1)S(1)}, u32[]{:S(2)}, u32[]{:S(2)}) collective-permute-start(bf16[16,8832]{1,0:T(8,128)(2,1)S(1)} %pad_maximum_fusion.2), channel_id=1, source_target_pairs={{0,64},{8,72},{16,80},{24,88},{32,96},{40,104},{48,112},{56,120},{... | collective-permute-start | bytes 847880 | tf_op jit(solution)/shard_map/ppermute | solution.py:41
  10.8 8.5 %collective-permute-start.6 = (bf16[8,8832]{1,0:T(8,128)(2,1)S(1)}, bf16[8,8832]{1,0:T(8,128)(2,1)S(1)}, u32[]{:S(2)}, u32[]{:S(2)}) collective-permute-start(bf16[8,8832]{1,0:T(8,128)(2,1)S(1)} %collective-permute-done.3), channel_id=1, source_target_pairs={{0,16},{8,24},{16,32},{24,40},{32,48},{40,56},{48,0},{56,8},{64,80... | collective-permute-start | bytes 423944 | tf_op jit(solution)/shard_map/ppermute | solution.py:41
  12.5 11.8 %collective-permute-start.2 = (bf16[16,8832]{1,0:T(8,128)(2,1)S(1)}, bf16[16,8832]{1,0:T(8,128)(2,1)S(1)}, u32[]{:S(2)}, u32[]{:S(2)}) collective-permute-start(bf16[16,8832]{1,0:T(8,128)(2,1)S(1)} %pad_maximum_fusion.1), channel_id=1, source_target_pairs={{0,48},{8,56},{16,0},{24,8},{32,16},{40,24},{48,32},{56,40},{64,11... | collective-permute-start | bytes 847880 | tf_op jit(solution)/shard_map/ppermute | solution.py:41
  14.9 9.4 %collective-permute-start.1 = (bf16[16,8832]{1,0:T(8,128)(2,1)S(1)}, bf16[16,8832]{1,0:T(8,128)(2,1)S(1)}, u32[]{:S(2)}, u32[]{:S(2)}) collective-permute-start(bf16[16,8832]{1,0:T(8,128)(2,1)S(1)} %pad_maximum_fusion.1), channel_id=1, source_target_pairs={{0,16},{8,24},{16,32},{24,40},{32,48},{40,56},{48,0},{56,8},{64,80... | collective-permute-start | bytes 847880 | tf_op jit(solution)/shard_map/ppermute | solution.py:41
  15.0 20.3 %collective-permute-start.10 = (bf16[48,8832]{1,0:T(8,128)(2,1)S(1)}, bf16[48,8832]{1,0:T(8,128)(2,1)S(1)}, u32[]{:S(2)}, u32[]{:S(2)}) collective-permute-start(bf16[48,8832]{1,0:T(8,128)(2,1)S(1)} %pad_maximum_fusion.refs_0_), channel_id=1, source_target_pairs={{0,8},{8,0},{16,24},{24,16},{32,40},{40,32},{48,56},{56,48},{64,72... | collective-permute-start | bytes 2543624 | tf_op jit(solution)/shard_map/ppermute | solution.py:41
  19.3 5.0 %collective-permute-start.7 = (bf16[8,8832]{1,0:T(8,128)(2,1)S(1)}, bf16[8,8832]{1,0:T(8,128)(2,1)S(1)}, u32[]{:S(2)}, u32[]{:S(2)}) collective-permute-start(bf16[8,8832]{1,0:T(8,128)(2,1)S(1)} %collective-permute-done.6), channel_id=1, source_target_pairs={{0,64},{8,72},{16,80},{24,88},{32,96},{40,104},{48,112},{56,120},{... | collective-permute-start | bytes 423944 | tf_op jit(solution)/shard_map/ppermute | solution.py:41
  24.4 8.5 %collective-permute-start.9 = (bf16[8,8832]{1,0:T(8,128)(2,1)S(1)}, bf16[8,8832]{1,0:T(8,128)(2,1)S(1)}, u32[]{:S(2)}, u32[]{:S(2)}) collective-permute-start(bf16[8,8832]{1,0:T(8,128)(2,1)S(1)} %slice.19), channel_id=1, source_target_pairs={{0,48},{8,56},{16,0},{24,8},{32,16},{40,24},{48,32},{56,40},{64,11... | collective-permute-start | bytes 423944 | tf_op jit(solution)/shard_map/ppermute | solution.py:41
  27.7 5.1 %collective-permute-start.8 = (bf16[8,8832]{1,0:T(8,128)(2,1)S(1)}, bf16[8,8832]{1,0:T(8,128)(2,1)S(1)}, u32[]{:S(2)}, u32[]{:S(2)}) collective-permute-start(bf16[8,8832]{1,0:T(8,128)(2,1)S(1)} %slice.18), channel_id=1, source_target_pairs={{0,16},{8,24},{16,32},{24,40},{32,48},{40,56},{48,0},{56,8},{64,80... | collective-permute-start | bytes 423944 | tf_op jit(solution)/shard_map/ppermute | solution.py:41
  27.8 9.1 %collective-permute-start.11 = (bf16[48,8832]{1,0:T(8,128)(2,1)S(1)}, bf16[48,8832]{1,0:T(8,128)(2,1)S(1)}, u32[]{:S(2)}, u32[]{:S(2)}) collective-permute-start(bf16[48,8832]{1,0:T(8,128)(2,1)S(1)} %constant_dynamic-update-slice_fusion.refs_1_), channel_id=1, source_target_pairs={{0,8},{8,0},{16,24},{24,16},{32,40},{40,32},{48,56},{56,48},{64,72... | collective-permute-start | bytes 2543624 | tf_op jit(solution)/shard_map/ppermute | solution.py:41
  32.9 4.0 %collective-permute-start.12 = (bf16[32,8832]{1,0:T(8,128)(2,1)S(1)}, bf16[32,8832]{1,0:T(8,128)(2,1)S(1)}, u32[]{:S(2)}, u32[]{:S(2)}) collective-permute-start(bf16[32,8832]{1,0:T(8,128)(2,1)S(1)} %constant_dynamic-update-slice_fusion.3.refs_2_), channel_id=1, source_target_pairs={{0,8},{8,0},{16,24},{24,16},{32,40},{40,32},{48,56},{56,48},{64,72... | collective-permute-start | bytes 1695752 | tf_op jit(solution)/shard_map/ppermute | solution.py:41
  68.6 13.0 %all-to-all-start.1 = ((bf16[8,256,128]{2,1,0:T(8,128)(2,1)}), bf16[8,256,128]{2,1,0:T(8,128)(2,1)S(1)}, u32[]{:S(2)}, u32[]{:S(2)}) async-start(bf16[8,256,128]{2,1,0:T(8,128)(2,1)} %shard_map.110), calls=%async_computation.1 | async-start | bytes 1048576 | tf_op jit(solution)/shard_map/all_to_all | solution.py:243
  88.6 9.0 %collective-permute-start.13 = (bf16[4480,256]{1,0:T(8,128)(2,1)}, bf16[4480,256]{1,0:T(8,128)(2,1)}, u32[]{:S(2)}, u32[]{:S(2)}) collective-permute-start(bf16[4480,256]{1,0:T(8,128)(2,1)} %shard_map.112), channel_id=1, source_target_pairs={{0,8},{8,0},{16,24},{24,16},{32,40},{40,32},{48,56},{56,48},{64,72... | collective-permute-start | bytes 6881288 | tf_op jit(solution)/shard_map/ppermute | solution.py:256

commit v4 on v3

--- a/solution.py
+++ b/solution.py
@@ -14,7 +14,6 @@
 SLOTS = 8
 TILE = 128
 PAIRS = [(i, i ^ 1) for i in range(LINES_AT)]
-SAME_CORE = [[a + c for a in range(0, LINES_AT, 2)] for c in (0, 1)]
 HALF = LINES_AT // 2
 BF16, F32 = jnp.bfloat16, jnp.float32
 NT = (((1,), (1,)), ((), ()))
@@ -85,9 +84,9 @@
     return a, b, (rest - b.astype(F32)).astype(BF16)
 
 
-def call(kernel, out, cost, operands, scalars=(), slab=None, limit=24):
+def call(kernel, out, cost, operands, scalars=(), slab=None, limit=24, scratch=()):
     whole = pl.BlockSpec(memory_space=pltpu.VMEM)
-    specs, scratch = [whole] * len(operands), []
+    specs = [whole] * len(operands)
     if slab:
         specs[0] = pl.BlockSpec(memory_space=pl.ANY)
         shape, parts = slab
@@ -96,7 +95,7 @@
         kernel,
         out_shape=out,
         in_specs=[pl.BlockSpec(memory_space=pltpu.SMEM)] * len(scalars) + specs,
-        out_specs=whole,
+        out_specs=jax.tree.map(lambda x: whole, out),
         scratch_shapes=scratch,
         compiler_params=pltpu.CompilerParams(vmem_limit_bytes=limit << 20),
         cost_estimate=pl.CostEstimate(flops=cost[0], bytes_accessed=cost[1], transcendentals=0),
@@ -160,13 +159,39 @@
     cut_rows(start[0], ptdf, dual, slab, sems, put)
 
 
-def add_kernel(spare, keep, got, out):
-    at = pl.ds(pl.multiple_of(spare[0], 16), out.shape[0])
-    out[...] = (keep[at, :] + got[at, :].astype(F32)).astype(BF16)
-
-
-def pick_kernel(plan, parts, out):
-    total = jnp.sum(parts[...].astype(F32), 0)
+def chip_kernel(at, keep, got, to_x, to_1, to_2, to_3, stay_low, stay_high, total):
+    total[...] = keep[...] + got[...].astype(F32)
+    spare, x, z = at[0], at[1], at[2]
+    size, half = to_x.shape[1], to_x.shape[2]
+
+    def block(dx, dz, high):
+        chip = jax.lax.rem(x + dx, 2) * 4 + jax.lax.rem(z + dz, 4)
+        rows = pl.ds(pl.multiple_of(spare + chip * size, 8), size)
+        return total[rows, half:] if high else total[rows, :half]
+
+    for dz in range(4):
+        to_x[dz] = block(1, dz, True).astype(BF16)
+        stay_high[dz] = block(0, dz, True)
+    for dx in range(2):
+        stay_low[dx] = block(dx, 0, False)
+        for dz, out in ((1, to_1), (2, to_2), (3, to_3)):
+            out[dx] = block(dx, dz, False).astype(BF16)
+
+
+def high_kernel(stay, got, to_1, to_2, to_3, mine):
+    for dz, out in enumerate((mine, to_1, to_2, to_3)):
+        out[...] = (stay[dz] + got[dz].astype(F32)).astype(out.dtype)
+
+
+def low_kernel(stay, got_1, got_2, got_3, to_x, mine):
+    for dx, out in enumerate((mine, to_x)):
+        more = got_1[dx].astype(F32) + got_2[dx].astype(F32) + got_3[dx].astype(F32)
+        out[...] = (stay[dx] + more).astype(out.dtype)
+
+
+def pick_kernel(plan, low, got_low, high, got_1, got_2, got_3, out):
+    high = high[...] + (got_1[...].astype(F32) + got_2[...].astype(F32) + got_3[...].astype(F32))
+    total = jnp.concatenate([low[...] + got_low[...].astype(F32), high], 1)
     at = lax.broadcasted_iota(jnp.int32, (out.shape[0], plan.shape[1]), 0)
     pick = (at == plan[0:1, :]).astype(BF16)
     mark = (at == plan[1:2, :]).astype(BF16)
@@ -254,21 +279,34 @@
 
     core = core.astype(jnp.int32)
     got = lax.ppermute(cuts((1 - core) * first, BF16), "line", PAIRS)
-    chip = call(
-        add_kernel,
-        shape((half, scen), BF16),
+    keep = cuts(core * first, F32)
+    x, z = line // 8, line // 2 % 4
+    at = jnp.stack([core * (window - half), x, z]).astype(jnp.int32)
+    side = scen // 2
+    pile = lambda n, dtype: shape((n, block, side), dtype)
+    one = lambda dtype: shape((block, side), dtype)
+    small = (block * scen, 8 * block * scen)
+    to_x, *to_z, stay_low, stay_high = call(
+        chip_kernel,
+        (pile(4, BF16), *[pile(2, BF16)] * 3, pile(2, F32), pile(4, F32)),
         (window * scen, 8 * window * scen),
-        (cuts(core * first, F32), got),
-        ((core * (window - half))[None],),
-    )
-    parts = lax.all_to_all(
-        chip.reshape(HALF, block, scen), "line", 0, 0, tiled=True, axis_index_groups=SAME_CORE
-    )
+        (keep, got),
+        (at,),
+        scratch=[pltpu.VMEM((window, scen), F32)],
+    )
+    go_x = lambda x: lax.ppermute(x, "line", along(1, 0, 0))
+    go_z = lambda xs: [lax.ppermute(x, "line", along(0, i + 1, 0)) for i, x in enumerate(xs)]
+    got_x, got_z = go_x(to_x), go_z(to_z)
+    *to_z, high = call(
+        high_kernel, (*[one(BF16)] * 3, one(F32)), small, (stay_high, got_x)
+    )
+    to_x, low = call(low_kernel, (one(BF16), one(F32)), small, (stay_low, *got_z))
+    parts = low, go_x(to_x), high, *go_z(to_z)
     send = call(
         pick_kernel,
         shape((DEVICES * SLOTS, scen), F32),
         (6 * DEVICES * SLOTS * block * scen, 2 * half * scen),
-        (plan, parts),
+        (plan, *parts),
     )
     terms = lax.all_to_all(
         send.reshape(DEVICES, SLOTS, scen), ("line", "bus"), 0, 0, tiled=True

time: 158 us -> 156 us (0.987)
  blocking collectives: 74.5 us -> 45.6 us
  waiting for transfers between devices: 23 us -> 41.4 us
  starting transfers between devices: 25.1 us -> 33.3 us
    all_to_all x1 -> x0, blocking collectives: 30.3 us -> none  [local(): lax.all_to_all(chip.reshape(HALF, block, scen), 'line', 0, 0, tiled=True,...]
    ppermute x0 -> x8, waiting for transfers between devices: none -> 18.4 us  [the longest x6 18.4 us: local(): lax.ppermute(x, 'line', along(0, i + 1, 0))]
    ppermute x0 -> x8, starting transfers between devices: none -> 8.23 us  [the longest x6 6.6 us: local(): lax.ppermute(x, 'line', along(0, i + 1, 0))]
    pallas_call x6 -> x8, Pallas kernels: 19.2 us -> 19.6 us  [call(): pl.pallas_call(kernel, out_shape=out, in_specs=[pl.BlockSpec(memory_space...]
  transfers between devices with their start and end apart: 15 -> 23, of which waited for: 6 -> 10; matrix products, arithmetic and copies ran while one was open for 2% -> 3% of each run, Pallas kernels for 4% -> 4%
where the time goes in v4:
time: 156 us; the launch traced here: 154 us
  blocking collectives  45.6 us (29%)
  waiting for transfers between devices  41.4 us (27%)
  starting transfers between devices  33.3 us (21%)
  Pallas kernels  28.3 us (18%)
  local copies, waits for them, and re-layouts  2.94 us (2%)
  other arithmetic  2.01 us (1%)
    all_to_all x1, blocking collectives, local(): lax.all_to_all(send.reshape(DEVICES, SLOTS, scen), ('line', 'bus'), 0, 0,...  23.7 us
    all_to_all x1, blocking collectives, local(): lax.all_to_all(partial_flows.reshape(BUSES_AT, rows, scen), 'bus', 0, 0,...  21.9 us
    pallas_call x8, Pallas kernels, call(): pl.pallas_call(kernel, out_shape=out, in_specs=[pl.BlockSpec(memory_space...  19.6 us
    ppermute x6, waiting for transfers between devices, local(): lax.ppermute(x, 'line', along(0, i + 1, 0))  18.4 us
    ppermute x13, starting transfers between devices, gather(): move = lambda x, *to: lax.ppermute(x, 'line', along(*to))  18.3 us
    ppermute x13, waiting for transfers between devices, gather(): move = lambda x, *to: lax.ppermute(x, 'line', along(*to))  13.5 us
    all_to_all x1, waiting for transfers between devices, local(): dual = lax.all_to_all(dual, 'bus', 0, 0, tiled=True)  9.48 us
    pallas_call x1, Pallas kernels, local(): pl.pallas_call(flows_kernel, out_shape=shape((lines, scen), F32), grid=(l...  8.72 us
  transfers between devices with their start and end apart: 23, of which 10 were waited for; matrix products, arithmetic and copies ran while one was open for 3% of the time, Pallas kernels for 4%

profile of v4, /device:TPU:3, one launch (start us, length us, event | category | flops | bytes accessed | tf_op | source)
XLA Modules:
  0.0 153.8 jit_solution(17952925860744571939)
XLA Ops:
  0.0 1.1 fusion.12
  1.1 3.8 %collective-permute-start.4 = (bf16[8,8832]{1,0:T(8,128)(2,1)S(1)}, bf16[8,8832]{1,0:T(8,128)(2,1)S(1)}, u32[]{:S(2)}, u32[]{:S(2)}) collective-permute-start(bf16[8,8832]{1,0:T(8,128)(2,1)S(1)} %get-tuple-element.47), channel_id=1, source_target_pairs={{0,48},{8,56},{16,0},{24,8},{32,16},{40,24},{48,32},{56,40},{64,11... | collective-permute-start | bytes 423944 | tf_op jit(solution)/shard_map/ppermute | solution.py:40
  4.9 0.3 collective-permute-start
  5.2 0.8 multiply_add_fusion
  6.0 0.3 convert_reduce_fusion
  6.3 0.8 dynamic-slice_bitcast_fusion
  7.1 0.7 fusion.10
  7.8 0.8 dynamic-slice_bitcast_fusion.2.sign
  8.6 0.1 copy.14
  8.8 1.7 %collective-permute-done.3 = bf16[8,8832]{1,0:T(8,128)(2,1)S(1)} collective-permute-done((bf16[8,8832]{1,0:T(8,128)(2,1)S(1)}, bf16[8,8832]{1,0:T(8,128)(2,1)S(1)}, u32[]{:S(2)}, u32[]{:S(2)}) %collective-permute-start.3) | collective-permute-done | bytes 141344 | tf_op jit(solution)/shard_map/ppermute | solution.py:40
  10.4 0.3 collective-permute-start.5
  10.8 0.0 collective-permute-start.6
  10.8 1.7 %collective-permute-done = bf16[16,8832]{1,0:T(8,128)(2,1)S(1)} collective-permute-done((bf16[16,8832]{1,0:T(8,128)(2,1)}, bf16[16,8832]{1,0:T(8,128)(2,1)S(1)}, u32[]{:S(2)}, u32[]{:S(2)}) %collective-permute-start) | collective-permute-done | bytes 282656 | tf_op jit(solution)/shard_map/ppermute | solution.py:40
  12.5 2.4 %collective-permute-start.2 = (bf16[16,8832]{1,0:T(8,128)(2,1)S(1)}, bf16[16,8832]{1,0:T(8,128)(2,1)S(1)}, u32[]{:S(2)}, u32[]{:S(2)}) collective-permute-start(bf16[16,8832]{1,0:T(8,128)(2,1)S(1)} %pad_maximum_fusion.1), channel_id=1, source_target_pairs={{0,48},{8,56},{16,0},{24,8},{32,16},{40,24},{48,32},{56,40},{64,11... | collective-permute-start | bytes 847880 | tf_op jit(solution)/shard_map/ppermute | solution.py:40
  14.9 0.0 collective-permute-start.1
  14.9 0.1 pad_maximum_fusion.refs_0_
  15.0 4.3 %collective-permute-start.10 = (bf16[48,8832]{1,0:T(8,128)(2,1)S(1)}, bf16[48,8832]{1,0:T(8,128)(2,1)S(1)}, u32[]{:S(2)}, u32[]{:S(2)}) collective-permute-start(bf16[48,8832]{1,0:T(8,128)(2,1)S(1)} %pad_maximum_fusion.refs_0_), channel_id=1, source_target_pairs={{0,8},{8,0},{16,24},{24,16},{32,40},{40,32},{48,56},{56,48},{64,72... | collective-permute-start | bytes 2543624 | tf_op jit(solution)/shard_map/ppermute | solution.py:40
  19.3 5.0 %collective-permute-done.7 = bf16[8,8832]{1,0:T(8,128)(2,1)S(1)} collective-permute-done((bf16[8,8832]{1,0:T(8,128)(2,1)S(1)}, bf16[8,8832]{1,0:T(8,128)(2,1)S(1)}, u32[]{:S(2)}, u32[]{:S(2)}) %collective-permute-start.7) | collective-permute-done | bytes 141344 | tf_op jit(solution)/shard_map/ppermute | solution.py:40
  24.4 3.3 %collective-permute-start.9 = (bf16[8,8832]{1,0:T(8,128)(2,1)S(1)}, bf16[8,8832]{1,0:T(8,128)(2,1)S(1)}, u32[]{:S(2)}, u32[]{:S(2)}) collective-permute-start(bf16[8,8832]{1,0:T(8,128)(2,1)S(1)} %slice.19), channel_id=1, source_target_pairs={{0,48},{8,56},{16,0},{24,8},{32,16},{40,24},{48,32},{56,40},{64,11... | collective-permute-start | bytes 423944 | tf_op jit(solution)/shard_map/ppermute | solution.py:40
  27.8 1.5 collective-permute-start.11
  29.2 3.6 %collective-permute-done.8 = bf16[8,8832]{1,0:T(8,128)(2,1)S(1)} collective-permute-done((bf16[8,8832]{1,0:T(8,128)(2,1)S(1)}, bf16[8,8832]{1,0:T(8,128)(2,1)S(1)}, u32[]{:S(2)}, u32[]{:S(2)}) %collective-permute-start.8) | collective-permute-done | bytes 141344 | tf_op jit(solution)/shard_map/ppermute | solution.py:40
  32.9 2.4 %collective-permute-start.12 = (bf16[32,8832]{1,0:T(8,128)(2,1)S(1)}, bf16[32,8832]{1,0:T(8,128)(2,1)S(1)}, u32[]{:S(2)}, u32[]{:S(2)}) collective-permute-start(bf16[32,8832]{1,0:T(8,128)(2,1)S(1)} %constant_dynamic-update-slice_fusion.3.refs_2_), channel_id=1, source_target_pairs={{0,8},{8,0},{16,24},{24,16},{32,40},{40,32},{48,56},{56,48},{64,72... | collective-permute-start | bytes 1695752 | tf_op jit(solution)/shard_map/ppermute | solution.py:40
  35.3 1.6 %collective-permute-done.12.refs_5_ = bf16[32,8832]{1,0:T(8,128)(2,1)S(1)} collective-permute-done((bf16[32,8832]{1,0:T(8,128)(2,1)S(1)}, bf16[32,8832]{1,0:T(8,128)(2,1)S(1)}, u32[]{:S(2)}, u32[]{:S(2)}) %collective-permute-start.12) | collective-permute-done | bytes 565280 | tf_op jit(solution)/shard_map/ppermute | solution.py:40
  36.9 8.7 %shard_map.109 = f32[1024,256]{1,0:T(8,128)S(1)} custom-call(bf16[1024,8832]{1,0:T(8,128)(2,1)} %ptdf.5, bf16[48,8832]{1,0:T(8,128)(2,1)S(1)} %pad_maximum_fusion.refs_0_, bf16[48,8832]{1,0:T(8,128)(2,1)S(1)} %constant_dynamic-update-slice_fusion.refs_1_, bf16[32,8832]{1,0:T(8,128)(2,1)S(1)} %constant_dynamic-update-slice_fusion.3.refs_2_, ...), custom_call_target="tpu_custom_call" | custom-call | flops 4630511616 | bytes 18087936 | tf_op jit(solution)/shard_map/pallas_call | solution.py:249
  45.6 21.9 %all_to_all.15.parts = f32[8,128,256]{2,1,0:T(8,128)S(1)} all-to-all(f32[8,128,256]{2,1,0:T(8,128)S(1)} %bitcast.16), channel_id=1, replica_groups=mesh['line'=16,'bus'=8] {'bus'}, dimensions={0} | all-to-all | bytes 2097152 | tf_op jit(solution)/shard_map/all_to_all | solution.py:261
  67.5 1.1 shard_map.110
  68.6 3.5 %all-to-all-start.1 = ((bf16[8,256,128]{2,1,0:T(8,128)(2,1)}), bf16[8,256,128]{2,1,0:T(8,128)(2,1)S(1)}, u32[]{:S(2)}, u32[]{:S(2)}) async-start(bf16[8,256,128]{2,1,0:T(8,128)(2,1)} %shard_map.110), calls=%async_computation.1 | async-start | bytes 1048576 | tf_op jit(solution)/shard_map/all_to_all | solution.py:268
  72.1 9.5 %all-to-all-done.1.dual = bf16[8,256,128]{2,1,0:T(8,128)(2,1)S(1)} async-done(((bf16[8,256,128]{2,1,0:T(8,128)(2,1)}), bf16[8,256,128]{2,1,0:T(8,128)(2,1)S(1)}, u32[]{:S(2)}, u32[]{:S(2)}) %all-to-all-start.1) | async-done | bytes 524320 | tf_op jit(solution)/shard_map/all_to_all | solution.py:268
  81.6 7.0 %shard_map.112 = bf16[4480,256]{1,0:T(8,128)(2,1)} custom-call(s32[1]{0:T(128)} %bitcast.11.start, bf16[1024,8832]{1,0:T(8,128)(2,1)} %ptdf.5, bf16[8,256,128]{2,1,0:T(8,128)(2,1)S(1)} %all-to-all-done.1.dual), custom_call_target="tpu_custom_call" | custom-call | flops 2315255808 | bytes 9043968 | tf_op jit(solution)/shard_map/pallas_call | solution.py:94
  88.6 3.3 %collective-permute-start.13 = (bf16[4480,256]{1,0:T(8,128)(2,1)}, bf16[4480,256]{1,0:T(8,128)(2,1)}, u32[]{:S(2)}, u32[]{:S(2)}) collective-permute-start(bf16[4480,256]{1,0:T(8,128)(2,1)} %shard_map.112), channel_id=1, source_target_pairs={{0,8},{8,0},{16,24},{24,16},{32,40},{40,32},{48,56},{56,48},{64,72... | collective-permute-start | bytes 6881288 | tf_op jit(solution)/shard_map/ppermute | solution.py:281
  91.9 0.1 pad_add_fusion.1.at
  92.0 5.7 %shard_map.111.keep = f32[4480,256]{1,0:T(8,128)S(1)} custom-call(s32[1]{0:T(128)} %bitcast.9.start, bf16[1024,8832]{1,0:T(8,128)(2,1)} %ptdf.5, bf16[8,256,128]{2,1,0:T(8,128)(2,1)S(1)} %all-to-all-done.1.dual), custom_call_target="tpu_custom_call" | custom-call | flops 2315255808 | bytes 9043968 | tf_op jit(solution)/shard_map/pallas_call | solution.py:94
  97.7 2.5 %shard_map.113 = (bf16[4,552,128]{2,1,0:T(8,128)(2,1)S(1)}, bf16[2,552,128]{2,1,0:T(8,128)(2,1)S(1)}, bf16[2,552,128]{2,1,0:T(8,128)(2,1)S(1)}, bf16[2,552,128]{...) custom-call(s32[3]{0:T(128)S(1)} %pad_add_fusion.1.at, f32[4480,256]{1,0:T(8,128)S(1)} %shard_map.111.keep, ...), custom_call_target="tpu_custom_call" | custom-call | flops 1146880 | bytes 9175040 | tf_op jit(solution)/shard_map/pallas_call | solution.py:94
  100.2 1.0 collective-permute-start.18
  101.2 1.1 collective-permute-start.15
  102.3 1.6 %collective-permute-start.16 = (bf16[2,552,128]{2,1,0:T(8,128)(2,1)S(1)}, bf16[2,552,128]{2,1,0:T(8,128)(2,1)S(1)}, u32[]{:S(2)}, u32[]{:S(2)}) collective-permute-start(bf16[2,552,128]{2,1,0:T(8,128)(2,1)S(1)} %get-tuple-element.36), channel_id=1, source_target_pairs={{0,48},{8,56},{16,0},{24,8},{32,16},{40,24},{48,32},{56,40},{64,11... | collective-permute-start | bytes 847880 | tf_op jit(solution)/shard_map/ppermute | solution.py:298
  103.9 12.6 %collective-permute-done.14.got_1 = bf16[2,552,128]{2,1,0:T(8,128)(2,1)S(1)} collective-permute-done((bf16[2,552,128]{2,1,0:T(8,128)(2,1)S(1)}, bf16[2,552,128]{2,1,0:T(8,128)(2,1)S(1)}, u32[]{:S(2)}, u32[]{:S(2)}) %collective-permute-start.14) | collective-permute-done | bytes 282656 | tf_op jit(solution)/shard_map/ppermute | solution.py:298
  116.5 0.3 collective-permute-done.16.got_3
  116.9 0.1 shard_map.114
  117.0 0.6 collective-permute-start.17
  117.6 0.1 shard_map.115
  117.7 0.9 collective-permute-start.19
  118.6 3.0 %collective-permute-start.20 = (bf16[552,128]{1,0:T(8,128)(2,1)S(1)}, bf16[552,128]{1,0:T(8,128)(2,1)S(1)}, u32[]{:S(2)}, u32[]{:S(2)}) collective-permute-start(bf16[552,128]{1,0:T(8,128)(2,1)S(1)} %get-tuple-element.43), channel_id=1, source_target_pairs={{0,32},{8,40},{16,48},{24,56},{32,0},{40,8},{48,16},{56,24},{64,96... | collective-permute-start | bytes 423944 | tf_op jit(solution)/shard_map/ppermute | solution.py:298
  121.6 1.3 collective-permute-done.19.got_1
  122.9 4.1 %collective-permute-done.20.got_2 = bf16[552,128]{1,0:T(8,128)(2,1)S(1)} collective-permute-done((bf16[552,128]{1,0:T(8,128)(2,1)S(1)}, bf16[552,128]{1,0:T(8,128)(2,1)S(1)}, u32[]{:S(2)}, u32[]{:S(2)}) %collective-permute-start.20) | collective-permute-done | bytes 141344 | tf_op jit(solution)/shard_map/ppermute | solution.py:298
  127.0 1.8 %shard_map.116 = f32[1024,256]{1,0:T(8,128)S(1)} custom-call(s32[4,552]{1,0:T(4,128)S(1)} %pad_add_fusion.plan, f32[552,128]{1,0:T(8,128)S(1)} %get-tuple-element.37.low, bf16[552,128]{1,0:T(8,128)(2,1)S(1)} %collective-permute-done.17.got_low, f32[552,128]{1,0:T(8,128)S(1)} %get-tuple-element.41.high, bf16[552,128]{1,0:T(8,128)(2,1)S(1)} %collective-permute-done.19.got_1, ...), custom_call_target="tpu_custom_call" | custom-call | flops 868220928 | bytes 2260992 | tf_op jit(solution)/shard_map/pallas_call | solution.py:94
  128.8 23.7 %all_to_all.16.terms = f32[128,8,256]{2,1,0:T(8,128)S(1)} all-to-all(f32[128,8,256]{2,1,0:T(8,128)S(1)} %bitcast.17), channel_id=1, replica_groups=mesh['line'=16,'bus'=8] {'line','bus'}, dimensions={0} | all-to-all | bytes 2097152 | tf_op jit(solution)/shard_map/all_to_all | solution.py:311
  152.5 1.3 shard_map.117
  (41 shorter events, 0.3 us)
Async XLA Ops:
  0.0 6.3 %copy-start = (s32[1024,256]{1,0:T(8,128)S(1)}, s32[1024,256]{1,0:T(8,128)}, u32[]{:S(2)}) copy-start(s32[1024,256]{1,0:T(8,128)} %param.13) | copy-start | bytes 3145732
  0.0 14.9 %copy-start.1 = (bf16[8832,16]{0,1:T(8,128)(2,1)S(1)}, bf16[8832,16]{0,1:T(8,128)(2,1)}, u32[]{:S(2)}) copy-start(bf16[8832,16]{0,1:T(8,128)(2,1)} %param.12) | copy-start | bytes 847876
  1.1 7.6 %collective-permute-start.4 = (bf16[8,8832]{1,0:T(8,128)(2,1)S(1)}, bf16[8,8832]{1,0:T(8,128)(2,1)S(1)}, u32[]{:S(2)}, u32[]{:S(2)}) collective-permute-start(bf16[8,8832]{1,0:T(8,128)(2,1)S(1)} %get-tuple-element.47), channel_id=1, source_target_pairs={{0,48},{8,56},{16,0},{24,8},{32,16},{40,24},{48,32},{56,40},{64,11... | collective-permute-start | bytes 423944 | tf_op jit(solution)/shard_map/ppermute | solution.py:40
  4.9 5.5 %collective-permute-start.3 = (bf16[8,8832]{1,0:T(8,128)(2,1)S(1)}, bf16[8,8832]{1,0:T(8,128)(2,1)S(1)}, u32[]{:S(2)}, u32[]{:S(2)}) collective-permute-start(bf16[8,8832]{1,0:T(8,128)(2,1)S(1)} %get-tuple-element.47), channel_id=1, source_target_pairs={{0,16},{8,24},{16,32},{24,40},{32,48},{40,56},{48,0},{56,8},{64,80... | collective-permute-start | bytes 423944 | tf_op jit(solution)/shard_map/ppermute | solution.py:40
  4.9 7.5 %collective-permute-start = (bf16[16,8832]{1,0:T(8,128)(2,1)}, bf16[16,8832]{1,0:T(8,128)(2,1)S(1)}, u32[]{:S(2)}, u32[]{:S(2)}) collective-permute-start(bf16[16,8832]{1,0:T(8,128)(2,1)} %bitcast.21), channel_id=1, source_target_pairs={{0,64},{8,72},{16,80},{24,88},{32,96},{40,104},{48,112},{56,120},{... | collective-permute-start | bytes 847880 | tf_op jit(solution)/shard_map/ppermute | solution.py:40
  10.4 17.3 %collective-permute-start.5 = (bf16[16,8832]{1,0:T(8,128)(2,1)S(1)}, bf16[16,8832]{1,0:T(8,128)(2,1)S(1)}, u32[]{:S(2)}, u32[]{:S(2)}) collective-permute-start(bf16[16,8832]{1,0:T(8,128)(2,1)S(1)} %pad_maximum_fusion.2), channel_id=1, source_target_pairs={{0,64},{8,72},{16,80},{24,88},{32,96},{40,104},{48,112},{56,120},{... | collective-permute-start | bytes 847880 | tf_op jit(solution)/shard_map/ppermute | solution.py:40
  10.8 8.5 %collective-permute-start.6 = (bf16[8,8832]{1,0:T(8,128)(2,1)S(1)}, bf16[8,8832]{1,0:T(8,128)(2,1)S(1)}, u32[]{:S(2)}, u32[]{:S(2)}) collective-permute-start(bf16[8,8832]{1,0:T(8,128)(2,1)S(1)} %collective-permute-done.3), channel_id=1, source_target_pairs={{0,16},{8,24},{16,32},{24,40},{32,48},{40,56},{48,0},{56,8},{64,80... | collective-permute-start | bytes 423944 | tf_op jit(solution)/shard_map/ppermute | solution.py:40
  12.5 11.8 %collective-permute-start.2 = (bf16[16,8832]{1,0:T(8,128)(2,1)S(1)}, bf16[16,8832]{1,0:T(8,128)(2,1)S(1)}, u32[]{:S(2)}, u32[]{:S(2)}) collective-permute-start(bf16[16,8832]{1,0:T(8,128)(2,1)S(1)} %pad_maximum_fusion.1), channel_id=1, source_target_pairs={{0,48},{8,56},{16,0},{24,8},{32,16},{40,24},{48,32},{56,40},{64,11... | collective-permute-start | bytes 847880 | tf_op jit(solution)/shard_map/ppermute | solution.py:40
  14.9 9.4 %collective-permute-start.1 = (bf16[16,8832]{1,0:T(8,128)(2,1)S(1)}, bf16[16,8832]{1,0:T(8,128)(2,1)S(1)}, u32[]{:S(2)}, u32[]{:S(2)}) collective-permute-start(bf16[16,8832]{1,0:T(8,128)(2,1)S(1)} %pad_maximum_fusion.1), channel_id=1, source_target_pairs={{0,16},{8,24},{16,32},{24,40},{32,48},{40,56},{48,0},{56,8},{64,80... | collective-permute-start | bytes 847880 | tf_op jit(solution)/shard_map/ppermute | solution.py:40
  15.0 20.3 %collective-permute-start.10 = (bf16[48,8832]{1,0:T(8,128)(2,1)S(1)}, bf16[48,8832]{1,0:T(8,128)(2,1)S(1)}, u32[]{:S(2)}, u32[]{:S(2)}) collective-permute-start(bf16[48,8832]{1,0:T(8,128)(2,1)S(1)} %pad_maximum_fusion.refs_0_), channel_id=1, source_target_pairs={{0,8},{8,0},{16,24},{24,16},{32,40},{40,32},{48,56},{56,48},{64,72... | collective-permute-start | bytes 2543624 | tf_op jit(solution)/shard_map/ppermute | solution.py:40
  19.3 5.0 %collective-permute-start.7 = (bf16[8,8832]{1,0:T(8,128)(2,1)S(1)}, bf16[8,8832]{1,0:T(8,128)(2,1)S(1)}, u32[]{:S(2)}, u32[]{:S(2)}) collective-permute-start(bf16[8,8832]{1,0:T(8,128)(2,1)S(1)} %collective-permute-done.6), channel_id=1, source_target_pairs={{0,64},{8,72},{16,80},{24,88},{32,96},{40,104},{48,112},{56,120},{... | collective-permute-start | bytes 423944 | tf_op jit(solution)/shard_map/ppermute | solution.py:40
  24.4 8.5 %collective-permute-start.9 = (bf16[8,8832]{1,0:T(8,128)(2,1)S(1)}, bf16[8,8832]{1,0:T(8,128)(2,1)S(1)}, u32[]{:S(2)}, u32[]{:S(2)}) collective-permute-start(bf16[8,8832]{1,0:T(8,128)(2,1)S(1)} %slice.19), channel_id=1, source_target_pairs={{0,48},{8,56},{16,0},{24,8},{32,16},{40,24},{48,32},{56,40},{64,11... | collective-permute-start | bytes 423944 | tf_op jit(solution)/shard_map/ppermute | solution.py:40
  27.7 5.1 %collective-permute-start.8 = (bf16[8,8832]{1,0:T(8,128)(2,1)S(1)}, bf16[8,8832]{1,0:T(8,128)(2,1)S(1)}, u32[]{:S(2)}, u32[]{:S(2)}) collective-permute-start(bf16[8,8832]{1,0:T(8,128)(2,1)S(1)} %slice.18), channel_id=1, source_target_pairs={{0,16},{8,24},{16,32},{24,40},{32,48},{40,56},{48,0},{56,8},{64,80... | collective-permute-start | bytes 423944 | tf_op jit(solution)/shard_map/ppermute | solution.py:40
  27.8 9.1 %collective-permute-start.11 = (bf16[48,8832]{1,0:T(8,128)(2,1)S(1)}, bf16[48,8832]{1,0:T(8,128)(2,1)S(1)}, u32[]{:S(2)}, u32[]{:S(2)}) collective-permute-start(bf16[48,8832]{1,0:T(8,128)(2,1)S(1)} %constant_dynamic-update-slice_fusion.refs_1_), channel_id=1, source_target_pairs={{0,8},{8,0},{16,24},{24,16},{32,40},{40,32},{48,56},{56,48},{64,72... | collective-permute-start | bytes 2543624 | tf_op jit(solution)/shard_map/ppermute | solution.py:40
  32.9 4.0 %collective-permute-start.12 = (bf16[32,8832]{1,0:T(8,128)(2,1)S(1)}, bf16[32,8832]{1,0:T(8,128)(2,1)S(1)}, u32[]{:S(2)}, u32[]{:S(2)}) collective-permute-start(bf16[32,8832]{1,0:T(8,128)(2,1)S(1)} %constant_dynamic-update-slice_fusion.3.refs_2_), channel_id=1, source_target_pairs={{0,8},{8,0},{16,24},{24,16},{32,40},{40,32},{48,56},{56,48},{64,72... | collective-permute-start | bytes 1695752 | tf_op jit(solution)/shard_map/ppermute | solution.py:40
  68.6 13.0 %all-to-all-start.1 = ((bf16[8,256,128]{2,1,0:T(8,128)(2,1)}), bf16[8,256,128]{2,1,0:T(8,128)(2,1)S(1)}, u32[]{:S(2)}, u32[]{:S(2)}) async-start(bf16[8,256,128]{2,1,0:T(8,128)(2,1)} %shard_map.110), calls=%async_computation.1 | async-start | bytes 1048576 | tf_op jit(solution)/shard_map/all_to_all | solution.py:268
  88.6 9.1 %collective-permute-start.13 = (bf16[4480,256]{1,0:T(8,128)(2,1)}, bf16[4480,256]{1,0:T(8,128)(2,1)}, u32[]{:S(2)}, u32[]{:S(2)}) collective-permute-start(bf16[4480,256]{1,0:T(8,128)(2,1)} %shard_map.112), channel_id=1, source_target_pairs={{0,8},{8,0},{16,24},{24,16},{32,40},{40,32},{48,56},{56,48},{64,72... | collective-permute-start | bytes 6881288 | tf_op jit(solution)/shard_map/ppermute | solution.py:281
  100.2 17.4 %collective-permute-start.18 = (bf16[4,552,128]{2,1,0:T(8,128)(2,1)S(1)}, bf16[4,552,128]{2,1,0:T(8,128)(2,1)S(1)}, u32[]{:S(2)}, u32[]{:S(2)}) collective-permute-start(bf16[4,552,128]{2,1,0:T(8,128)(2,1)S(1)} %get-tuple-element.40), channel_id=1, source_target_pairs={{0,64},{8,72},{16,80},{24,88},{32,96},{40,104},{48,112},{56,120},{... | collective-permute-start | bytes 1695752 | tf_op jit(solution)/shard_map/ppermute | solution.py:297
  101.2 15.3 %collective-permute-start.14 = (bf16[2,552,128]{2,1,0:T(8,128)(2,1)S(1)}, bf16[2,552,128]{2,1,0:T(8,128)(2,1)S(1)}, u32[]{:S(2)}, u32[]{:S(2)}) collective-permute-start(bf16[2,552,128]{2,1,0:T(8,128)(2,1)S(1)} %get-tuple-element.34), channel_id=1, source_target_pairs={{0,16},{8,24},{16,32},{24,40},{32,48},{40,56},{48,0},{56,8},{64,80... | collective-permute-start | bytes 847880 | tf_op jit(solution)/shard_map/ppermute | solution.py:298
  101.2 15.3 %collective-permute-start.15 = (bf16[2,552,128]{2,1,0:T(8,128)(2,1)S(1)}, bf16[2,552,128]{2,1,0:T(8,128)(2,1)S(1)}, u32[]{:S(2)}, u32[]{:S(2)}) collective-permute-start(bf16[2,552,128]{2,1,0:T(8,128)(2,1)S(1)} %get-tuple-element.35), channel_id=1, source_target_pairs={{0,32},{8,40},{16,48},{24,56},{32,0},{40,8},{48,16},{56,24},{64,96... | collective-permute-start | bytes 847880 | tf_op jit(solution)/shard_map/ppermute | solution.py:298
  102.3 14.6 %collective-permute-start.16 = (bf16[2,552,128]{2,1,0:T(8,128)(2,1)S(1)}, bf16[2,552,128]{2,1,0:T(8,128)(2,1)S(1)}, u32[]{:S(2)}, u32[]{:S(2)}) collective-permute-start(bf16[2,552,128]{2,1,0:T(8,128)(2,1)S(1)} %get-tuple-element.36), channel_id=1, source_target_pairs={{0,48},{8,56},{16,0},{24,8},{32,16},{40,24},{48,32},{56,40},{64,11... | collective-permute-start | bytes 847880 | tf_op jit(solution)/shard_map/ppermute | solution.py:298
  117.0 4.6 %collective-permute-start.17 = (bf16[552,128]{1,0:T(8,128)(2,1)S(1)}, bf16[552,128]{1,0:T(8,128)(2,1)S(1)}, u32[]{:S(2)}, u32[]{:S(2)}) collective-permute-start(bf16[552,128]{1,0:T(8,128)(2,1)S(1)} %get-tuple-element.38), channel_id=1, source_target_pairs={{0,64},{8,72},{16,80},{24,88},{32,96},{40,104},{48,112},{56,120},{... | collective-permute-start | bytes 423944 | tf_op jit(solution)/shard_map/ppermute | solution.py:297
  117.7 5.2 %collective-permute-start.19 = (bf16[552,128]{1,0:T(8,128)(2,1)S(1)}, bf16[552,128]{1,0:T(8,128)(2,1)S(1)}, u32[]{:S(2)}, u32[]{:S(2)}) collective-permute-start(bf16[552,128]{1,0:T(8,128)(2,1)S(1)} %get-tuple-element.42), channel_id=1, source_target_pairs={{0,16},{8,24},{16,32},{24,40},{32,48},{40,56},{48,0},{56,8},{64,80... | collective-permute-start | bytes 423944 | tf_op jit(solution)/shard_map/ppermute | solution.py:298
  118.6 8.4 %collective-permute-start.20 = (bf16[552,128]{1,0:T(8,128)(2,1)S(1)}, bf16[552,128]{1,0:T(8,128)(2,1)S(1)}, u32[]{:S(2)}, u32[]{:S(2)}) collective-permute-start(bf16[552,128]{1,0:T(8,128)(2,1)S(1)} %get-tuple-element.43), channel_id=1, source_target_pairs={{0,32},{8,40},{16,48},{24,56},{32,0},{40,8},{48,16},{56,24},{64,96... | collective-permute-start | bytes 423944 | tf_op jit(solution)/shard_map/ppermute | solution.py:298
  121.6 5.4 %collective-permute-start.21 = (bf16[552,128]{1,0:T(8,128)(2,1)S(1)}, bf16[552,128]{1,0:T(8,128)(2,1)S(1)}, u32[]{:S(2)}, u32[]{:S(2)}) collective-permute-start(bf16[552,128]{1,0:T(8,128)(2,1)S(1)} %get-tuple-element.44), channel_id=1, source_target_pairs={{0,48},{8,56},{16,0},{24,8},{32,16},{40,24},{48,32},{56,40},{64,11... | collective-permute-start | bytes 423944 | tf_op jit(solution)/shard_map/ppermute | solution.py:298

commit v5 on v4

--- a/solution.py
+++ b/solution.py
@@ -41,10 +41,12 @@
     stack = lambda *x: jnp.concatenate(x, 0)
     half = block.shape[0] // 2
     low, high = block[:half], block[half:]
+    low_x = move(low, 1, 0, 0)
+    high, low_x = lax.optimization_barrier((high, low_x))
+    high_x = move(high, 1, 0, 0)
     high_1, high_3 = move(high, 0, 1, 0), move(high, 0, 3, 0)
-    beside = move(block, 1, 0, 0)
     high_2 = move(high_1, 0, 1, 0)
-    pair = stack(low, beside[:half])
+    pair = stack(low, low_x)
     pair_1, pair_3 = move(pair, 0, 1, 0), move(pair, 0, 3, 0)
     high_z = stack(high_1, high_3)
     high_zx = move(high_z, 1, 0, 0)
@@ -52,7 +54,7 @@
     pair_1, pair_3, ready = lax.optimization_barrier((pair_1, pair_3, ready))
     low_2, beside_2 = move(pair_1[:half], 0, 1, 0), move(pair_3[half:], 0, 3, 0)
     pieces = [
-        stack(block, beside, high_z),
+        stack(block, low_x, high_x, high_z),
         stack(pair_1, pair_3, high_zx),
         stack(high_2, high_2x, low_2, beside_2),
     ]

time: 156 us -> 153 us (0.981)
  waiting for transfers between devices: 41.4 us -> 38.7 us
    ppermute x13 -> x14, waiting for transfers between devices: 13.5 us -> 10.8 us  [gather(): move = lambda x, *to: lax.ppermute(x, 'line', along(*to))]
    ppermute x13 -> x14, starting transfers between devices: 18.3 us -> 18.2 us  [gather(): move = lambda x, *to: lax.ppermute(x, 'line', along(*to))]
  transfers between devices with their start and end apart: 23 -> 24, of which waited for: 10 -> 11; matrix products, arithmetic and copies ran while one was open for 3% -> 3% of each run, Pallas kernels for 4% -> 4%
where the time goes in v5:
time: 153 us; the launch traced here: 151 us
  blocking collectives  45.2 us (30%)
  waiting for transfers between devices  38.7 us (25%)
  starting transfers between devices  33.2 us (22%)
  Pallas kernels  28.3 us (18%)
  local copies, waits for them, and re-layouts  3.98 us (3%)
    all_to_all x1, blocking collectives, local(): lax.all_to_all(send.reshape(DEVICES, SLOTS, scen), ('line', 'bus'), 0, 0,...  23.7 us
    all_to_all x1, blocking collectives, local(): lax.all_to_all(partial_flows.reshape(BUSES_AT, rows, scen), 'bus', 0, 0,...  21.5 us
    pallas_call x8, Pallas kernels, call(): pl.pallas_call(kernel, out_shape=out, in_specs=[pl.BlockSpec(memory_space...  19.6 us
    ppermute x6, waiting for transfers between devices, local(): lax.ppermute(x, 'line', along(0, i + 1, 0))  18.4 us
    ppermute x14, starting transfers between devices, gather(): move = lambda x, *to: lax.ppermute(x, 'line', along(*to))  18.2 us
    ppermute x14, waiting for transfers between devices, gather(): move = lambda x, *to: lax.ppermute(x, 'line', along(*to))  10.8 us
    all_to_all x1, waiting for transfers between devices, local(): dual = lax.all_to_all(dual, 'bus', 0, 0, tiled=True)  9.48 us
    pallas_call x1, Pallas kernels, local(): pl.pallas_call(flows_kernel, out_shape=shape((lines, scen), F32), grid=(l...  8.73 us
  transfers between devices with their start and end apart: 24, of which 11 were waited for; matrix products, arithmetic and copies ran while one was open for 3% of the time, Pallas kernels for 4%

profile of v5, /device:TPU:3, one launch (start us, length us, event | category | flops | bytes accessed | tf_op | source)
XLA Modules:
  0.0 151.0 jit_solution(13771977044591687893)
XLA Ops:
  0.0 1.1 fusion.12
  1.1 0.1 collective-permute-start
  1.3 1.0 constant_dynamic-update-slice_fusion.4
  2.3 0.8 multiply_add_fusion
  3.1 0.3 convert_reduce_fusion
  3.4 0.8 dynamic-slice_bitcast_fusion
  4.2 0.8 dynamic-slice_bitcast_fusion.2.sign
  5.0 0.1 copy.14
  5.1 0.6 collective-permute-done
  5.8 3.8 %collective-permute-start.5 = (bf16[8,8832]{1,0:T(8,128)(2,1)S(1)}, bf16[8,8832]{1,0:T(8,128)(2,1)S(1)}, u32[]{:S(2)}, u32[]{:S(2)}) collective-permute-start(bf16[8,8832]{1,0:T(8,128)(2,1)S(1)} %get-tuple-element.30), channel_id=1, source_target_pairs={{0,48},{8,56},{16,0},{24,8},{32,16},{40,24},{48,32},{56,40},{64,11... | collective-permute-start | bytes 423944 | tf_op jit(solution)/shard_map/ppermute | solution.py:40
  9.5 0.8 collective-permute-start.3
  10.4 2.7 %collective-permute-start.2 = (bf16[16,8832]{1,0:T(8,128)(2,1)S(1)}, bf16[16,8832]{1,0:T(8,128)(2,1)S(1)}, u32[]{:S(2)}, u32[]{:S(2)}) collective-permute-start(bf16[16,8832]{1,0:T(8,128)(2,1)S(1)} %pad_maximum_fusion), channel_id=1, source_target_pairs={{0,48},{8,56},{16,0},{24,8},{32,16},{40,24},{48,32},{56,40},{64,11... | collective-permute-start | bytes 847880 | tf_op jit(solution)/shard_map/ppermute | solution.py:40
  13.2 1.5 collective-permute-done.4
  14.7 0.9 collective-permute-start.6
  15.7 2.7 %collective-permute-start.11 = (bf16[48,8832]{1,0:T(8,128)(2,1)S(1)}, bf16[48,8832]{1,0:T(8,128)(2,1)S(1)}, u32[]{:S(2)}, u32[]{:S(2)}) collective-permute-start(bf16[48,8832]{1,0:T(8,128)(2,1)S(1)} %constant_dynamic-update-slice_fusion.refs_0_), channel_id=1, source_target_pairs={{0,8},{8,0},{16,24},{24,16},{32,40},{40,32},{48,56},{56,48},{64,72... | collective-permute-start | bytes 2543624 | tf_op jit(solution)/shard_map/ppermute | solution.py:40
  18.4 2.5 %collective-permute-done.1 = bf16[16,8832]{1,0:T(8,128)(2,1)S(1)} collective-permute-done((bf16[16,8832]{1,0:T(8,128)(2,1)S(1)}, bf16[16,8832]{1,0:T(8,128)(2,1)S(1)}, u32[]{:S(2)}, u32[]{:S(2)}) %collective-permute-start.1) | collective-permute-done | bytes 282656 | tf_op jit(solution)/shard_map/ppermute | solution.py:40
  21.0 0.3 collective-permute-start.10
  21.3 1.2 collective-permute-start.9
  22.5 2.9 %collective-permute-done.7 = bf16[8,8832]{1,0:T(8,128)(2,1)S(1)} collective-permute-done((bf16[8,8832]{1,0:T(8,128)(2,1)S(1)}, bf16[8,8832]{1,0:T(8,128)(2,1)S(1)}, u32[]{:S(2)}, u32[]{:S(2)}) %collective-permute-start.7) | collective-permute-done | bytes 141344 | tf_op jit(solution)/shard_map/ppermute | solution.py:40
  25.5 1.1 collective-permute-start.8
  26.6 1.4 collective-permute-start.12
  28.0 1.7 %collective-permute-done.8 = bf16[8,8832]{1,0:T(8,128)(2,1)S(1)} collective-permute-done((bf16[8,8832]{1,0:T(8,128)(2,1)S(1)}, bf16[8,8832]{1,0:T(8,128)(2,1)S(1)}, u32[]{:S(2)}, u32[]{:S(2)}) %collective-permute-start.8) | collective-permute-done | bytes 141344 | tf_op jit(solution)/shard_map/ppermute | solution.py:40
  29.8 3.1 %collective-permute-start.13 = (bf16[32,8832]{1,0:T(8,128)(2,1)S(1)}, bf16[32,8832]{1,0:T(8,128)(2,1)S(1)}, u32[]{:S(2)}, u32[]{:S(2)}) collective-permute-start(bf16[32,8832]{1,0:T(8,128)(2,1)S(1)} %constant_dynamic-update-slice_fusion.8.refs_2_), channel_id=1, source_target_pairs={{0,8},{8,0},{16,24},{24,16},{32,40},{40,32},{48,56},{56,48},{64,72... | collective-permute-start | bytes 1695752 | tf_op jit(solution)/shard_map/ppermute | solution.py:40
  32.9 1.6 %collective-permute-done.13.refs_5_ = bf16[32,8832]{1,0:T(8,128)(2,1)S(1)} collective-permute-done((bf16[32,8832]{1,0:T(8,128)(2,1)S(1)}, bf16[32,8832]{1,0:T(8,128)(2,1)S(1)}, u32[]{:S(2)}, u32[]{:S(2)}) %collective-permute-start.13) | collective-permute-done | bytes 565280 | tf_op jit(solution)/shard_map/ppermute | solution.py:40
  34.5 8.7 %shard_map.109 = f32[1024,256]{1,0:T(8,128)S(1)} custom-call(bf16[1024,8832]{1,0:T(8,128)(2,1)} %ptdf.5, bf16[48,8832]{1,0:T(8,128)(2,1)S(1)} %constant_dynamic-update-slice_fusion.refs_0_, bf16[48,8832]{1,0:T(8,128)(2,1)S(1)} %constant_dynamic-update-slice_fusion.5.refs_1_, bf16[32,8832]{1,0:T(8,128)(2,1)S(1)} %constant_dynamic-update-slice_fusion.8.refs_2_, ...), custom_call_target="tpu_custom_call" | custom-call | flops 4630511616 | bytes 18087936 | tf_op jit(solution)/shard_map/pallas_call | solution.py:251
  43.2 21.5 %all_to_all.15.parts = f32[8,128,256]{2,1,0:T(8,128)S(1)} all-to-all(f32[8,128,256]{2,1,0:T(8,128)S(1)} %bitcast.17), channel_id=1, replica_groups=mesh['line'=16,'bus'=8] {'bus'}, dimensions={0} | all-to-all | bytes 2097152 | tf_op jit(solution)/shard_map/all_to_all | solution.py:263
  64.7 1.1 shard_map.110
  65.8 3.5 %all-to-all-start.1 = ((bf16[8,256,128]{2,1,0:T(8,128)(2,1)}), bf16[8,256,128]{2,1,0:T(8,128)(2,1)S(1)}, u32[]{:S(2)}, u32[]{:S(2)}) async-start(bf16[8,256,128]{2,1,0:T(8,128)(2,1)} %shard_map.110), calls=%async_computation.1 | async-start | bytes 1048576 | tf_op jit(solution)/shard_map/all_to_all | solution.py:270
  69.3 9.5 %all-to-all-done.1.dual = bf16[8,256,128]{2,1,0:T(8,128)(2,1)S(1)} async-done(((bf16[8,256,128]{2,1,0:T(8,128)(2,1)}), bf16[8,256,128]{2,1,0:T(8,128)(2,1)S(1)}, u32[]{:S(2)}, u32[]{:S(2)}) %all-to-all-start.1) | async-done | bytes 524320 | tf_op jit(solution)/shard_map/all_to_all | solution.py:270
  78.8 7.0 %shard_map.112 = bf16[4480,256]{1,0:T(8,128)(2,1)} custom-call(s32[1]{0:T(128)} %bitcast.11.start, bf16[1024,8832]{1,0:T(8,128)(2,1)} %ptdf.5, bf16[8,256,128]{2,1,0:T(8,128)(2,1)S(1)} %all-to-all-done.1.dual), custom_call_target="tpu_custom_call" | custom-call | flops 2315255808 | bytes 9043968 | tf_op jit(solution)/shard_map/pallas_call | solution.py:96
  85.9 3.3 %collective-permute-start.14 = (bf16[4480,256]{1,0:T(8,128)(2,1)}, bf16[4480,256]{1,0:T(8,128)(2,1)}, u32[]{:S(2)}, u32[]{:S(2)}) collective-permute-start(bf16[4480,256]{1,0:T(8,128)(2,1)} %shard_map.112), channel_id=1, source_target_pairs={{0,8},{8,0},{16,24},{24,16},{32,40},{40,32},{48,56},{56,48},{64,72... | collective-permute-start | bytes 6881288 | tf_op jit(solution)/shard_map/ppermute | solution.py:283
  89.2 5.7 %shard_map.111.keep = f32[4480,256]{1,0:T(8,128)S(1)} custom-call(s32[1]{0:T(128)} %bitcast.9.start, bf16[1024,8832]{1,0:T(8,128)(2,1)} %ptdf.5, bf16[8,256,128]{2,1,0:T(8,128)(2,1)S(1)} %all-to-all-done.1.dual), custom_call_target="tpu_custom_call" | custom-call | flops 2315255808 | bytes 9043968 | tf_op jit(solution)/shard_map/pallas_call | solution.py:96
  94.9 2.5 %shard_map.113 = (bf16[4,552,128]{2,1,0:T(8,128)(2,1)S(1)}, bf16[2,552,128]{2,1,0:T(8,128)(2,1)S(1)}, bf16[2,552,128]{2,1,0:T(8,128)(2,1)S(1)}, bf16[2,552,128]{...) custom-call(s32[3]{0:T(128)S(1)} %pad_add_fusion.1.at, f32[4480,256]{1,0:T(8,128)S(1)} %shard_map.111.keep, ...), custom_call_target="tpu_custom_call" | custom-call | flops 1146880 | bytes 9175040 | tf_op jit(solution)/shard_map/pallas_call | solution.py:96
  97.4 1.0 collective-permute-start.19
  98.4 1.2 collective-permute-start.16
  99.6 1.5 collective-permute-start.17
  101.1 12.6 %collective-permute-done.15.got_1 = bf16[2,552,128]{2,1,0:T(8,128)(2,1)S(1)} collective-permute-done((bf16[2,552,128]{2,1,0:T(8,128)(2,1)S(1)}, bf16[2,552,128]{2,1,0:T(8,128)(2,1)S(1)}, u32[]{:S(2)}, u32[]{:S(2)}) %collective-permute-start.15) | collective-permute-done | bytes 282656 | tf_op jit(solution)/shard_map/ppermute | solution.py:300
  113.7 0.3 collective-permute-done.17.got_3
  114.1 0.1 shard_map.114
  114.2 0.6 collective-permute-start.18
  114.8 0.1 shard_map.115
  114.9 0.9 collective-permute-start.20
  115.9 3.0 %collective-permute-start.21 = (bf16[552,128]{1,0:T(8,128)(2,1)S(1)}, bf16[552,128]{1,0:T(8,128)(2,1)S(1)}, u32[]{:S(2)}, u32[]{:S(2)}) collective-permute-start(bf16[552,128]{1,0:T(8,128)(2,1)S(1)} %get-tuple-element.47), channel_id=1, source_target_pairs={{0,32},{8,40},{16,48},{24,56},{32,0},{40,8},{48,16},{56,24},{64,96... | collective-permute-start | bytes 423944 | tf_op jit(solution)/shard_map/ppermute | solution.py:300
  118.8 1.3 collective-permute-done.20.got_1
  120.1 4.1 %collective-permute-done.21.got_2 = bf16[552,128]{1,0:T(8,128)(2,1)S(1)} collective-permute-done((bf16[552,128]{1,0:T(8,128)(2,1)S(1)}, bf16[552,128]{1,0:T(8,128)(2,1)S(1)}, u32[]{:S(2)}, u32[]{:S(2)}) %collective-permute-start.21) | collective-permute-done | bytes 141344 | tf_op jit(solution)/shard_map/ppermute | solution.py:300
  124.2 1.8 %shard_map.116 = f32[1024,256]{1,0:T(8,128)S(1)} custom-call(s32[4,552]{1,0:T(4,128)S(1)} %pad_add_fusion.plan, f32[552,128]{1,0:T(8,128)S(1)} %get-tuple-element.41.low, bf16[552,128]{1,0:T(8,128)(2,1)S(1)} %collective-permute-done.18.got_low, f32[552,128]{1,0:T(8,128)S(1)} %get-tuple-element.45.high, bf16[552,128]{1,0:T(8,128)(2,1)S(1)} %collective-permute-done.20.got_1, ...), custom_call_target="tpu_custom_call" | custom-call | flops 868220928 | bytes 2260992 | tf_op jit(solution)/shard_map/pallas_call | solution.py:96
  126.1 23.7 %all_to_all.16.terms = f32[128,8,256]{2,1,0:T(8,128)S(1)} all-to-all(f32[128,8,256]{2,1,0:T(8,128)S(1)} %bitcast.18), channel_id=1, replica_groups=mesh['line'=16,'bus'=8] {'line','bus'}, dimensions={0} | all-to-all | bytes 2097152 | tf_op jit(solution)/shard_map/all_to_all | solution.py:313
  149.7 1.3 shard_map.117
  (52 shorter events, 0.5 us)
Async XLA Ops:
  0.0 3.4 %copy-start = (s32[1024,256]{1,0:T(8,128)S(1)}, s32[1024,256]{1,0:T(8,128)}, u32[]{:S(2)}) copy-start(s32[1024,256]{1,0:T(8,128)} %param.13) | copy-start | bytes 3145732
  0.0 4.2 %copy-start.1 = (s32[256]{0:T(256)S(1)}, s32[256]{0:T(256)}, u32[]{:S(2)}) copy-start(s32[256]{0:T(256)} %constant.132.clone) | copy-start | bytes 3076
  0.0 4.2 %copy-start.2 = (s32[256]{0:T(256)S(1)}, s32[256]{0:T(256)}, u32[]{:S(2)}) copy-start(s32[256]{0:T(256)} %constant.131.clone) | copy-start | bytes 3076
  0.0 4.2 %copy-start.3 = (s32[256]{0:T(256)S(1)}, s32[256]{0:T(256)}, u32[]{:S(2)}) copy-start(s32[256]{0:T(256)} %constant.130.clone) | copy-start | bytes 3076
  0.0 4.2 %copy-start.4 = (s32[256]{0:T(256)S(1)}, s32[256]{0:T(256)}, u32[]{:S(2)}) copy-start(s32[256]{0:T(256)} %constant.129.clone) | copy-start | bytes 3076
  1.1 4.7 %collective-permute-start = (bf16[8,8832]{1,0:T(8,128)(2,1)S(1)}, bf16[8,8832]{1,0:T(8,128)(2,1)S(1)}, u32[]{:S(2)}, u32[]{:S(2)}) collective-permute-start(bf16[8,8832]{1,0:T(8,128)(2,1)S(1)} %get-tuple-element.51), channel_id=1, source_target_pairs={{0,64},{8,72},{16,80},{24,88},{32,96},{40,104},{48,112},{56,120},{... | collective-permute-start | bytes 423944 | tf_op jit(solution)/shard_map/ppermute | solution.py:40
  5.8 7.4 %collective-permute-start.5 = (bf16[8,8832]{1,0:T(8,128)(2,1)S(1)}, bf16[8,8832]{1,0:T(8,128)(2,1)S(1)}, u32[]{:S(2)}, u32[]{:S(2)}) collective-permute-start(bf16[8,8832]{1,0:T(8,128)(2,1)S(1)} %get-tuple-element.30), channel_id=1, source_target_pairs={{0,48},{8,56},{16,0},{24,8},{32,16},{40,24},{48,32},{56,40},{64,11... | collective-permute-start | bytes 423944 | tf_op jit(solution)/shard_map/ppermute | solution.py:40
  9.5 5.1 %collective-permute-start.4 = (bf16[8,8832]{1,0:T(8,128)(2,1)S(1)}, bf16[8,8832]{1,0:T(8,128)(2,1)S(1)}, u32[]{:S(2)}, u32[]{:S(2)}) collective-permute-start(bf16[8,8832]{1,0:T(8,128)(2,1)S(1)} %get-tuple-element.30), channel_id=1, source_target_pairs={{0,16},{8,24},{16,32},{24,40},{32,48},{40,56},{48,0},{56,8},{64,80... | collective-permute-start | bytes 423944 | tf_op jit(solution)/shard_map/ppermute | solution.py:40
  9.5 6.1 %collective-permute-start.3 = (bf16[8,8832]{1,0:T(8,128)(2,1)S(1)}, bf16[8,8832]{1,0:T(8,128)(2,1)S(1)}, u32[]{:S(2)}, u32[]{:S(2)}) collective-permute-start(bf16[8,8832]{1,0:T(8,128)(2,1)S(1)} %get-tuple-element.30), channel_id=1, source_target_pairs={{0,64},{8,72},{16,80},{24,88},{32,96},{40,104},{48,112},{56,120},{... | collective-permute-start | bytes 423944 | tf_op jit(solution)/shard_map/ppermute | solution.py:40
  10.4 8.0 %collective-permute-start.2 = (bf16[16,8832]{1,0:T(8,128)(2,1)S(1)}, bf16[16,8832]{1,0:T(8,128)(2,1)S(1)}, u32[]{:S(2)}, u32[]{:S(2)}) collective-permute-start(bf16[16,8832]{1,0:T(8,128)(2,1)S(1)} %pad_maximum_fusion), channel_id=1, source_target_pairs={{0,48},{8,56},{16,0},{24,8},{32,16},{40,24},{48,32},{56,40},{64,11... | collective-permute-start | bytes 847880 | tf_op jit(solution)/shard_map/ppermute | solution.py:40
  13.2 7.7 %collective-permute-start.1 = (bf16[16,8832]{1,0:T(8,128)(2,1)S(1)}, bf16[16,8832]{1,0:T(8,128)(2,1)S(1)}, u32[]{:S(2)}, u32[]{:S(2)}) collective-permute-start(bf16[16,8832]{1,0:T(8,128)(2,1)S(1)} %pad_maximum_fusion), channel_id=1, source_target_pairs={{0,16},{8,24},{16,32},{24,40},{32,48},{40,56},{48,0},{56,8},{64,80... | collective-permute-start | bytes 847880 | tf_op jit(solution)/shard_map/ppermute | solution.py:40
  14.7 11.9 %collective-permute-start.6 = (bf16[16,8832]{1,0:T(8,128)(2,1)S(1)}, bf16[16,8832]{1,0:T(8,128)(2,1)S(1)}, u32[]{:S(2)}, u32[]{:S(2)}) collective-permute-start(bf16[16,8832]{1,0:T(8,128)(2,1)S(1)} %pad_maximum_fusion.1), channel_id=1, source_target_pairs={{0,64},{8,72},{16,80},{24,88},{32,96},{40,104},{48,112},{56,120},{... | collective-permute-start | bytes 847880 | tf_op jit(solution)/shard_map/ppermute | solution.py:40
  15.7 17.2 %collective-permute-start.11 = (bf16[48,8832]{1,0:T(8,128)(2,1)S(1)}, bf16[48,8832]{1,0:T(8,128)(2,1)S(1)}, u32[]{:S(2)}, u32[]{:S(2)}) collective-permute-start(bf16[48,8832]{1,0:T(8,128)(2,1)S(1)} %constant_dynamic-update-slice_fusion.refs_0_), channel_id=1, source_target_pairs={{0,8},{8,0},{16,24},{24,16},{32,40},{40,32},{48,56},{56,48},{64,72... | collective-permute-start | bytes 2543624 | tf_op jit(solution)/shard_map/ppermute | solution.py:40
  18.4 7.0 %collective-permute-start.7 = (bf16[8,8832]{1,0:T(8,128)(2,1)S(1)}, bf16[8,8832]{1,0:T(8,128)(2,1)S(1)}, u32[]{:S(2)}, u32[]{:S(2)}) collective-permute-start(bf16[8,8832]{1,0:T(8,128)(2,1)S(1)} %collective-permute-done.4), channel_id=1, source_target_pairs={{0,16},{8,24},{16,32},{24,40},{32,48},{40,56},{48,0},{56,8},{64,80... | collective-permute-start | bytes 423944 | tf_op jit(solution)/shard_map/ppermute | solution.py:40
  21.0 8.8 %collective-permute-start.10 = (bf16[8,8832]{1,0:T(8,128)(2,1)S(1)}, bf16[8,8832]{1,0:T(8,128)(2,1)S(1)}, u32[]{:S(2)}, u32[]{:S(2)}) collective-permute-start(bf16[8,8832]{1,0:T(8,128)(2,1)S(1)} %slice.15), channel_id=1, source_target_pairs={{0,48},{8,56},{16,0},{24,8},{32,16},{40,24},{48,32},{56,40},{64,11... | collective-permute-start | bytes 423944 | tf_op jit(solution)/shard_map/ppermute | solution.py:40
  21.3 8.4 %collective-permute-start.9 = (bf16[8,8832]{1,0:T(8,128)(2,1)S(1)}, bf16[8,8832]{1,0:T(8,128)(2,1)S(1)}, u32[]{:S(2)}, u32[]{:S(2)}) collective-permute-start(bf16[8,8832]{1,0:T(8,128)(2,1)S(1)} %slice.14), channel_id=1, source_target_pairs={{0,16},{8,24},{16,32},{24,40},{32,48},{40,56},{48,0},{56,8},{64,80... | collective-permute-start | bytes 423944 | tf_op jit(solution)/shard_map/ppermute | solution.py:40
  25.5 4.2 %collective-permute-start.8 = (bf16[8,8832]{1,0:T(8,128)(2,1)S(1)}, bf16[8,8832]{1,0:T(8,128)(2,1)S(1)}, u32[]{:S(2)}, u32[]{:S(2)}) collective-permute-start(bf16[8,8832]{1,0:T(8,128)(2,1)S(1)} %collective-permute-done.7), channel_id=1, source_target_pairs={{0,64},{8,72},{16,80},{24,88},{32,96},{40,104},{48,112},{56,120},{... | collective-permute-start | bytes 423944 | tf_op jit(solution)/shard_map/ppermute | solution.py:40
  26.6 7.8 %collective-permute-start.12 = (bf16[48,8832]{1,0:T(8,128)(2,1)S(1)}, bf16[48,8832]{1,0:T(8,128)(2,1)S(1)}, u32[]{:S(2)}, u32[]{:S(2)}) collective-permute-start(bf16[48,8832]{1,0:T(8,128)(2,1)S(1)} %constant_dynamic-update-slice_fusion.5.refs_1_), channel_id=1, source_target_pairs={{0,8},{8,0},{16,24},{24,16},{32,40},{40,32},{48,56},{56,48},{64,72... | collective-permute-start | bytes 2543624 | tf_op jit(solution)/shard_map/ppermute | solution.py:40
  29.8 4.7 %collective-permute-start.13 = (bf16[32,8832]{1,0:T(8,128)(2,1)S(1)}, bf16[32,8832]{1,0:T(8,128)(2,1)S(1)}, u32[]{:S(2)}, u32[]{:S(2)}) collective-permute-start(bf16[32,8832]{1,0:T(8,128)(2,1)S(1)} %constant_dynamic-update-slice_fusion.8.refs_2_), channel_id=1, source_target_pairs={{0,8},{8,0},{16,24},{24,16},{32,40},{40,32},{48,56},{56,48},{64,72... | collective-permute-start | bytes 1695752 | tf_op jit(solution)/shard_map/ppermute | solution.py:40
  65.8 13.0 %all-to-all-start.1 = ((bf16[8,256,128]{2,1,0:T(8,128)(2,1)}), bf16[8,256,128]{2,1,0:T(8,128)(2,1)S(1)}, u32[]{:S(2)}, u32[]{:S(2)}) async-start(bf16[8,256,128]{2,1,0:T(8,128)(2,1)} %shard_map.110), calls=%async_computation.1 | async-start | bytes 1048576 | tf_op jit(solution)/shard_map/all_to_all | solution.py:270
  85.9 9.0 %collective-permute-start.14 = (bf16[4480,256]{1,0:T(8,128)(2,1)}, bf16[4480,256]{1,0:T(8,128)(2,1)}, u32[]{:S(2)}, u32[]{:S(2)}) collective-permute-start(bf16[4480,256]{1,0:T(8,128)(2,1)} %shard_map.112), channel_id=1, source_target_pairs={{0,8},{8,0},{16,24},{24,16},{32,40},{40,32},{48,56},{56,48},{64,72... | collective-permute-start | bytes 6881288 | tf_op jit(solution)/shard_map/ppermute | solution.py:283
  97.4 17.4 %collective-permute-start.19 = (bf16[4,552,128]{2,1,0:T(8,128)(2,1)S(1)}, bf16[4,552,128]{2,1,0:T(8,128)(2,1)S(1)}, u32[]{:S(2)}, u32[]{:S(2)}) collective-permute-start(bf16[4,552,128]{2,1,0:T(8,128)(2,1)S(1)} %get-tuple-element.44), channel_id=1, source_target_pairs={{0,64},{8,72},{16,80},{24,88},{32,96},{40,104},{48,112},{56,120},{... | collective-permute-start | bytes 1695752 | tf_op jit(solution)/shard_map/ppermute | solution.py:299
  98.4 15.3 %collective-permute-start.15 = (bf16[2,552,128]{2,1,0:T(8,128)(2,1)S(1)}, bf16[2,552,128]{2,1,0:T(8,128)(2,1)S(1)}, u32[]{:S(2)}, u32[]{:S(2)}) collective-permute-start(bf16[2,552,128]{2,1,0:T(8,128)(2,1)S(1)} %get-tuple-element.38), channel_id=1, source_target_pairs={{0,16},{8,24},{16,32},{24,40},{32,48},{40,56},{48,0},{56,8},{64,80... | collective-permute-start | bytes 847880 | tf_op jit(solution)/shard_map/ppermute | solution.py:300
  98.4 15.3 %collective-permute-start.16 = (bf16[2,552,128]{2,1,0:T(8,128)(2,1)S(1)}, bf16[2,552,128]{2,1,0:T(8,128)(2,1)S(1)}, u32[]{:S(2)}, u32[]{:S(2)}) collective-permute-start(bf16[2,552,128]{2,1,0:T(8,128)(2,1)S(1)} %get-tuple-element.39), channel_id=1, source_target_pairs={{0,32},{8,40},{16,48},{24,56},{32,0},{40,8},{48,16},{56,24},{64,96... | collective-permute-start | bytes 847880 | tf_op jit(solution)/shard_map/ppermute | solution.py:300
  99.6 14.5 %collective-permute-start.17 = (bf16[2,552,128]{2,1,0:T(8,128)(2,1)S(1)}, bf16[2,552,128]{2,1,0:T(8,128)(2,1)S(1)}, u32[]{:S(2)}, u32[]{:S(2)}) collective-permute-start(bf16[2,552,128]{2,1,0:T(8,128)(2,1)S(1)} %get-tuple-element.40), channel_id=1, source_target_pairs={{0,48},{8,56},{16,0},{24,8},{32,16},{40,24},{48,32},{56,40},{64,11... | collective-permute-start | bytes 847880 | tf_op jit(solution)/shard_map/ppermute | solution.py:300
  114.2 4.7 %collective-permute-start.18 = (bf16[552,128]{1,0:T(8,128)(2,1)S(1)}, bf16[552,128]{1,0:T(8,128)(2,1)S(1)}, u32[]{:S(2)}, u32[]{:S(2)}) collective-permute-start(bf16[552,128]{1,0:T(8,128)(2,1)S(1)} %get-tuple-element.42), channel_id=1, source_target_pairs={{0,64},{8,72},{16,80},{24,88},{32,96},{40,104},{48,112},{56,120},{... | collective-permute-start | bytes 423944 | tf_op jit(solution)/shard_map/ppermute | solution.py:299
  114.9 5.2 %collective-permute-start.20 = (bf16[552,128]{1,0:T(8,128)(2,1)S(1)}, bf16[552,128]{1,0:T(8,128)(2,1)S(1)}, u32[]{:S(2)}, u32[]{:S(2)}) collective-permute-start(bf16[552,128]{1,0:T(8,128)(2,1)S(1)} %get-tuple-element.46), channel_id=1, source_target_pairs={{0,16},{8,24},{16,32},{24,40},{32,48},{40,56},{48,0},{56,8},{64,80... | collective-permute-start | bytes 423944 | tf_op jit(solution)/shard_map/ppermute | solution.py:300
  115.9 8.4 %collective-permute-start.21 = (bf16[552,128]{1,0:T(8,128)(2,1)S(1)}, bf16[552,128]{1,0:T(8,128)(2,1)S(1)}, u32[]{:S(2)}, u32[]{:S(2)}) collective-permute-start(bf16[552,128]{1,0:T(8,128)(2,1)S(1)} %get-tuple-element.47), channel_id=1, source_target_pairs={{0,32},{8,40},{16,48},{24,56},{32,0},{40,8},{48,16},{56,24},{64,96... | collective-permute-start | bytes 423944 | tf_op jit(solution)/shard_map/ppermute | solution.py:300
  118.8 5.4 %collective-permute-start.22 = (bf16[552,128]{1,0:T(8,128)(2,1)S(1)}, bf16[552,128]{1,0:T(8,128)(2,1)S(1)}, u32[]{:S(2)}, u32[]{:S(2)}) collective-permute-start(bf16[552,128]{1,0:T(8,128)(2,1)S(1)} %get-tuple-element.48), channel_id=1, source_target_pairs={{0,48},{8,56},{16,0},{24,8},{32,16},{40,24},{48,32},{56,40},{64,11... | collective-permute-start | bytes 423944 | tf_op jit(solution)/shard_map/ppermute | solution.py:300

commit v6 on v5

--- a/solution.py
+++ b/solution.py
@@ -44,10 +44,11 @@
     low_x = move(low, 1, 0, 0)
     high, low_x = lax.optimization_barrier((high, low_x))
     high_x = move(high, 1, 0, 0)
+    pair = stack(low, low_x)
+    high, pair = lax.optimization_barrier((high, pair))
+    pair_1, pair_3 = move(pair, 0, 1, 0), move(pair, 0, 3, 0)
     high_1, high_3 = move(high, 0, 1, 0), move(high, 0, 3, 0)
     high_2 = move(high_1, 0, 1, 0)
-    pair = stack(low, low_x)
-    pair_1, pair_3 = move(pair, 0, 1, 0), move(pair, 0, 3, 0)
     high_z = stack(high_1, high_3)
     high_zx = move(high_z, 1, 0, 0)
     high_2x = move(high_2, 1, 0, 0)
@@ -302,6 +303,7 @@
     *to_z, high = call(
         high_kernel, (*[one(BF16)] * 3, one(F32)), small, (stay_high, got_x)
     )
+    got_z, to_z = lax.optimization_barrier((got_z, to_z))
     to_x, low = call(low_kernel, (one(BF16), one(F32)), small, (stay_low, *got_z))
     parts = low, go_x(to_x), high, *go_z(to_z)
     send = call(

time: 153 us -> 153 us (level)
    ppermute x6, waiting for transfers between devices: 18.4 us -> 7.44 us  [local(): lax.ppermute(x, 'line', along(0, i + 1, 0))]
    ppermute x2, waiting for transfers between devices: 0.01 us -> 10.8 us  [local(): go_x = lambda x: lax.ppermute(x, 'line', along(1, 0, 0))]
  transfers between devices with their start and end apart: 24 -> 24, of which waited for: 11 -> 12; matrix products, arithmetic and copies ran while one was open for 3% -> 3% of each run, Pallas kernels for 4% -> 4%
where the time goes in v6:
time: 153 us; the launch traced here: 151 us
  blocking collectives  45 us (29%)
  waiting for transfers between devices  38.9 us (25%)
  starting transfers between devices  33 us (22%)
  Pallas kernels  28.3 us (18%)
  local copies, waits for them, and re-layouts  3.98 us (3%)
    all_to_all x1, blocking collectives, local(): lax.all_to_all(send.reshape(DEVICES, SLOTS, scen), ('line', 'bus'), 0, 0,...  23.6 us
    all_to_all x1, blocking collectives, local(): lax.all_to_all(partial_flows.reshape(BUSES_AT, rows, scen), 'bus', 0, 0,...  21.4 us
    pallas_call x8, Pallas kernels, call(): pl.pallas_call(kernel, out_shape=out, in_specs=[pl.BlockSpec(memory_space...  19.6 us
    ppermute x14, starting transfers between devices, gather(): move = lambda x, *to: lax.ppermute(x, 'line', along(*to))  18 us
    ppermute x14, waiting for transfers between devices, gather(): move = lambda x, *to: lax.ppermute(x, 'line', along(*to))  11.1 us
    ppermute x2, waiting for transfers between devices, local(): go_x = lambda x: lax.ppermute(x, 'line', along(1, 0, 0))  10.8 us
    all_to_all x1, waiting for transfers between devices, local(): dual = lax.all_to_all(dual, 'bus', 0, 0, tiled=True)  9.49 us
    pallas_call x1, Pallas kernels, local(): pl.pallas_call(flows_kernel, out_shape=shape((lines, scen), F32), grid=(l...  8.72 us
  transfers between devices with their start and end apart: 24, of which 12 were waited for; matrix products, arithmetic and copies ran while one was open for 3% of the time, Pallas kernels for 4%

profile of v6, /device:TPU:3, one launch (start us, length us, event | category | flops | bytes accessed | tf_op | source)
XLA Modules:
  0.0 150.7 jit_solution(5217548976490170699)
XLA Ops:
  0.0 1.1 fusion.12
  1.3 1.0 constant_dynamic-update-slice_fusion.4
  2.3 0.8 multiply_add_fusion
  3.1 0.3 convert_reduce_fusion
  3.4 0.8 dynamic-slice_bitcast_fusion
  4.2 0.8 dynamic-slice_bitcast_fusion.2.sign
  5.0 0.1 copy.14
  5.1 0.6 collective-permute-done
  5.8 3.8 %collective-permute-start.5 = (bf16[8,8832]{1,0:T(8,128)(2,1)S(1)}, bf16[8,8832]{1,0:T(8,128)(2,1)S(1)}, u32[]{:S(2)}, u32[]{:S(2)}) collective-permute-start(bf16[8,8832]{1,0:T(8,128)(2,1)S(1)} %get-tuple-element.40), channel_id=1, source_target_pairs={{0,48},{8,56},{16,0},{24,8},{32,16},{40,24},{48,32},{56,40},{64,11... | collective-permute-start | bytes 423944 | tf_op jit(solution)/shard_map/ppermute | solution.py:40
  9.6 0.8 collective-permute-start.3
  10.4 2.7 %collective-permute-start.2 = (bf16[16,8832]{1,0:T(8,128)(2,1)S(1)}, bf16[16,8832]{1,0:T(8,128)(2,1)S(1)}, u32[]{:S(2)}, u32[]{:S(2)}) collective-permute-start(bf16[16,8832]{1,0:T(8,128)(2,1)S(1)} %pad_maximum_fusion), channel_id=1, source_target_pairs={{0,48},{8,56},{16,0},{24,8},{32,16},{40,24},{48,32},{56,40},{64,11... | collective-permute-start | bytes 847880 | tf_op jit(solution)/shard_map/ppermute | solution.py:40
  13.1 1.7 %collective-permute-done.4 = bf16[8,8832]{1,0:T(8,128)(2,1)S(1)} collective-permute-done((bf16[8,8832]{1,0:T(8,128)(2,1)S(1)}, bf16[8,8832]{1,0:T(8,128)(2,1)S(1)}, u32[]{:S(2)}, u32[]{:S(2)}) %collective-permute-start.4) | collective-permute-done | bytes 141344 | tf_op jit(solution)/shard_map/ppermute | solution.py:40
  14.8 0.9 collective-permute-start.6
  15.7 2.8 %collective-permute-start.11 = (bf16[48,8832]{1,0:T(8,128)(2,1)S(1)}, bf16[48,8832]{1,0:T(8,128)(2,1)S(1)}, u32[]{:S(2)}, u32[]{:S(2)}) collective-permute-start(bf16[48,8832]{1,0:T(8,128)(2,1)S(1)} %constant_dynamic-update-slice_fusion.refs_0_), channel_id=1, source_target_pairs={{0,8},{8,0},{16,24},{24,16},{32,40},{40,32},{48,56},{56,48},{64,72... | collective-permute-start | bytes 2543624 | tf_op jit(solution)/shard_map/ppermute | solution.py:40
  18.5 2.5 %collective-permute-done.1 = bf16[16,8832]{1,0:T(8,128)(2,1)S(1)} collective-permute-done((bf16[16,8832]{1,0:T(8,128)(2,1)S(1)}, bf16[16,8832]{1,0:T(8,128)(2,1)S(1)}, u32[]{:S(2)}, u32[]{:S(2)}) %collective-permute-start.1) | collective-permute-done | bytes 282656 | tf_op jit(solution)/shard_map/ppermute | solution.py:40
  21.2 0.2 collective-permute-start.10
  21.4 1.3 collective-permute-start.9
  22.7 2.8 %collective-permute-done.7 = bf16[8,8832]{1,0:T(8,128)(2,1)S(1)} collective-permute-done((bf16[8,8832]{1,0:T(8,128)(2,1)S(1)}, bf16[8,8832]{1,0:T(8,128)(2,1)S(1)}, u32[]{:S(2)}, u32[]{:S(2)}) %collective-permute-start.7) | collective-permute-done | bytes 141344 | tf_op jit(solution)/shard_map/ppermute | solution.py:40
  25.6 1.0 collective-permute-start.8
  26.6 1.4 collective-permute-start.12
  28.0 1.8 %collective-permute-done.8 = bf16[8,8832]{1,0:T(8,128)(2,1)S(1)} collective-permute-done((bf16[8,8832]{1,0:T(8,128)(2,1)S(1)}, bf16[8,8832]{1,0:T(8,128)(2,1)S(1)}, u32[]{:S(2)}, u32[]{:S(2)}) %collective-permute-start.8) | collective-permute-done | bytes 141344 | tf_op jit(solution)/shard_map/ppermute | solution.py:40
  29.9 3.1 %collective-permute-start.13 = (bf16[32,8832]{1,0:T(8,128)(2,1)S(1)}, bf16[32,8832]{1,0:T(8,128)(2,1)S(1)}, u32[]{:S(2)}, u32[]{:S(2)}) collective-permute-start(bf16[32,8832]{1,0:T(8,128)(2,1)S(1)} %constant_dynamic-update-slice_fusion.8.refs_2_), channel_id=1, source_target_pairs={{0,8},{8,0},{16,24},{24,16},{32,40},{40,32},{48,56},{56,48},{64,72... | collective-permute-start | bytes 1695752 | tf_op jit(solution)/shard_map/ppermute | solution.py:40
  33.0 1.6 %collective-permute-done.13.refs_5_ = bf16[32,8832]{1,0:T(8,128)(2,1)S(1)} collective-permute-done((bf16[32,8832]{1,0:T(8,128)(2,1)S(1)}, bf16[32,8832]{1,0:T(8,128)(2,1)S(1)}, u32[]{:S(2)}, u32[]{:S(2)}) %collective-permute-start.13) | collective-permute-done | bytes 565280 | tf_op jit(solution)/shard_map/ppermute | solution.py:40
  34.6 8.7 %shard_map.109 = f32[1024,256]{1,0:T(8,128)S(1)} custom-call(bf16[1024,8832]{1,0:T(8,128)(2,1)} %ptdf.5, bf16[48,8832]{1,0:T(8,128)(2,1)S(1)} %constant_dynamic-update-slice_fusion.refs_0_, bf16[48,8832]{1,0:T(8,128)(2,1)S(1)} %constant_dynamic-update-slice_fusion.5.refs_1_, bf16[32,8832]{1,0:T(8,128)(2,1)S(1)} %constant_dynamic-update-slice_fusion.8.refs_2_, ...), custom_call_target="tpu_custom_call" | custom-call | flops 4630511616 | bytes 18087936 | tf_op jit(solution)/shard_map/pallas_call | solution.py:252
  43.3 21.4 %all_to_all.15.parts = f32[8,128,256]{2,1,0:T(8,128)S(1)} all-to-all(f32[8,128,256]{2,1,0:T(8,128)S(1)} %bitcast.17), channel_id=1, replica_groups=mesh['line'=16,'bus'=8] {'bus'}, dimensions={0} | all-to-all | bytes 2097152 | tf_op jit(solution)/shard_map/all_to_all | solution.py:264
  64.7 1.1 shard_map.110
  65.8 3.5 %all-to-all-start.1 = ((bf16[8,256,128]{2,1,0:T(8,128)(2,1)}), bf16[8,256,128]{2,1,0:T(8,128)(2,1)S(1)}, u32[]{:S(2)}, u32[]{:S(2)}) async-start(bf16[8,256,128]{2,1,0:T(8,128)(2,1)} %shard_map.110), calls=%async_computation.1 | async-start | bytes 1048576 | tf_op jit(solution)/shard_map/all_to_all | solution.py:271
  69.3 9.5 %all-to-all-done.1.dual = bf16[8,256,128]{2,1,0:T(8,128)(2,1)S(1)} async-done(((bf16[8,256,128]{2,1,0:T(8,128)(2,1)}), bf16[8,256,128]{2,1,0:T(8,128)(2,1)S(1)}, u32[]{:S(2)}, u32[]{:S(2)}) %all-to-all-start.1) | async-done | bytes 524320 | tf_op jit(solution)/shard_map/all_to_all | solution.py:271
  78.8 7.0 %shard_map.112 = bf16[4480,256]{1,0:T(8,128)(2,1)} custom-call(s32[1]{0:T(128)} %bitcast.11.start, bf16[1024,8832]{1,0:T(8,128)(2,1)} %ptdf.5, bf16[8,256,128]{2,1,0:T(8,128)(2,1)S(1)} %all-to-all-done.1.dual), custom_call_target="tpu_custom_call" | custom-call | flops 2315255808 | bytes 9043968 | tf_op jit(solution)/shard_map/pallas_call | solution.py:97
  85.9 3.3 %collective-permute-start.14 = (bf16[4480,256]{1,0:T(8,128)(2,1)}, bf16[4480,256]{1,0:T(8,128)(2,1)}, u32[]{:S(2)}, u32[]{:S(2)}) collective-permute-start(bf16[4480,256]{1,0:T(8,128)(2,1)} %shard_map.112), channel_id=1, source_target_pairs={{0,8},{8,0},{16,24},{24,16},{32,40},{40,32},{48,56},{56,48},{64,72... | collective-permute-start | bytes 6881288 | tf_op jit(solution)/shard_map/ppermute | solution.py:284
  89.2 5.7 %shard_map.111.keep = f32[4480,256]{1,0:T(8,128)S(1)} custom-call(s32[1]{0:T(128)} %bitcast.9.start, bf16[1024,8832]{1,0:T(8,128)(2,1)} %ptdf.5, bf16[8,256,128]{2,1,0:T(8,128)(2,1)S(1)} %all-to-all-done.1.dual), custom_call_target="tpu_custom_call" | custom-call | flops 2315255808 | bytes 9043968 | tf_op jit(solution)/shard_map/pallas_call | solution.py:97
  94.9 2.5 %shard_map.113 = (bf16[4,552,128]{2,1,0:T(8,128)(2,1)S(1)}, bf16[2,552,128]{2,1,0:T(8,128)(2,1)S(1)}, bf16[2,552,128]{2,1,0:T(8,128)(2,1)S(1)}, bf16[2,552,128]{...) custom-call(s32[3]{0:T(128)S(1)} %pad_add_fusion.1.at, f32[4480,256]{1,0:T(8,128)S(1)} %shard_map.111.keep, ...), custom_call_target="tpu_custom_call" | custom-call | flops 1146880 | bytes 9175040 | tf_op jit(solution)/shard_map/pallas_call | solution.py:97
  97.4 1.0 collective-permute-start.18
  98.4 1.2 collective-permute-start.16
  99.6 1.5 collective-permute-start.17
  101.1 10.8 %collective-permute-done.18.got = bf16[4,552,128]{2,1,0:T(8,128)(2,1)S(1)} collective-permute-done((bf16[4,552,128]{2,1,0:T(8,128)(2,1)S(1)}, bf16[4,552,128]{2,1,0:T(8,128)(2,1)S(1)}, u32[]{:S(2)}, u32[]{:S(2)}) %collective-permute-start.18) | collective-permute-done | bytes 565280 | tf_op jit(solution)/shard_map/ppermute | solution.py:300
  111.9 0.1 shard_map.114
  112.0 1.7 %collective-permute-done.15.got_1 = bf16[2,552,128]{2,1,0:T(8,128)(2,1)S(1)} collective-permute-done((bf16[2,552,128]{2,1,0:T(8,128)(2,1)S(1)}, bf16[2,552,128]{2,1,0:T(8,128)(2,1)S(1)}, u32[]{:S(2)}, u32[]{:S(2)}) %collective-permute-start.15) | collective-permute-done | bytes 282656 | tf_op jit(solution)/shard_map/ppermute | solution.py:301
  113.7 0.3 collective-permute-done.17.got_3
  114.0 0.1 shard_map.115
  114.2 0.6 collective-permute-start.19
  114.8 0.9 collective-permute-start.20
  115.7 3.0 %collective-permute-start.21 = (bf16[552,128]{1,0:T(8,128)(2,1)S(1)}, bf16[552,128]{1,0:T(8,128)(2,1)S(1)}, u32[]{:S(2)}, u32[]{:S(2)}) collective-permute-start(bf16[552,128]{1,0:T(8,128)(2,1)S(1)} %get-tuple-element.63), channel_id=1, source_target_pairs={{0,32},{8,40},{16,48},{24,56},{32,0},{40,8},{48,16},{56,24},{64,96... | collective-permute-start | bytes 423944 | tf_op jit(solution)/shard_map/ppermute | solution.py:301
  118.7 1.3 collective-permute-done.20.got_1
  120.0 4.1 %collective-permute-done.21.got_2 = bf16[552,128]{1,0:T(8,128)(2,1)S(1)} collective-permute-done((bf16[552,128]{1,0:T(8,128)(2,1)S(1)}, bf16[552,128]{1,0:T(8,128)(2,1)S(1)}, u32[]{:S(2)}, u32[]{:S(2)}) %collective-permute-start.21) | collective-permute-done | bytes 141344 | tf_op jit(solution)/shard_map/ppermute | solution.py:301
  124.1 1.8 %shard_map.116 = f32[1024,256]{1,0:T(8,128)S(1)} custom-call(s32[4,552]{1,0:T(4,128)S(1)} %pad_add_fusion.plan, f32[552,128]{1,0:T(8,128)S(1)} %get-tuple-element.59.low, bf16[552,128]{1,0:T(8,128)(2,1)S(1)} %collective-permute-done.19.got_low, f32[552,128]{1,0:T(8,128)S(1)} %get-tuple-element.61.high, bf16[552,128]{1,0:T(8,128)(2,1)S(1)} %collective-permute-done.20.got_1, ...), custom_call_target="tpu_custom_call" | custom-call | flops 868220928 | bytes 2260992 | tf_op jit(solution)/shard_map/pallas_call | solution.py:97
  125.9 23.6 %all_to_all.16.terms = f32[128,8,256]{2,1,0:T(8,128)S(1)} all-to-all(f32[128,8,256]{2,1,0:T(8,128)S(1)} %bitcast.18), channel_id=1, replica_groups=mesh['line'=16,'bus'=8] {'line','bus'}, dimensions={0} | all-to-all | bytes 2097152 | tf_op jit(solution)/shard_map/all_to_all | solution.py:315
  149.5 1.3 shard_map.117
  (52 shorter events, 0.6 us)
Async XLA Ops:
  0.0 3.4 %copy-start = (s32[1024,256]{1,0:T(8,128)S(1)}, s32[1024,256]{1,0:T(8,128)}, u32[]{:S(2)}) copy-start(s32[1024,256]{1,0:T(8,128)} %param.13) | copy-start | bytes 3145732
  0.0 4.2 %copy-start.1 = (s32[256]{0:T(256)S(1)}, s32[256]{0:T(256)}, u32[]{:S(2)}) copy-start(s32[256]{0:T(256)} %constant.132.clone) | copy-start | bytes 3076
  0.0 4.2 %copy-start.2 = (s32[256]{0:T(256)S(1)}, s32[256]{0:T(256)}, u32[]{:S(2)}) copy-start(s32[256]{0:T(256)} %constant.131.clone) | copy-start | bytes 3076
  0.0 4.2 %copy-start.3 = (s32[256]{0:T(256)S(1)}, s32[256]{0:T(256)}, u32[]{:S(2)}) copy-start(s32[256]{0:T(256)} %constant.130.clone) | copy-start | bytes 3076
  0.0 4.2 %copy-start.4 = (s32[256]{0:T(256)S(1)}, s32[256]{0:T(256)}, u32[]{:S(2)}) copy-start(s32[256]{0:T(256)} %constant.129.clone) | copy-start | bytes 3076
  1.1 4.7 %collective-permute-start = (bf16[8,8832]{1,0:T(8,128)(2,1)S(1)}, bf16[8,8832]{1,0:T(8,128)(2,1)S(1)}, u32[]{:S(2)}, u32[]{:S(2)}) collective-permute-start(bf16[8,8832]{1,0:T(8,128)(2,1)S(1)} %get-tuple-element.67), channel_id=1, source_target_pairs={{0,64},{8,72},{16,80},{24,88},{32,96},{40,104},{48,112},{56,120},{... | collective-permute-start | bytes 423944 | tf_op jit(solution)/shard_map/ppermute | solution.py:40
  5.8 7.3 %collective-permute-start.5 = (bf16[8,8832]{1,0:T(8,128)(2,1)S(1)}, bf16[8,8832]{1,0:T(8,128)(2,1)S(1)}, u32[]{:S(2)}, u32[]{:S(2)}) collective-permute-start(bf16[8,8832]{1,0:T(8,128)(2,1)S(1)} %get-tuple-element.40), channel_id=1, source_target_pairs={{0,48},{8,56},{16,0},{24,8},{32,16},{40,24},{48,32},{56,40},{64,11... | collective-permute-start | bytes 423944 | tf_op jit(solution)/shard_map/ppermute | solution.py:40
  9.6 5.1 %collective-permute-start.4 = (bf16[8,8832]{1,0:T(8,128)(2,1)S(1)}, bf16[8,8832]{1,0:T(8,128)(2,1)S(1)}, u32[]{:S(2)}, u32[]{:S(2)}) collective-permute-start(bf16[8,8832]{1,0:T(8,128)(2,1)S(1)} %get-tuple-element.40), channel_id=1, source_target_pairs={{0,16},{8,24},{16,32},{24,40},{32,48},{40,56},{48,0},{56,8},{64,80... | collective-permute-start | bytes 423944 | tf_op jit(solution)/shard_map/ppermute | solution.py:40
  9.6 6.0 %collective-permute-start.3 = (bf16[8,8832]{1,0:T(8,128)(2,1)S(1)}, bf16[8,8832]{1,0:T(8,128)(2,1)S(1)}, u32[]{:S(2)}, u32[]{:S(2)}) collective-permute-start(bf16[8,8832]{1,0:T(8,128)(2,1)S(1)} %get-tuple-element.40), channel_id=1, source_target_pairs={{0,64},{8,72},{16,80},{24,88},{32,96},{40,104},{48,112},{56,120},{... | collective-permute-start | bytes 423944 | tf_op jit(solution)/shard_map/ppermute | solution.py:40
  10.4 8.1 %collective-permute-start.2 = (bf16[16,8832]{1,0:T(8,128)(2,1)S(1)}, bf16[16,8832]{1,0:T(8,128)(2,1)S(1)}, u32[]{:S(2)}, u32[]{:S(2)}) collective-permute-start(bf16[16,8832]{1,0:T(8,128)(2,1)S(1)} %pad_maximum_fusion), channel_id=1, source_target_pairs={{0,48},{8,56},{16,0},{24,8},{32,16},{40,24},{48,32},{56,40},{64,11... | collective-permute-start | bytes 847880 | tf_op jit(solution)/shard_map/ppermute | solution.py:40
  13.1 8.0 %collective-permute-start.1 = (bf16[16,8832]{1,0:T(8,128)(2,1)S(1)}, bf16[16,8832]{1,0:T(8,128)(2,1)S(1)}, u32[]{:S(2)}, u32[]{:S(2)}) collective-permute-start(bf16[16,8832]{1,0:T(8,128)(2,1)S(1)} %pad_maximum_fusion), channel_id=1, source_target_pairs={{0,16},{8,24},{16,32},{24,40},{32,48},{40,56},{48,0},{56,8},{64,80... | collective-permute-start | bytes 847880 | tf_op jit(solution)/shard_map/ppermute | solution.py:40
  14.8 11.8 %collective-permute-start.6 = (bf16[16,8832]{1,0:T(8,128)(2,1)S(1)}, bf16[16,8832]{1,0:T(8,128)(2,1)S(1)}, u32[]{:S(2)}, u32[]{:S(2)}) collective-permute-start(bf16[16,8832]{1,0:T(8,128)(2,1)S(1)} %pad_maximum_fusion.1), channel_id=1, source_target_pairs={{0,64},{8,72},{16,80},{24,88},{32,96},{40,104},{48,112},{56,120},{... | collective-permute-start | bytes 847880 | tf_op jit(solution)/shard_map/ppermute | solution.py:40
  15.7 17.2 %collective-permute-start.11 = (bf16[48,8832]{1,0:T(8,128)(2,1)S(1)}, bf16[48,8832]{1,0:T(8,128)(2,1)S(1)}, u32[]{:S(2)}, u32[]{:S(2)}) collective-permute-start(bf16[48,8832]{1,0:T(8,128)(2,1)S(1)} %constant_dynamic-update-slice_fusion.refs_0_), channel_id=1, source_target_pairs={{0,8},{8,0},{16,24},{24,16},{32,40},{40,32},{48,56},{56,48},{64,72... | collective-permute-start | bytes 2543624 | tf_op jit(solution)/shard_map/ppermute | solution.py:40
  18.5 7.0 %collective-permute-start.7 = (bf16[8,8832]{1,0:T(8,128)(2,1)S(1)}, bf16[8,8832]{1,0:T(8,128)(2,1)S(1)}, u32[]{:S(2)}, u32[]{:S(2)}) collective-permute-start(bf16[8,8832]{1,0:T(8,128)(2,1)S(1)} %collective-permute-done.4), channel_id=1, source_target_pairs={{0,16},{8,24},{16,32},{24,40},{32,48},{40,56},{48,0},{56,8},{64,80... | collective-permute-start | bytes 423944 | tf_op jit(solution)/shard_map/ppermute | solution.py:40
  21.2 8.7 %collective-permute-start.10 = (bf16[8,8832]{1,0:T(8,128)(2,1)S(1)}, bf16[8,8832]{1,0:T(8,128)(2,1)S(1)}, u32[]{:S(2)}, u32[]{:S(2)}) collective-permute-start(bf16[8,8832]{1,0:T(8,128)(2,1)S(1)} %slice.15), channel_id=1, source_target_pairs={{0,48},{8,56},{16,0},{24,8},{32,16},{40,24},{48,32},{56,40},{64,11... | collective-permute-start | bytes 423944 | tf_op jit(solution)/shard_map/ppermute | solution.py:40
  21.4 8.4 %collective-permute-start.9 = (bf16[8,8832]{1,0:T(8,128)(2,1)S(1)}, bf16[8,8832]{1,0:T(8,128)(2,1)S(1)}, u32[]{:S(2)}, u32[]{:S(2)}) collective-permute-start(bf16[8,8832]{1,0:T(8,128)(2,1)S(1)} %slice.14), channel_id=1, source_target_pairs={{0,16},{8,24},{16,32},{24,40},{32,48},{40,56},{48,0},{56,8},{64,80... | collective-permute-start | bytes 423944 | tf_op jit(solution)/shard_map/ppermute | solution.py:40
  25.6 4.2 %collective-permute-start.8 = (bf16[8,8832]{1,0:T(8,128)(2,1)S(1)}, bf16[8,8832]{1,0:T(8,128)(2,1)S(1)}, u32[]{:S(2)}, u32[]{:S(2)}) collective-permute-start(bf16[8,8832]{1,0:T(8,128)(2,1)S(1)} %collective-permute-done.7), channel_id=1, source_target_pairs={{0,64},{8,72},{16,80},{24,88},{32,96},{40,104},{48,112},{56,120},{... | collective-permute-start | bytes 423944 | tf_op jit(solution)/shard_map/ppermute | solution.py:40
  26.6 7.9 %collective-permute-start.12 = (bf16[48,8832]{1,0:T(8,128)(2,1)S(1)}, bf16[48,8832]{1,0:T(8,128)(2,1)S(1)}, u32[]{:S(2)}, u32[]{:S(2)}) collective-permute-start(bf16[48,8832]{1,0:T(8,128)(2,1)S(1)} %constant_dynamic-update-slice_fusion.5.refs_1_), channel_id=1, source_target_pairs={{0,8},{8,0},{16,24},{24,16},{32,40},{40,32},{48,56},{56,48},{64,72... | collective-permute-start | bytes 2543624 | tf_op jit(solution)/shard_map/ppermute | solution.py:40
  29.9 4.7 %collective-permute-start.13 = (bf16[32,8832]{1,0:T(8,128)(2,1)S(1)}, bf16[32,8832]{1,0:T(8,128)(2,1)S(1)}, u32[]{:S(2)}, u32[]{:S(2)}) collective-permute-start(bf16[32,8832]{1,0:T(8,128)(2,1)S(1)} %constant_dynamic-update-slice_fusion.8.refs_2_), channel_id=1, source_target_pairs={{0,8},{8,0},{16,24},{24,16},{32,40},{40,32},{48,56},{56,48},{64,72... | collective-permute-start | bytes 1695752 | tf_op jit(solution)/shard_map/ppermute | solution.py:40
  65.8 13.0 %all-to-all-start.1 = ((bf16[8,256,128]{2,1,0:T(8,128)(2,1)}), bf16[8,256,128]{2,1,0:T(8,128)(2,1)S(1)}, u32[]{:S(2)}, u32[]{:S(2)}) async-start(bf16[8,256,128]{2,1,0:T(8,128)(2,1)} %shard_map.110), calls=%async_computation.1 | async-start | bytes 1048576 | tf_op jit(solution)/shard_map/all_to_all | solution.py:271
  85.9 9.0 %collective-permute-start.14 = (bf16[4480,256]{1,0:T(8,128)(2,1)}, bf16[4480,256]{1,0:T(8,128)(2,1)}, u32[]{:S(2)}, u32[]{:S(2)}) collective-permute-start(bf16[4480,256]{1,0:T(8,128)(2,1)} %shard_map.112), channel_id=1, source_target_pairs={{0,8},{8,0},{16,24},{24,16},{32,40},{40,32},{48,56},{56,48},{64,72... | collective-permute-start | bytes 6881288 | tf_op jit(solution)/shard_map/ppermute | solution.py:284
  97.4 14.5 %collective-permute-start.18 = (bf16[4,552,128]{2,1,0:T(8,128)(2,1)S(1)}, bf16[4,552,128]{2,1,0:T(8,128)(2,1)S(1)}, u32[]{:S(2)}, u32[]{:S(2)}) collective-permute-start(bf16[4,552,128]{2,1,0:T(8,128)(2,1)S(1)} %get-tuple-element.52), channel_id=1, source_target_pairs={{0,64},{8,72},{16,80},{24,88},{32,96},{40,104},{48,112},{56,120},{... | collective-permute-start | bytes 1695752 | tf_op jit(solution)/shard_map/ppermute | solution.py:300
  98.4 15.3 %collective-permute-start.15 = (bf16[2,552,128]{2,1,0:T(8,128)(2,1)S(1)}, bf16[2,552,128]{2,1,0:T(8,128)(2,1)S(1)}, u32[]{:S(2)}, u32[]{:S(2)}) collective-permute-start(bf16[2,552,128]{2,1,0:T(8,128)(2,1)S(1)} %get-tuple-element.48), channel_id=1, source_target_pairs={{0,16},{8,24},{16,32},{24,40},{32,48},{40,56},{48,0},{56,8},{64,80... | collective-permute-start | bytes 847880 | tf_op jit(solution)/shard_map/ppermute | solution.py:301
  98.4 15.3 %collective-permute-start.16 = (bf16[2,552,128]{2,1,0:T(8,128)(2,1)S(1)}, bf16[2,552,128]{2,1,0:T(8,128)(2,1)S(1)}, u32[]{:S(2)}, u32[]{:S(2)}) collective-permute-start(bf16[2,552,128]{2,1,0:T(8,128)(2,1)S(1)} %get-tuple-element.49), channel_id=1, source_target_pairs={{0,32},{8,40},{16,48},{24,56},{32,0},{40,8},{48,16},{56,24},{64,96... | collective-permute-start | bytes 847880 | tf_op jit(solution)/shard_map/ppermute | solution.py:301
  99.6 14.5 %collective-permute-start.17 = (bf16[2,552,128]{2,1,0:T(8,128)(2,1)S(1)}, bf16[2,552,128]{2,1,0:T(8,128)(2,1)S(1)}, u32[]{:S(2)}, u32[]{:S(2)}) collective-permute-start(bf16[2,552,128]{2,1,0:T(8,128)(2,1)S(1)} %get-tuple-element.50), channel_id=1, source_target_pairs={{0,48},{8,56},{16,0},{24,8},{32,16},{40,24},{48,32},{56,40},{64,11... | collective-permute-start | bytes 847880 | tf_op jit(solution)/shard_map/ppermute | solution.py:301
  114.2 4.5 %collective-permute-start.19 = (bf16[552,128]{1,0:T(8,128)(2,1)S(1)}, bf16[552,128]{1,0:T(8,128)(2,1)S(1)}, u32[]{:S(2)}, u32[]{:S(2)}) collective-permute-start(bf16[552,128]{1,0:T(8,128)(2,1)S(1)} %get-tuple-element.60), channel_id=1, source_target_pairs={{0,64},{8,72},{16,80},{24,88},{32,96},{40,104},{48,112},{56,120},{... | collective-permute-start | bytes 423944 | tf_op jit(solution)/shard_map/ppermute | solution.py:300
  114.8 5.1 %collective-permute-start.20 = (bf16[552,128]{1,0:T(8,128)(2,1)S(1)}, bf16[552,128]{1,0:T(8,128)(2,1)S(1)}, u32[]{:S(2)}, u32[]{:S(2)}) collective-permute-start(bf16[552,128]{1,0:T(8,128)(2,1)S(1)} %get-tuple-element.62), channel_id=1, source_target_pairs={{0,16},{8,24},{16,32},{24,40},{32,48},{40,56},{48,0},{56,8},{64,80... | collective-permute-start | bytes 423944 | tf_op jit(solution)/shard_map/ppermute | solution.py:301
  115.7 8.4 %collective-permute-start.21 = (bf16[552,128]{1,0:T(8,128)(2,1)S(1)}, bf16[552,128]{1,0:T(8,128)(2,1)S(1)}, u32[]{:S(2)}, u32[]{:S(2)}) collective-permute-start(bf16[552,128]{1,0:T(8,128)(2,1)S(1)} %get-tuple-element.63), channel_id=1, source_target_pairs={{0,32},{8,40},{16,48},{24,56},{32,0},{40,8},{48,16},{56,24},{64,96... | collective-permute-start | bytes 423944 | tf_op jit(solution)/shard_map/ppermute | solution.py:301
  118.7 5.4 %collective-permute-start.22 = (bf16[552,128]{1,0:T(8,128)(2,1)S(1)}, bf16[552,128]{1,0:T(8,128)(2,1)S(1)}, u32[]{:S(2)}, u32[]{:S(2)}) collective-permute-start(bf16[552,128]{1,0:T(8,128)(2,1)S(1)} %get-tuple-element.64), channel_id=1, source_target_pairs={{0,48},{8,56},{16,0},{24,8},{32,16},{40,24},{48,32},{56,40},{64,11... | collective-permute-start | bytes 423944 | tf_op jit(solution)/shard_map/ppermute | solution.py:301
